TPU v7x, 32 devices: a whole 2x2x4 slice. The times are simulated.
32 devices in a mesh: exp: 8 (over z, x), sub: 4 (over y, core).
Axes of the slice: x: 2, y: 2, z: 4, core: 2. Of those that a mesh axis runs over, the one named last changes fastest.
Arguments:
- sky_map: float32 [32, 8, 8, 128], P(('exp', 'sub')), may hold values from -6 to 6
- coeffs: bfloat16 [16, 12, 512, 512], P('exp', None, 'sub'), may hold values from -1.75 to 1.75
- observed: float32 [16, 512, 512], P('exp', 'sub'), may hold values from -6 to 6
- vert_taps: bfloat16 [12, 21], replicated, may hold values from -1.25 to 1.25
- horiz_taps: bfloat16 [12, 21], replicated, may hold values from -1.25 to 1.25
- owner_ids: int32 [16, 64, 4, 1], P('exp', 'sub'), may hold values from 0 to 7; in each aligned block of 64 rows (0 to 63, 64 to 127, ..., all dimensions but the last counted through in order) at most 16 rows name the same one
- offset: int32 [16, 64, 4], P('exp', 'sub'), may hold values from 0 to 7
Outputs:
- sky_final: float32 [32, 8, 8, 128], P(('exp', 'sub'))
- clipped: float32 [16, 512, 512], P('exp', 'sub')
Inputs may be any that keep to these rules, and one draw needn't show every extreme that they name: Patch (e, r, q) reads sky tile owner_ids[e, r, q, 0] * 4 + r // 16. Among the 64 patches of one band of one piece (the rows of one device's piece) no owner is named more than 16 times, and in every draw some band names one owner exactly 16 times.
All inputs are finite; a program needn't handle non-finite values.
Results may differ from a plain program's by a relative error of at most 0.0035.
Values may be sent and summed in bfloat16 or wider, within the bound.
No kernel may reach another device: no remote copies, remote signals or barrier semaphores. Data moves between devices by JAX's collectives and lax.ppermute only.
A program may use at most 64 MiB of HBM per device.

v0:
```python
import jax
import jax.numpy as jnp
from jax import lax
from jax.sharding import PartitionSpec as P

STEPS = 2


ETA = 0.5
DELTA = 1.0


def padded_2(cells, sides, width):
    for axis, dim in sides:
        count = lax.axis_size(axis)
        ends = count - 1
        head = lax.slice_in_dim(cells, 0, width, axis=dim)
        tail = lax.slice_in_dim(cells, cells.shape[dim] - width, cells.shape[dim], axis=dim)
        cells = jnp.concatenate(
            [
                lax.ppermute(tail, axis, [(i, (i + 1) % count) for i in range(ends)]),
                cells,
                lax.ppermute(head, axis, [((i + 1) % count, i) for i in range(ends)]),
            ],
            axis=dim,
        )
    return cells


def from_behind(block, axis, distance):
    devices = range(lax.axis_size(axis))
    route = [(i - distance, i) for i in devices if i - distance in devices]
    return lax.ppermute(block, axis, route)


def band_table(filters, height, breadth, direction):
    row_ids = lax.broadcasted_iota(jnp.int32, (height, breadth), 0)
    col_ids = lax.broadcasted_iota(jnp.int32, (height, breadth), 1)
    lag_ids = direction * (col_ids - row_ids)
    tap_ids = lax.broadcasted_iota(jnp.int32, (filters.shape[1], height, breadth), 0)
    select = (tap_ids == lag_ids[None]).astype(jnp.float32)
    return jnp.einsum("mt,tij->mij", filters.astype(jnp.float32), select).astype(jnp.bfloat16)


def per_device(sky_map, coeffs, observed, vert_taps, horiz_taps, owner_ids, offset):
    pieces, height, breadth = observed.shape
    mode_count = coeffs.shape[1]
    per_tile = sky_map.shape[1]
    patch_rows = sky_map.shape[2]
    patch_cols = sky_map.shape[3]
    patch_size = patch_rows * patch_cols
    margin = (vert_taps.shape[1] - 1) // 2
    exp_count = lax.axis_size("exp")
    rows_band = height // patch_rows
    cols_band = breadth // patch_cols
    per_band = rows_band * cols_band
    requests = pieces * per_band
    vertical = band_table(vert_taps, height, height + 2 * margin, 1)
    horizontal = band_table(horiz_taps, patch_cols + 2 * margin, patch_cols, -1)
    owners = owner_ids.reshape(requests)
    offsets = offset.reshape(requests)
    slot_cap = max(2, 2 * per_band // exp_count)
    slot_count = exp_count * pieces * slot_cap
    named_one = (
        owners.reshape(pieces, per_band)[:, :, None]
        == lax.broadcasted_iota(jnp.int32, (1, 1, exp_count), 2)
    ).astype(jnp.int32)
    earlier = jnp.cumsum(named_one, axis=1) - named_one
    ranking = jnp.sum(earlier * named_one, axis=2).reshape(requests)
    piece_of = lax.broadcasted_iota(jnp.int32, (requests,), 0) // per_band
    target = owners * (pieces * slot_cap) + piece_of * slot_cap + ranking
    picked = target[:, None] == lax.broadcasted_iota(jnp.int32, (1, slot_count), 1)
    wanted = jnp.sum(jnp.where(picked, offsets[:, None] + 1, 0), axis=0) - 1
    asked_ids = lax.all_to_all(
        wanted.reshape(exp_count, pieces * slot_cap), "exp", split_axis=0, concat_axis=0, tiled=True
    ).reshape(slot_count)
    chosen = (asked_ids[:, None] == lax.broadcasted_iota(jnp.int32, (1, per_tile), 1)).astype(
        jnp.float32
    )
    counts = jnp.sum(chosen, axis=0)
    picked_f = picked.astype(jnp.float32)
    picked_b = picked.astype(jnp.bfloat16)
    chosen_b = chosen.astype(jnp.bfloat16)
    current = sky_map.reshape(per_tile, patch_size)
    clipped = jnp.zeros(observed.shape, jnp.float32)
    for step_index in range(STEPS):
        replies = jnp.dot(
            chosen_b, current.astype(jnp.bfloat16), preferred_element_type=jnp.float32
        ).astype(jnp.bfloat16)
        arrived = lax.all_to_all(
            replies.reshape(exp_count, pieces * slot_cap, patch_size),
            "exp",
            split_axis=0,
            concat_axis=0,
            tiled=True,
        )
        patches = jnp.dot(
            picked_b, arrived.reshape(slot_count, patch_size), preferred_element_type=jnp.float32
        ).astype(jnp.bfloat16)
        to_stacked = patches.reshape(pieces, rows_band, cols_band, patch_rows, patch_cols)
        extended = padded_2(
            to_stacked.transpose(0, 1, 3, 2, 4).reshape(pieces, height, breadth),
            (("sub", 1),),
            margin,
        )
        smoothed = jnp.einsum(
            "mia,pac->pmic", vertical, extended, preferred_element_type=jnp.float32
        ).astype(jnp.bfloat16)
        padded = jnp.pad(smoothed, ((0, 0), (0, 0), (0, 0), (margin, margin)))
        windows = jnp.stack(
            [
                padded[
                    ...,
                    block_index * patch_cols : block_index * patch_cols + patch_cols + 2 * margin,
                ]
                for block_index in range(cols_band)
            ],
            axis=3,
        )
        blurred = jnp.einsum(
            "pmbkw,mwc->pmbkc", windows, horizontal, preferred_element_type=jnp.float32
        ).reshape(pieces, mode_count, height, breadth)
        modeled = jnp.sum(coeffs.astype(jnp.float32) * blurred, axis=1)
        evaluate_clipped = jnp.clip(modeled - observed, -DELTA, DELTA)
        weighted = (coeffs.astype(jnp.float32) * evaluate_clipped[:, None]).astype(jnp.bfloat16)
        spread = jnp.einsum(
            "pmbkc,mwc->pmbkw",
            weighted.reshape(pieces, mode_count, height, cols_band, patch_cols),
            horizontal,
            preferred_element_type=jnp.float32,
        )
        summed = jnp.zeros((pieces, mode_count, height, breadth + 2 * margin), jnp.float32)
        for block_index in range(cols_band):
            summed = summed + jnp.pad(
                spread[:, :, :, block_index],
                (
                    (0, 0),
                    (0, 0),
                    (0, 0),
                    (block_index * patch_cols, breadth - (block_index + 1) * patch_cols),
                ),
            )
        back_rows = summed[..., margin : margin + breadth].astype(jnp.bfloat16)
        gathered_rows = jnp.einsum(
            "mia,pmic->pac", vertical, back_rows, preferred_element_type=jnp.float32
        )
        upper_rim = gathered_rows[:, :margin]
        lower_rim = gathered_rows[:, height + margin :]
        from_below = from_behind(upper_rim, "sub", -1)
        from_above = from_behind(lower_rim, "sub", 1)
        gradient = gathered_rows[:, margin : margin + height]
        gradient = (
            gradient
            + jnp.pad(from_above, ((0, 0), (0, height - margin), (0, 0)))
            + jnp.pad(from_below, ((0, 0), (height - margin, 0), (0, 0)))
        )
        clipped, gradient = (evaluate_clipped, gradient)
        stacked = gradient.reshape(pieces, rows_band, patch_rows, cols_band, patch_cols)
        outgoing = lax.dot_general(
            picked_f,
            stacked.transpose(0, 1, 3, 2, 4).reshape(requests, patch_size),
            (((0,), (0,)), ((), ())),
            precision=lax.Precision.HIGHEST,
        )
        incoming = lax.all_to_all(
            outgoing.reshape(exp_count, pieces * slot_cap, patch_size),
            "exp",
            split_axis=0,
            concat_axis=0,
            tiled=True,
        )
        summed = lax.dot_general(
            chosen,
            incoming.reshape(slot_count, patch_size),
            (((0,), (0,)), ((), ())),
            precision=lax.Precision.HIGHEST,
        )
        current = current - ETA * summed / jnp.maximum(counts, 1.0)[:, None]
    return (current.reshape(sky_map.shape), clipped)


def solution(mesh):
    return jax.shard_map(
        per_device,
        mesh=mesh,
        in_specs=(
            P(("exp", "sub"), None, None, None),
            P("exp", None, "sub", None),
            P("exp", "sub", None),
            P(),
            P(),
            P("exp", "sub", None, None),
            P("exp", "sub", None),
        ),
        out_specs=(P(("exp", "sub"), None, None, None), P("exp", "sub", None)),
        check_vma=False,
    )
```

profile of v0, /device:TPU:1, one launch (start us, length us, event | category | flops | bytes accessed | tf_op | source)
XLA Modules:
  0.0 213.9 jit_solution(11260882723240964229)
XLA Ops:
  0.7 0.8 copy.62
  1.4 0.7 broadcast_multiply_fusion
  2.9 0.7 broadcast_add_fusion
  4.0 11.5 %all_to_all.26 = s32[8,1,32]{2,1,0:T(1,128)S(1)} all-to-all(s32[8,1,32]{2,1,0:T(1,128)S(1)} %sub.44), channel_id=1, replica_groups=mesh['exp'=8,'sub'=4] {'exp'}, dimensions={0} | all-to-all | bytes 2048 | tf_op jit(solution)/shard_map/all_to_all | solution.py:74
  16.0 0.7 reduce.3
  16.7 1.9 convolution_convert_fusion.1
  18.6 3.5 %all-to-all-start.1 = ((bf16[8,32,1024]{2,1,0:T(8,128)(2,1)}), bf16[8,32,1024]{2,1,0:T(8,128)(2,1)S(1)}, u32[]{:S(2)}, u32[]{:S(2)}) async-start(bf16[8,32,1024]{2,1,0:T(8,128)(2,1)} %bitcast.4), calls=%async_computation.1 | async-start | bytes 1048576 | tf_op jit(solution)/shard_map/all_to_all | solution.py:90
  22.6 10.4 %all-to-all-done.1 = bf16[8,32,1024]{2,1,0:T(8,128)(2,1)S(1)} async-done(((bf16[8,32,1024]{2,1,0:T(8,128)(2,1)}), bf16[8,32,1024]{2,1,0:T(8,128)(2,1)S(1)}, u32[]{:S(2)}, u32[]{:S(2)}) %all-to-all-start.1) | async-done | bytes 524320 | tf_op jit(solution)/shard_map/all_to_all | solution.py:90
  33.4 7.5 %collective-permute-start = (bf16[2,10,512]{2,1,0:T(8,128)(2,1)S(1)}, bf16[2,10,512]{2,1,0:T(8,128)(2,1)S(1)}, u32[]{:S(2)}, u32[]{:S(2)}) collective-permute-start(bf16[2,10,512]{2,1,0:T(8,128)(2,1)S(1)} %get-tuple-element.30), channel_id=1, source_target_pairs={{0,1},{1,2},{2,3},{4,5},{5,6},{6,7},{8,9},{9,10},{10,11},{12,13},{... | collective-permute-start | bytes 61448 | tf_op jit(solution)/shard_map/ppermute | solution.py:21
  40.9 1.9 collective-permute-start.1
  43.3 2.8 %collective-permute-done.1 = bf16[2,10,512]{2,1,0:T(8,128)(2,1)S(1)} collective-permute-done((bf16[2,10,512]{2,1,0:T(8,128)(2,1)S(1)}, bf16[2,10,512]{2,1,0:T(8,128)(2,1)S(1)}, u32[]{:S(2)}, u32[]{:S(2)}) %collective-permute-start.1) | collective-permute-done | bytes 20512 | tf_op jit(solution)/shard_map/ppermute | solution.py:23
  46.1 1.0 convert_bitcast_fusion.1
  47.1 1.9 fusion.42
  49.0 3.3 %fusion.8 = f32[12,128,2,128,4]{3,1,4,2,0:T(8,128)} fusion(bf16[12,148,128,1,1]{2,0,1,4,3:T(8,128)(2,1)S(1)} %fusion.34, bf16[2,12,128,1,148]{2,4,1,0,3:T(8,128)(2,1)S(1)} %get-tuple-element.21, bf16[2,12,128,1,148]{2,4,1,0,3:T(8,128)(2,1)S(1)} %get-tuple-element.22, bf16[2,12,128,1,148]{2,4,1,0,3:T(8,128)(2,1)S(1)} %get-tuple-element.23, ...), kind=kOutput, calls=%fused_computation.20 | convolution fusion | flops 471023616 | bytes 10383360 | tf_op jit(solution)/shard_map/pmbkw,mwc->pmbkc/dot_general | solution.py:120
  52.4 6.7 %copy.67 = f32[2,12,128,512]{3,2,1,0:T(8,128)} copy(f32[2,12,128,512]{2,3,0,1:T(8,128)} %bitcast.159) | data formatting | bytes 12582912 | tf_op jit(solution)/shard_map/reshape | solution.py:122
  59.1 4.1 %fusion = f32[2,128,512]{2,1,0:T(8,128)S(1)} fusion(f32[2,12,128,512]{3,2,1,0:T(8,128)} %copy.67, bf16[2,12,128,512]{3,2,1,0:T(8,128)(2,1)S(1)} %copy-done.2), kind=kLoop, calls=%fused_computation.4 | loop fusion | flops 4587520 | bytes 9961472 | tf_op jit(solution)/shard_map/reduce_sum | solution.py:123
  63.3 2.4 %fusion.1 = bf16[2,12,128,512]{3,2,1,0:T(8,128)(2,1)} fusion(bf16[2,12,128,512]{3,2,1,0:T(8,128)(2,1)S(1)} %copy-done.2, f32[2,128,512]{2,1,0:T(8,128)S(1)} %subtract_clamp_fusion.1), kind=kLoop, calls=%fused_computation.5 | loop fusion | flops 4718592 | bytes 6815744 | tf_op jit(solution)/shard_map/convert_element_type | solution.py:125
  65.8 5.5 %reshape.171 = bf16[2,12,128,4,128]{4,3,2,1,0:T(4,128)(2,1)} reshape(bf16[2,12,128,512]{3,2,1,0:T(8,128)(2,1)} %fusion.1) | data formatting | bytes 6291456 | tf_op jit(solution)/shard_map/reshape | solution.py:128
  71.3 4.3 %fusion.18 = f32[2,12,128,4,148]{2,4,3,0,1:T(8,128)S(1)} fusion(bf16[2,12,128,4,128]{4,3,2,1,0:T(4,128)(2,1)} %reshape.171, bf16[12,148,128,1,1]{2,0,1,4,3:T(8,128)(2,1)} %copy-done.3), kind=kOutput, calls=%fused_computation.34 | convolution fusion | flops 465567744 | bytes 10874880 | tf_op jit(solution)/shard_map/pmbkc,mwc->pmbkw/dot_general | solution.py:126
  75.6 0.6 slice_bitcast_fusion.7
  76.6 1.2 fusion.31
  77.9 1.9 collective-permute-start.2
  79.8 2.6 %collective-permute-start.3 = (f32[2,10,512]{2,1,0:T(8,128)S(1)}, f32[2,10,512]{2,1,0:T(8,128)S(1)}, u32[]{:S(2)}, u32[]{:S(2)}) collective-permute-start(f32[2,10,512]{2,1,0:T(8,128)S(1)} %get-tuple-element.27), channel_id=1, source_target_pairs={{1,0},{2,1},{3,2},{5,4},{6,5},{7,6},{9,8},{10,9},{11,10},{13,12},{... | collective-permute-start | bytes 122888 | tf_op jit(solution)/shard_map/ppermute | solution.py:33
  82.4 3.0 %collective-permute-done.3 = f32[2,10,512]{2,1,0:T(8,128)S(1)} collective-permute-done((f32[2,10,512]{2,1,0:T(8,128)S(1)}, f32[2,10,512]{2,1,0:T(8,128)S(1)}, u32[]{:S(2)}, u32[]{:S(2)}) %collective-permute-start.3) | collective-permute-done | bytes 40992 | tf_op jit(solution)/shard_map/ppermute | solution.py:33
  85.4 0.9 fusion.51
  86.2 2.0 reshape.193
  88.2 2.6 %fusion.68 = f32[8,32,1024]{2,1,0:T(8,128)} fusion(f32[128,1024,1]{1,0,2:T(8,128)} %reshape.193, s32[8,32]{1,0:T(8,128)S(1)} %multiply_add_fusion, s32[128]{0:T(128)S(1)} %fusion.90), kind=kOutput, calls=%fused_computation.102 | convolution fusion | flops 402685952 | bytes 1574400 | tf_op jit(solution)/shard_map/dot_general | solution.py:159
  90.8 4.2 %all-to-all-start.2 = ((f32[8,32,1024]{2,1,0:T(8,128)}), f32[8,32,1024]{2,1,0:T(8,128)}, u32[]{:S(2)}, u32[]{:S(2)}) async-start(f32[8,32,1024]{2,1,0:T(8,128)} %fusion.68), calls=%async_computation.2 | async-start | bytes 2097152 | tf_op jit(solution)/shard_map/all_to_all | solution.py:165
  95.2 24.9 %all-to-all-done.2 = f32[8,32,1024]{2,1,0:T(8,128)} async-done(((f32[8,32,1024]{2,1,0:T(8,128)}), f32[8,32,1024]{2,1,0:T(8,128)}, u32[]{:S(2)}, u32[]{:S(2)}) %all-to-all-start.2) | async-done | bytes 1048608 | tf_op jit(solution)/shard_map/all_to_all | solution.py:165
  120.1 1.7 fusion.41
  122.2 16.5 %all_to_all.27 = bf16[8,32,1024]{2,1,0:T(8,128)(2,1)S(1)} all-to-all(bf16[8,32,1024]{2,1,0:T(8,128)(2,1)S(1)} %bitcast.168), channel_id=1, replica_groups=mesh['exp'=8,'sub'=4] {'exp'}, dimensions={0} | all-to-all | bytes 1048576 | tf_op jit(solution)/shard_map/all_to_all | solution.py:90
  139.0 2.1 collective-permute-start.4
  141.1 2.9 %collective-permute-start.5 = (bf16[2,10,512]{2,1,0:T(8,128)(2,1)S(1)}, bf16[2,10,512]{2,1,0:T(8,128)(2,1)S(1)}, u32[]{:S(2)}, u32[]{:S(2)}) collective-permute-start(bf16[2,10,512]{2,1,0:T(8,128)(2,1)S(1)} %get-tuple-element.29), channel_id=1, source_target_pairs={{1,0},{2,1},{3,2},{5,4},{6,5},{7,6},{9,8},{10,9},{11,10},{13,12},{... | collective-permute-start | bytes 61448 | tf_op jit(solution)/shard_map/ppermute | solution.py:23
  144.0 2.4 %collective-permute-done.5 = bf16[2,10,512]{2,1,0:T(8,128)(2,1)S(1)} collective-permute-done((bf16[2,10,512]{2,1,0:T(8,128)(2,1)S(1)}, bf16[2,10,512]{2,1,0:T(8,128)(2,1)S(1)}, u32[]{:S(2)}, u32[]{:S(2)}) %collective-permute-start.5) | collective-permute-done | bytes 20512 | tf_op jit(solution)/shard_map/ppermute | solution.py:23
  146.4 1.0 convert_bitcast_fusion
  147.4 1.9 fusion.44
  149.3 3.3 %fusion.6 = f32[12,128,2,128,4]{3,1,4,2,0:T(8,128)} fusion(bf16[12,148,128,1,1]{2,0,1,4,3:T(8,128)(2,1)S(1)} %copy-done.4, bf16[2,12,128,1,148]{2,4,1,0,3:T(8,128)(2,1)S(1)} %get-tuple-element.17, bf16[2,12,128,1,148]{2,4,1,0,3:T(8,128)(2,1)S(1)} %get-tuple-element.18, bf16[2,12,128,1,148]{2,4,1,0,3:T(8,128)(2,1)S(1)} %get-tuple-element.19, ...), kind=kOutput, calls=%fused_computation.18 | convolution fusion | flops 471023616 | bytes 10383360 | tf_op jit(solution)/shard_map/pmbkw,mwc->pmbkc/dot_general | solution.py:120
  152.7 6.6 %copy.78 = f32[2,12,128,512]{3,2,1,0:T(8,128)} copy(f32[2,12,128,512]{2,3,0,1:T(8,128)} %bitcast.160) | data formatting | bytes 12582912 | tf_op jit(solution)/shard_map/reshape | solution.py:122
  159.2 4.1 %fusion.2 = f32[2,128,512]{2,1,0:T(8,128)S(1)} fusion(f32[2,12,128,512]{3,2,1,0:T(8,128)} %copy.78, bf16[2,12,128,512]{3,2,1,0:T(8,128)(2,1)S(1)} %copy-done.2), kind=kLoop, calls=%fused_computation.6 | loop fusion | flops 4587520 | bytes 9961472 | tf_op jit(solution)/shard_map/reduce_sum | solution.py:123
  163.5 0.8 copy-done.11
  164.3 2.4 %fusion.3 = bf16[2,12,128,512]{3,2,1,0:T(8,128)(2,1)} fusion(bf16[2,12,128,512]{3,2,1,0:T(8,128)(2,1)S(1)} %copy-done.2, f32[2,128,512]{2,1,0:T(8,128)S(1)} %subtract_clamp_fusion), kind=kLoop, calls=%fused_computation.7 | loop fusion | flops 4718592 | bytes 6815744 | tf_op jit(solution)/shard_map/convert_element_type | solution.py:125
  166.7 3.8 %reshape.180 = bf16[2,12,128,4,128]{4,3,2,1,0:T(4,128)(2,1)S(1)} reshape(bf16[2,12,128,512]{3,2,1,0:T(8,128)(2,1)} %fusion.3) | data formatting | bytes 6291456 | tf_op jit(solution)/shard_map/reshape | solution.py:128
  170.5 3.3 %fusion.21 = f32[2,12,128,4,148]{2,4,3,0,1:T(8,128)S(1)} fusion(bf16[2,12,128,4,128]{4,3,2,1,0:T(4,128)(2,1)S(1)} %reshape.180, bf16[12,148,128,1,1]{2,0,1,4,3:T(8,128)(2,1)} %copy-done.3), kind=kOutput, calls=%fused_computation.35 | convolution fusion | flops 465567744 | bytes 10874880 | tf_op jit(solution)/shard_map/pmbkc,mwc->pmbkw/dot_general | solution.py:126
  174.8 1.2 fusion.28
  176.0 1.9 collective-permute-start.6
  178.0 2.4 %collective-permute-start.7 = (f32[2,10,512]{2,1,0:T(8,128)S(1)}, f32[2,10,512]{2,1,0:T(8,128)S(1)}, u32[]{:S(2)}, u32[]{:S(2)}) collective-permute-start(f32[2,10,512]{2,1,0:T(8,128)S(1)} %get-tuple-element.25), channel_id=1, source_target_pairs={{1,0},{2,1},{3,2},{5,4},{6,5},{7,6},{9,8},{10,9},{11,10},{13,12},{... | collective-permute-start | bytes 122888 | tf_op jit(solution)/shard_map/ppermute | solution.py:33
  180.4 3.2 %collective-permute-done.7 = f32[2,10,512]{2,1,0:T(8,128)S(1)} collective-permute-done((f32[2,10,512]{2,1,0:T(8,128)S(1)}, f32[2,10,512]{2,1,0:T(8,128)S(1)}, u32[]{:S(2)}, u32[]{:S(2)}) %collective-permute-start.7) | collective-permute-done | bytes 40992 | tf_op jit(solution)/shard_map/ppermute | solution.py:33
  184.3 28.5 %all_to_all.28 = f32[8,32,1024]{2,1,0:T(8,128)S(1)} all-to-all(f32[8,32,1024]{2,1,0:T(8,128)S(1)} %fusion.66), channel_id=1, replica_groups=mesh['exp'=8,'sub'=4] {'exp'}, dimensions={0} | all-to-all | bytes 2097152 | tf_op jit(solution)/shard_map/all_to_all | solution.py:165
  (70 shorter events, 7.4 us)
Async XLA Ops:
  0.6 21.5 %copy-start = (bf16[12,21]{1,0:T(8,128)(2,1)S(1)}, bf16[12,21]{1,0:T(8,128)(2,1)}, u32[]{:S(2)}) copy-start(bf16[12,21]{1,0:T(8,128)(2,1)} %param.10) | copy-start | bytes 1516
  0.6 42.1 %copy-start.13 = (bf16[12,21]{1,0:T(8,128)(2,1)S(1)}, bf16[12,21]{1,0:T(8,128)(2,1)}, u32[]{:S(2)}) copy-start(bf16[12,21]{1,0:T(8,128)(2,1)} %param.11) | copy-start | bytes 1516
  18.6 14.4 %all-to-all-start.1 = ((bf16[8,32,1024]{2,1,0:T(8,128)(2,1)}), bf16[8,32,1024]{2,1,0:T(8,128)(2,1)S(1)}, u32[]{:S(2)}, u32[]{:S(2)}) async-start(bf16[8,32,1024]{2,1,0:T(8,128)(2,1)} %bitcast.4), calls=%async_computation.1 | async-start | bytes 1048576 | tf_op jit(solution)/shard_map/all_to_all | solution.py:90
  22.6 26.4 %copy-start.5 = (bf16[128,148,12]{0,2,1:T(8,128)(2,1)}, bf16[128,148,12]{0,2,1:T(8,128)(2,1)S(1)}, u32[]{:S(2)}) copy-start(bf16[128,148,12]{0,2,1:T(8,128)(2,1)S(1)} %fusion.26) | copy-start | bytes 1363972
  33.4 9.9 %collective-permute-start = (bf16[2,10,512]{2,1,0:T(8,128)(2,1)S(1)}, bf16[2,10,512]{2,1,0:T(8,128)(2,1)S(1)}, u32[]{:S(2)}, u32[]{:S(2)}) collective-permute-start(bf16[2,10,512]{2,1,0:T(8,128)(2,1)S(1)} %get-tuple-element.30), channel_id=1, source_target_pairs={{0,1},{1,2},{2,3},{4,5},{5,6},{6,7},{8,9},{9,10},{10,11},{12,13},{... | collective-permute-start | bytes 61448 | tf_op jit(solution)/shard_map/ppermute | solution.py:21
  40.9 5.2 %collective-permute-start.1 = (bf16[2,10,512]{2,1,0:T(8,128)(2,1)S(1)}, bf16[2,10,512]{2,1,0:T(8,128)(2,1)S(1)}, u32[]{:S(2)}, u32[]{:S(2)}) collective-permute-start(bf16[2,10,512]{2,1,0:T(8,128)(2,1)S(1)} %get-tuple-element.31), channel_id=1, source_target_pairs={{1,0},{2,1},{3,2},{5,4},{6,5},{7,6},{9,8},{10,9},{11,10},{13,12},{... | collective-permute-start | bytes 61448 | tf_op jit(solution)/shard_map/ppermute | solution.py:23
  43.3 5.8 %copy-start.3 = (bf16[12,148,128,1,1]{2,0,1,4,3:T(8,128)(2,1)}, bf16[12,148,128,1,1]{2,0,1,4,3:T(8,128)(2,1)S(1)}, u32[]{:S(2)}) copy-start(bf16[12,148,128,1,1]{2,0,1,4,3:T(8,128)(2,1)S(1)} %fusion.34) | copy-start | bytes 1363972
  52.4 6.7 %copy-start.2 = (bf16[2,12,128,512]{3,2,1,0:T(8,128)(2,1)S(1)}, bf16[2,12,128,512]{3,2,1,0:T(8,128)(2,1)}, u32[]{:S(2)}) copy-start(bf16[2,12,128,512]{3,2,1,0:T(8,128)(2,1)} %param.8) | copy-start | bytes 9437188
  59.1 4.1 %copy-start.9 = (f32[2,128,512]{2,1,0:T(8,128)S(1)}, f32[2,128,512]{2,1,0:T(8,128)}, u32[]{:S(2)}) copy-start(f32[2,128,512]{2,1,0:T(8,128)} %param.9) | copy-start | bytes 1572868
  75.5 1.1 copy-start.6
  77.8 42.3 %copy-start.12 = (f32[1,8,8,128]{3,2,1,0:T(8,128)S(1)}, f32[1,8,8,128]{3,2,1,0:T(8,128)}, u32[]{:S(2)}) copy-start(f32[1,8,8,128]{3,2,1,0:T(8,128)} %param.7) | copy-start | bytes 98308
  77.9 4.5 %collective-permute-start.2 = (f32[2,10,512]{2,1,0:T(8,128)S(1)}, f32[2,10,512]{2,1,0:T(8,128)S(1)}, u32[]{:S(2)}, u32[]{:S(2)}) collective-permute-start(f32[2,10,512]{2,1,0:T(8,128)S(1)} %get-tuple-element.26), channel_id=1, source_target_pairs={{0,1},{1,2},{2,3},{4,5},{5,6},{6,7},{8,9},{9,10},{10,11},{12,13},{... | collective-permute-start | bytes 122888 | tf_op jit(solution)/shard_map/ppermute | solution.py:33
  79.8 5.6 %collective-permute-start.3 = (f32[2,10,512]{2,1,0:T(8,128)S(1)}, f32[2,10,512]{2,1,0:T(8,128)S(1)}, u32[]{:S(2)}, u32[]{:S(2)}) collective-permute-start(f32[2,10,512]{2,1,0:T(8,128)S(1)} %get-tuple-element.27), channel_id=1, source_target_pairs={{1,0},{2,1},{3,2},{5,4},{6,5},{7,6},{9,8},{10,9},{11,10},{13,12},{... | collective-permute-start | bytes 122888 | tf_op jit(solution)/shard_map/ppermute | solution.py:33
  90.8 29.3 %all-to-all-start.2 = ((f32[8,32,1024]{2,1,0:T(8,128)}), f32[8,32,1024]{2,1,0:T(8,128)}, u32[]{:S(2)}, u32[]{:S(2)}) async-start(f32[8,32,1024]{2,1,0:T(8,128)} %fusion.68), calls=%async_computation.2 | async-start | bytes 2097152 | tf_op jit(solution)/shard_map/all_to_all | solution.py:165
  120.1 26.3 %copy-start.7 = (bf16[128,148,12]{0,2,1:T(8,128)(2,1)S(1)}, bf16[128,148,12]{0,2,1:T(8,128)(2,1)}, u32[]{:S(2)}) copy-start(bf16[128,148,12]{0,2,1:T(8,128)(2,1)} %copy-done.5) | copy-start | bytes 1363972
  139.0 5.0 %collective-permute-start.4 = (bf16[2,10,512]{2,1,0:T(8,128)(2,1)S(1)}, bf16[2,10,512]{2,1,0:T(8,128)(2,1)S(1)}, u32[]{:S(2)}, u32[]{:S(2)}) collective-permute-start(bf16[2,10,512]{2,1,0:T(8,128)(2,1)S(1)} %get-tuple-element.28), channel_id=1, source_target_pairs={{0,1},{1,2},{2,3},{4,5},{5,6},{6,7},{8,9},{9,10},{10,11},{12,13},{... | collective-permute-start | bytes 61448 | tf_op jit(solution)/shard_map/ppermute | solution.py:21
  141.1 5.2 %collective-permute-start.5 = (bf16[2,10,512]{2,1,0:T(8,128)(2,1)S(1)}, bf16[2,10,512]{2,1,0:T(8,128)(2,1)S(1)}, u32[]{:S(2)}, u32[]{:S(2)}) collective-permute-start(bf16[2,10,512]{2,1,0:T(8,128)(2,1)S(1)} %get-tuple-element.29), channel_id=1, source_target_pairs={{1,0},{2,1},{3,2},{5,4},{6,5},{7,6},{9,8},{10,9},{11,10},{13,12},{... | collective-permute-start | bytes 61448 | tf_op jit(solution)/shard_map/ppermute | solution.py:23
  147.4 1.9 copy-start.4
  159.2 4.1 %copy-start.10 = (f32[2,128,512]{2,1,0:T(8,128)S(1)}, f32[2,128,512]{2,1,0:T(8,128)}, u32[]{:S(2)}) copy-start(f32[2,128,512]{2,1,0:T(8,128)} %param.9) | copy-start | bytes 1572868
  163.5 0.8 copy-start.11
  173.7 1.1 copy-start.8
  176.0 4.3 %collective-permute-start.6 = (f32[2,10,512]{2,1,0:T(8,128)S(1)}, f32[2,10,512]{2,1,0:T(8,128)S(1)}, u32[]{:S(2)}, u32[]{:S(2)}) collective-permute-start(f32[2,10,512]{2,1,0:T(8,128)S(1)} %get-tuple-element.24), channel_id=1, source_target_pairs={{0,1},{1,2},{2,3},{4,5},{5,6},{6,7},{8,9},{9,10},{10,11},{12,13},{... | collective-permute-start | bytes 122888 | tf_op jit(solution)/shard_map/ppermute | solution.py:33
  178.0 5.6 %collective-permute-start.7 = (f32[2,10,512]{2,1,0:T(8,128)S(1)}, f32[2,10,512]{2,1,0:T(8,128)S(1)}, u32[]{:S(2)}, u32[]{:S(2)}) collective-permute-start(f32[2,10,512]{2,1,0:T(8,128)S(1)} %get-tuple-element.25), channel_id=1, source_target_pairs={{1,0},{2,1},{3,2},{5,4},{6,5},{7,6},{9,8},{10,9},{11,10},{13,12},{... | collective-permute-start | bytes 122888 | tf_op jit(solution)/shard_map/ppermute | solution.py:33
  183.6 30.4 %copy-start.1 = (bf16[12,21]{1,0:T(8,128)(2,1)S(1)}, bf16[12,21]{1,0:T(8,128)(2,1)}, u32[]{:S(2)}) copy-start(bf16[12,21]{1,0:T(8,128)(2,1)} %param.10) | copy-start | bytes 1516
where the time goes:
time: 215 us; the launch traced here: 214 us
  blocking collectives  56.4 us (26%)
  waiting for transfers between devices  46.6 us (22%)
  local copies, waits for them, and re-layouts  34.1 us (16%)
  starting transfers between devices  30.9 us (14%)
  matrix products  27.8 us (13%)
  other arithmetic  16.9 us (8%)
    all_to_all x1, blocking collectives, per_device(): lax.all_to_all(outgoing.reshape(exp_count, pieces * slot_cap, patch_size)...  28.5 us
    all_to_all x1, waiting for transfers between devices, per_device(): lax.all_to_all(outgoing.reshape(exp_count, pieces * slot_cap, patch_size)...  24.9 us
    all_to_all x1, blocking collectives, per_device(): lax.all_to_all(replies.reshape(exp_count, pieces * slot_cap, patch_size),...  16.5 us
    reshape x2, local copies, waits for them, and re-layouts, per_device(): blurred = jnp.einsum('pmbkw,mwc->pmbkc', windows, horizontal, preferred_e...  13.3 us
    all_to_all x1, blocking collectives, per_device(): lax.all_to_all(wanted.reshape(exp_count, pieces * slot_cap), 'exp', split...  11.5 us
    all_to_all x1, waiting for transfers between devices, per_device(): lax.all_to_all(replies.reshape(exp_count, pieces * slot_cap, patch_size),...  10.4 us
    ppermute x2, starting transfers between devices, padded_2(): lax.ppermute(tail, axis, [(i, (i + 1) % count) for i in range(ends)])  9.56 us
    reshape x2, local copies, waits for them, and re-layouts, per_device(): weighted.reshape(pieces, mode_count, height, cols_band, patch_cols)  9.24 us
  transfers between devices with their start and end apart: 10, of which 6 were waited for; matrix products, arithmetic and copies ran while one was open for 1% of the time, Pallas kernels for 0%

commit v1 on v0

v1 whole, which is shorter than its diff:
```python
import functools

import jax
import jax.numpy as jnp
from jax import lax
from jax.experimental import pallas as pl
from jax.experimental.pallas import tpu as pltpu
from jax.sharding import PartitionSpec as P

STEPS = 2
ETA = 0.5
DELTA = 1.0
ROWS = 16
F32 = jnp.float32
BF16 = jnp.bfloat16


def round_up(value, unit):
    return -(-value // unit) * unit


def divisor(value, most):
    return max(k for k in range(1, most + 1) if value % k == 0)


def band_table(filters, height, breadth, direction, shift):
    row_ids = lax.broadcasted_iota(jnp.int32, (height, breadth), 0)
    col_ids = lax.broadcasted_iota(jnp.int32, (height, breadth), 1)
    lag_ids = direction * (col_ids - row_ids) + shift
    tap_ids = lax.broadcasted_iota(jnp.int32, (filters.shape[1], height, breadth), 0)
    select = (tap_ids == lag_ids[None]).astype(BF16)
    return jnp.einsum("mt,tij->mij", filters, select, preferred_element_type=F32).astype(BF16)


def side_table(filters, height, breadth, shift):
    modes, taps = filters.shape
    spread = jnp.repeat(filters.astype(F32).T, breadth, axis=1)
    places = lax.broadcasted_iota(jnp.int32, (height, modes * breadth), 1) % breadth
    lags = lax.broadcasted_iota(jnp.int32, (height, modes * breadth), 0) + shift - places
    table = jnp.zeros((height, modes * breadth), F32)
    for tap in range(taps):
        table = jnp.where(lags == tap, spread[tap][None], table)
    return table.astype(BF16)


def swap_rims(upper, lower, axis):
    count = lax.axis_size(axis)
    even = lax.axis_index(axis) % 2 == 0
    routes = []
    for first in (0, 1):
        pairs = [(k, k + 1) for k in range(first, count - 1, 2)]
        routes.append(pairs + [(b, a) for a, b in pairs])
    near = lax.ppermute(jnp.where(even, lower, upper), axis, routes[0])
    far = lax.ppermute(jnp.where(even, upper, lower), axis, routes[1])
    return near, far


def picture_kernel(even_ref, ids_ref, tiles_ref, picture_ref, near_ref, far_ref, wide_ref, *, patch, rim):
    pieces, height, breadth = picture_ref.shape
    patch_rows, patch_cols = patch
    wide_ref[...] = tiles_ref[...].astype(F32)
    cols = breadth // patch_cols
    rows = height // patch_rows
    together = ROWS // patch_rows
    for piece in range(pieces):
        for row in range(0, rows, together):
            for col in range(cols):
                parts = []
                for inner in range(together):
                    index = ids_ref[(piece * rows + row + inner) * cols + col]
                    start = pl.multiple_of(index * patch_rows, patch_rows)
                    parts.append(wide_ref[pl.ds(start, patch_rows), :])
                picture_ref[
                    piece, row * patch_rows : (row + together) * patch_rows, col * patch_cols : (col + 1) * patch_cols
                ] = jnp.concatenate(parts, axis=0).astype(BF16)

    @pl.when(even_ref[0] == 1)
    def _():
        near_ref[...] = picture_ref[:, height - rim :, :]
        far_ref[...] = picture_ref[:, :rim, :]

    @pl.when(even_ref[0] == 0)
    def _():
        near_ref[...] = picture_ref[:, :rim, :]
        far_ref[...] = picture_ref[:, height - rim :, :]


def windows_of(block, width, stride):
    count = max(1, (block.shape[1] - width) // stride + 1)
    return [block[:, k * stride : k * stride + width] for k in range(count)]


def joined(outs, width, stride):
    if len(outs) == 1:
        return [outs[0][:, k : k + stride] for k in range(0, width, stride)]
    lane = lax.broadcasted_iota(jnp.int32, (outs[0].shape[0], stride), 1)
    blocks = [outs[0][:, :stride]]
    for left, right in zip(outs[:-1], outs[1:]):
        blocks.append(jnp.where(lane < stride // 2, left[:, stride:], right[:, :stride]))
    blocks.append(outs[-1][:, stride:])
    return blocks


def step_kernel(
    even_ref, ids_ref, picture_ref, near_ref, far_ref, coeffs_ref, coeffs_up_ref, coeffs_down_ref, observed_ref,
    observed_up_ref, observed_down_ref, vertical_ref, side_ref, forward_ref, backward_ref, counted_ref,
    clipped_ref, sums_ref, image_ref, field_ref, model_ref, gradient_ref, *, patch, per_tile, with_counts,
):
    pieces, height, breadth = picture_ref.shape
    modes = coeffs_ref.shape[1]
    rim = near_ref.shape[1]
    ext = coeffs_up_ref.shape[2]
    tall = height + 2 * ext
    patch_rows, patch_cols = patch
    width = forward_ref.shape[1]
    stride = patch_cols
    image_ref[:, rim : rim + height, :] = picture_ref[...]

    @pl.when(even_ref[0] == 1)
    def _():
        image_ref[:, :rim, :] = far_ref[...]
        image_ref[:, rim + height :, :] = near_ref[...]

    @pl.when(even_ref[0] == 0)
    def _():
        image_ref[:, :rim, :] = near_ref[...]
        image_ref[:, rim + height :, :] = far_ref[...]

    group = divisor(modes, 4)
    chunk = group * tall

    def smooth(index, carry):
        start = pl.multiple_of(index * chunk, ROWS)
        table = vertical_ref[pl.ds(start, chunk), :]
        for piece in range(pieces):
            for low in range(0, breadth, width):
                field_ref[piece, pl.ds(start, chunk), low : low + width] = jnp.dot(
                    table, image_ref[piece, :, low : low + width], preferred_element_type=F32
                ).astype(BF16)
        return carry

    lax.fori_loop(0, modes // group, smooth, 0)
    model_ref[...] = jnp.zeros(model_ref.shape, F32)

    def coefficient(piece, mode):
        return jnp.concatenate(
            [coeffs_up_ref[piece, mode], coeffs_ref[piece, mode], coeffs_down_ref[piece, mode]], axis=0
        ).astype(F32)

    def blur(table, blocks):
        cuts = [cut for block in blocks for cut in windows_of(block, width, stride)]
        result = jnp.dot(jnp.concatenate(cuts, axis=0), table, preferred_element_type=F32)
        per = len(cuts) // len(blocks)
        outs = [result[k * tall : (k + 1) * tall] for k in range(len(cuts))]
        return [joined(outs[k * per : (k + 1) * per], width, stride) for k in range(len(blocks))]

    def forward(mode, carry):
        start = pl.multiple_of(mode * tall, ROWS)
        blocks = [field_ref[piece, pl.ds(start, tall), :] for piece in range(pieces)]
        for piece, columns in enumerate(blur(forward_ref[mode], blocks)):
            weight = coefficient(piece, mode)
            for k, column in enumerate(columns):
                place = slice(k * stride, (k + 1) * stride)
                model_ref[piece, :, place] += weight[:, place] * column
        return carry

    lax.fori_loop(0, modes, forward, 0)
    for piece in range(pieces):
        seen = jnp.concatenate([observed_up_ref[piece], observed_ref[piece], observed_down_ref[piece]], axis=0)
        model_ref[piece] = jnp.clip(model_ref[piece] - seen, -DELTA, DELTA)
        clipped_ref[piece] = model_ref[piece, ext : ext + height, :]

    def backward(mode, carry):
        start = pl.multiple_of(mode * tall, ROWS)
        blocks = [(coefficient(piece, mode) * model_ref[piece]).astype(BF16) for piece in range(pieces)]
        for piece, columns in enumerate(blur(backward_ref[mode], blocks)):
            for k, column in enumerate(columns):
                field_ref[piece, pl.ds(start, tall), k * stride : (k + 1) * stride] = column.astype(BF16)
        return carry

    lax.fori_loop(0, modes, backward, 0)
    for piece in range(pieces):
        for low in range(0, breadth, width):
            gradient_ref[piece, :, low : low + width] = jnp.dot(
                side_ref[...], field_ref[piece, :, low : low + width], preferred_element_type=F32
            )
    sums_ref[...] = jnp.zeros(sums_ref.shape, F32)
    cols = breadth // patch_cols
    rows = height // patch_rows
    for row in range(rows):
        for col in range(cols):
            for piece in range(pieces):
                index = ids_ref[(piece * rows + row) * cols + col]
                place = pl.ds(pl.multiple_of(index * patch_rows, patch_rows), patch_rows)
                sums_ref[place, :] += gradient_ref[
                    piece, row * patch_rows : (row + 1) * patch_rows, col * patch_cols : (col + 1) * patch_cols
                ]


def update_kernel(sky_ref, parts_ref, counts_ref, next_ref, spread_ref, *, sources, patch_rows):
    held = sky_ref.shape[0]
    total = parts_ref[:held, :]
    for source in range(1, sources):
        total = total + parts_ref[source * held : (source + 1) * held, :]
    fresh = sky_ref[...] - ETA * total / jnp.maximum(counts_ref[...], 1.0)
    next_ref[...] = fresh
    for source in range(sources):
        spread_ref[source * held : (source + 1) * held, :] = fresh.astype(BF16)


def per_device(sky_map, coeffs, observed, vert_taps, horiz_taps, owner_ids, offset):
    pieces, height, breadth = observed.shape
    modes = coeffs.shape[1]
    per_tile, patch_rows, patch_cols = sky_map.shape[1:]
    patch = (patch_rows, patch_cols)
    margin = (vert_taps.shape[1] - 1) // 2
    exp_count = lax.axis_size("exp")
    held = per_tile * patch_rows
    known = exp_count * held
    ext = round_up(margin, ROWS)
    rim = round_up(ext + margin, ROWS)
    tall = height + 2 * ext
    width = min(breadth, 2 * patch_cols)

    sky = sky_map.reshape(held, patch_cols)
    spread = jnp.broadcast_to(sky.astype(BF16)[None], (exp_count, held, patch_cols)).reshape(known, patch_cols)

    def exchange(block):
        return lax.all_to_all(block, "exp", split_axis=0, concat_axis=0, tiled=True)

    tiles = exchange(spread)

    even = (lax.axis_index("sub") % 2 == 0).astype(jnp.int32).reshape(1)
    is_even = lax.axis_index("sub") % 2 == 0
    ids = (owner_ids.reshape(offset.shape) * per_tile + offset).reshape(-1)
    c_near, c_far = swap_rims(coeffs[:, :, :ext], coeffs[:, :, height - ext :], "sub")
    o_near, o_far = swap_rims(observed[:, :ext], observed[:, height - ext :], "sub")
    c_up, c_down = jnp.where(is_even, c_far, c_near), jnp.where(is_even, c_near, c_far)
    o_up, o_down = jnp.where(is_even, o_far, o_near), jnp.where(is_even, o_near, o_far)
    vertical = band_table(vert_taps, tall, height + 2 * rim, 1, margin + ext - rim).reshape(modes * tall, -1)
    side = side_table(vert_taps, height, tall, ext + margin)
    forward = band_table(horiz_taps, width, width, -1, margin)
    backward = band_table(horiz_taps, width, width, 1, margin)

    named = ids[None, :] == lax.broadcasted_iota(jnp.int32, (exp_count * per_tile, ids.shape[0]), 0)
    counted = jnp.sum(named.astype(F32), axis=1)
    counted = jnp.broadcast_to(counted[:, None], (exp_count * per_tile, patch_cols))
    counts = jnp.sum(exchange(counted).reshape(exp_count, per_tile, patch_cols), axis=0)
    counts = jnp.broadcast_to(counts[:, None], (per_tile, patch_rows, patch_cols)).reshape(held, patch_cols)

    vmem = pl.BlockSpec(memory_space=pltpu.VMEM)
    smem = pl.BlockSpec(memory_space=pltpu.SMEM)
    clipped = None
    for step in range(STEPS):
        picture, near, far = pl.pallas_call(
            functools.partial(picture_kernel, patch=patch, rim=rim),
            out_shape=(
                jax.ShapeDtypeStruct((pieces, height, breadth), BF16),
                jax.ShapeDtypeStruct((pieces, rim, breadth), BF16),
                jax.ShapeDtypeStruct((pieces, rim, breadth), BF16),
            ),
            in_specs=[smem, smem, vmem],
            out_specs=(vmem, vmem, vmem),
            scratch_shapes=[pltpu.VMEM((known, patch_cols), F32)],
            compiler_params=pltpu.CompilerParams(vmem_limit_bytes=8 << 20),
            name="picture",
        )(even, ids, tiles)
        count = lax.axis_size("sub")
        routes = []
        for first in (0, 1):
            pairs = [(k, k + 1) for k in range(first, count - 1, 2)]
            routes.append(pairs + [(b, a) for a, b in pairs])
        far = lax.ppermute(far, "sub", routes[1])
        near = lax.ppermute(near, "sub", routes[0])
        clipped, sums = pl.pallas_call(
            functools.partial(step_kernel, patch=patch, per_tile=per_tile, with_counts=step == 0),
            out_shape=(
                jax.ShapeDtypeStruct((pieces, height, breadth), F32),
                jax.ShapeDtypeStruct((known, patch_cols), F32),
            ),
            in_specs=[smem, smem] + [vmem] * 14,
            out_specs=(vmem, vmem),
            scratch_shapes=[
                pltpu.VMEM((pieces, height + 2 * rim, breadth), BF16),
                pltpu.VMEM((pieces, modes * tall, breadth), BF16),
                pltpu.VMEM((pieces, tall, breadth), F32),
                pltpu.VMEM((pieces, height, breadth), F32),
            ],
            compiler_params=pltpu.CompilerParams(vmem_limit_bytes=40 << 20),
            name="step",
        )(
            even, ids, picture, near, far, coeffs, c_up, c_down, observed, o_up, o_down,
            vertical, side, forward, backward, counts,
        )
        parts = exchange(sums)
        sky, spread = pl.pallas_call(
            functools.partial(update_kernel, sources=exp_count, patch_rows=patch_rows),
            out_shape=(
                jax.ShapeDtypeStruct((held, patch_cols), F32),
                jax.ShapeDtypeStruct((known, patch_cols), BF16),
            ),
            in_specs=[vmem] * 3,
            out_specs=(vmem, vmem),
            name="update",
        )(sky, parts, counts)
        if step + 1 < STEPS:
            tiles = exchange(spread)
    return sky.reshape(sky_map.shape), clipped


def solution(mesh):
    return jax.shard_map(
        per_device,
        mesh=mesh,
        in_specs=(
            P(("exp", "sub"), None, None, None),
            P("exp", None, "sub", None),
            P("exp", "sub", None),
            P(),
            P(),
            P("exp", "sub", None, None),
            P("exp", "sub", None),
        ),
        out_specs=(P(("exp", "sub"), None, None, None), P("exp", "sub", None)),
        check_vma=False,
    )
```

time: 215 us -> 140 us (0.65)
  waiting for transfers between devices: 46.6 us -> 8.04 us
  Pallas kernels: 0 us -> 27 us
  blocking collectives: 56.4 us -> 29.7 us
  matrix products: 27.8 us -> 4.83 us
  other arithmetic: 16.9 us -> 10 us
  local copies, waits for them, and re-layouts: 34.1 us -> 28.7 us
    all_to_all x2, waiting for transfers between devices: 35.3 us -> 4.91 us  [exchange(): return lax.all_to_all(block, 'exp', split_axis=0, concat_axis=0, tiled=True)]
    pallas_call x0 -> x6, Pallas kernels: none -> 27 us  [the longest x2 22.4 us: per_device(): pl.pallas_call(functools.partial(step_kernel, patch=patch, per_tile=per_t...]
    all_to_all x3, blocking collectives: 56.4 us -> 29.7 us  [exchange(): return lax.all_to_all(block, 'exp', split_axis=0, concat_axis=0, tiled=True)]
    reshape x7 -> x2, local copies, waits for them, and re-layouts: 24.7 us -> 0.71 us  [the longest x1 0.6 us: per_device(): jnp.broadcast_to(counts[:, None], (per_tile, patch_rows, patch_cols))]
    dot_general x18 -> x3, matrix products: 27.8 us -> 4.83 us  [band_table(): jnp.einsum('mt,tij->mij', filters, select, preferred_element_type=F32)]
    unnamed x32 -> x44, local copies, waits for them, and re-layouts: 3.19 us -> 16.7 us
    reduce_sum x5 -> x2, other arithmetic: 8.66 us -> 0.12 us  [the longest x1 0.11 us: per_device(): counted = jnp.sum(named.astype(F32), axis=1)]
    ppermute x8, waiting for transfers between devices: 11.3 us -> 3.13 us  [the longest x2 3.11 us: per_device(): far = lax.ppermute(far, 'sub', routes[1])]
  transfers between devices with their start and end apart: 10 -> 10, of which waited for: 6 -> 3; matrix products, arithmetic and copies ran while one was open for 1% -> 18% of each run, Pallas kernels for 0% -> 0%
where the time goes in v1:
time: 140 us; the launch traced here: 138 us
  blocking collectives  29.7 us (21%)
  starting transfers between devices  28.8 us (21%)
  local copies, waits for them, and re-layouts  28.7 us (20%)
  Pallas kernels  27 us (19%)
  other arithmetic  10 us (7%)
  waiting for transfers between devices  8.04 us (6%)
  matrix products  4.83 us (3%)
    all_to_all x3, blocking collectives, exchange(): return lax.all_to_all(block, 'exp', split_axis=0, concat_axis=0, tiled=True)  29.7 us
    pallas_call x2, Pallas kernels, per_device(): pl.pallas_call(functools.partial(step_kernel, patch=patch, per_tile=per_t...  22.4 us
    unnamed x44, local copies, waits for them, and re-layouts  16.7 us
    all_to_all x2, starting transfers between devices, exchange(): return lax.all_to_all(block, 'exp', split_axis=0, concat_axis=0, tiled=True)  11 us
    ppermute x2, starting transfers between devices, per_device(): far = lax.ppermute(far, 'sub', routes[1])  8.65 us
    ppermute x2, starting transfers between devices, swap_rims(): far = lax.ppermute(jnp.where(even, upper, lower), axis, routes[1])  6.43 us
    convert_element_type x2, local copies, waits for them, and re-layouts, band_table(): jnp.einsum('mt,tij->mij', filters, select, preferred_element_type=F32)  5.58 us
    all_to_all x2, waiting for transfers between devices, exchange(): return lax.all_to_all(block, 'exp', split_axis=0, concat_axis=0, tiled=True)  4.91 us
  transfers between devices with their start and end apart: 10, of which 3 were waited for; matrix products, arithmetic and copies ran while one was open for 18% of the time, Pallas kernels for 0%

profile of v1, /device:TPU:1, one launch (start us, length us, event | category | flops | bytes accessed | tf_op | source)
XLA Modules:
  0.0 138.1 jit_solution(11941597551129016058)
XLA Ops:
  0.7 2.1 %broadcast_select_fusion.2 = (bf16[2,12,16,512]{3,2,1,0:T(8,128)(2,1)}, bf16[2,12,16,512]{3,2,1,0:T(8,128)(2,1)}) fusion(pred[]{:T(512)S(6)} %eq.169, bf16[2,12,128,512]{3,2,1,0:T(8,128)(2,1)} %coeffs_ref.3), kind=kLoop, calls=%fused_computation.40 | loop fusion | flops 393216 | bytes 1572865 | tf_op jit(solution)/shard_map/jit(_where)/select_n | solution.py:53
  2.7 4.5 %collective-permute-start.2 = (bf16[2,12,16,512]{3,2,1,0:T(8,128)(2,1)}, bf16[2,12,16,512]{3,2,1,0:T(8,128)(2,1)}, u32[]{:S(2)}, u32[]{:S(2)}) collective-permute-start(bf16[2,12,16,512]{3,2,1,0:T(8,128)(2,1)} %get-tuple-element.48), channel_id=1, source_target_pairs={{1,2},{2,1},{5,6},{6,5},{9,10},{10,9},{13,14},{14,13},{17,18},{18,... | collective-permute-start | bytes 1179656 | tf_op jit(solution)/shard_map/ppermute | solution.py:54
  7.3 1.5 %slice_select_fusion = (f32[2,16,512]{2,1,0:T(8,128)S(1)}, f32[2,16,512]{2,1,0:T(8,128)}) fusion(f32[2,128,512]{2,1,0:T(8,128)} %observed_ref.3, pred[]{:T(512)S(6)} %eq.169), kind=kLoop, calls=%fused_computation.46 | loop fusion | flops 32768 | bytes 262145 | tf_op jit(solution)/shard_map/jit(_where)/select_n | solution.py:53
  8.8 1.9 %collective-permute-start.4 = (f32[2,16,512]{2,1,0:T(8,128)}, f32[2,16,512]{2,1,0:T(8,128)S(1)}, u32[]{:S(2)}, u32[]{:S(2)}) collective-permute-start(f32[2,16,512]{2,1,0:T(8,128)} %get-tuple-element.52), channel_id=1, source_target_pairs={{1,2},{2,1},{5,6},{6,5},{9,10},{10,9},{13,14},{14,13},{17,18},{18,... | collective-permute-start | bytes 196616 | tf_op jit(solution)/shard_map/ppermute | solution.py:54
  10.8 0.7 broadcast_multiply_fusion
  11.5 0.7 add.129
  12.6 0.7 broadcast_in_dim.285
  13.3 5.5 %all-to-all-start.1 = ((f32[8,8,128]{2,1,0:T(8,128)}), f32[8,8,128]{2,1,0:T(8,128)S(1)}, u32[]{:S(2)}, u32[]{:S(2)}) async-start(f32[8,8,128]{2,1,0:T(8,128)} %broadcast_in_dim.285), calls=%async_computation.1 | async-start | bytes 65536 | tf_op jit(solution)/shard_map/all_to_all | solution.py:229
  18.8 0.7 convert_bitcast_fusion
  23.9 1.4 %fusion = bf16[256,256,12]{1,2,0:T(8,128)(2,1)S(1)} fusion(s32[256,256]{1,0:T(8,128)S(1)} %multiply_add_fusion, bf16[12,21]{1,0:T(8,128)(2,1)S(1)} %copy-done), kind=kOutput, calls=%fused_computation.2 | convolution fusion | flops 34406400 | bytes 1835512 | tf_op jit(solution)/shard_map/mt,tij->mij/dot_general | solution.py:32
  25.3 1.4 %fusion.1 = bf16[256,256,12]{1,2,0:T(8,128)(2,1)S(1)} fusion(s32[256,256]{1,0:T(8,128)S(1)} %fusion.31, bf16[12,21]{1,0:T(8,128)(2,1)S(1)} %copy-done), kind=kOutput, calls=%fused_computation.3 | convolution fusion | flops 34406400 | bytes 1835512 | tf_op jit(solution)/shard_map/mt,tij->mij/dot_general | solution.py:32
  26.8 2.0 %fusion.9 = bf16[12,160,192]{2,0,1:T(8,128)(2,1)} fusion(s32[160,192]{1,0:T(8,128)S(1)} %subtract_add_fusion, bf16[12,21]{1,0:T(8,128)(2,1)S(1)} %copy-done.21), kind=kOutput, calls=%fused_computation.14 | convolution fusion | flops 16496640 | bytes 860664 | tf_op jit(solution)/shard_map/mt,tij->mij/dot_general | solution.py:32
  28.8 2.8 %fusion.7 = (bf16[12,256,256]{2,1,0:T(8,128)(2,1)}, bf16[12,256,256]{2,1,0:T(8,128)(2,1)}) fusion(bf16[256,256,12]{1,2,0:T(8,128)(2,1)S(1)} %fusion, bf16[256,256,12]{1,2,0:T(8,128)(2,1)S(1)} %fusion.1), kind=kLoop, calls=%fused_computation.12 | loop fusion | bytes 6291456 | tf_op jit(solution)/shard_map/convert_element_type | solution.py:32
  31.6 2.3 %select_convert_fusion.side_ref = bf16[128,1920]{1,0:T(8,128)(2,1)} fusion(bf16[1920]{0:T(1024)(128)(2,1)S(1)} %broadcast_in_dim.281, bf16[1920]{0:T(1024)(128)(2,1)S(1)} %broadcast_in_dim.278, bf16[1920]{0:T(1024)(128)(2,1)S(1)} %broadcast_in_dim.275, bf16[1920]{0:T(1024)(128)(2,1)S(1)} %broadcast_in_dim.272, bf16[1920]{0:T(1024)(128)(2,1)S(1)} %broadcast_in_dim.269, ...), kind=kLoop, calls=%fused_computation.15 | loop fusion | flops 10813440 | bytes 589952 | tf_op jit(solution)/shard_map/convert_element_type | solution.py:43
  33.9 2.7 %copy.18 = bf16[12,160,192]{2,1,0:T(8,128)(2,1)} copy(bf16[12,160,192]{2,0,1:T(8,128)(2,1)} %fusion.9) | data formatting | bytes 1474560 | tf_op jit(solution)/shard_map/convert_element_type | solution.py:32
  37.3 5.4 %all-to-all-start = ((bf16[8,64,128]{2,1,0:T(8,128)(2,1)}), bf16[8,64,128]{2,1,0:T(8,128)(2,1)S(1)}, u32[]{:S(2)}, u32[]{:S(2)}) async-start(bf16[8,64,128]{2,1,0:T(8,128)(2,1)} %broadcast_in_dim.219), calls=%async_computation | async-start | bytes 262144 | tf_op jit(solution)/shard_map/all_to_all | solution.py:229
  44.1 4.9 %all-to-all-done = bf16[8,64,128]{2,1,0:T(8,128)(2,1)S(1)} async-done(((bf16[8,64,128]{2,1,0:T(8,128)(2,1)}), bf16[8,64,128]{2,1,0:T(8,128)(2,1)S(1)}, u32[]{:S(2)}, u32[]{:S(2)}) %all-to-all-start) | async-done | bytes 131104 | tf_op jit(solution)/shard_map/all_to_all | solution.py:229
  49.0 0.7 picture.2
  49.7 2.5 %collective-permute-start = (bf16[2,32,512]{2,1,0:T(8,128)(2,1)S(1)}, bf16[2,32,512]{2,1,0:T(8,128)(2,1)S(1)}, u32[]{:S(2)}, u32[]{:S(2)}) collective-permute-start(bf16[2,32,512]{2,1,0:T(8,128)(2,1)S(1)} %get-tuple-element.15), channel_id=1, source_target_pairs={{0,1},{2,3},{1,0},{3,2},{4,5},{6,7},{5,4},{7,6},{8,9},{10,11},{9,8... | collective-permute-start | bytes 196616 | tf_op jit(solution)/shard_map/ppermute | solution.py:274
  52.2 3.2 %collective-permute-start.1 = (bf16[2,32,512]{2,1,0:T(8,128)(2,1)S(1)}, bf16[2,32,512]{2,1,0:T(8,128)(2,1)S(1)}, u32[]{:S(2)}, u32[]{:S(2)}) collective-permute-start(bf16[2,32,512]{2,1,0:T(8,128)(2,1)S(1)} %get-tuple-element.16), channel_id=1, source_target_pairs={{1,2},{2,1},{5,6},{6,5},{9,10},{10,9},{13,14},{14,13},{17,18},{18,... | collective-permute-start | bytes 196616 | tf_op jit(solution)/shard_map/ppermute | solution.py:273
  55.4 1.2 broadcast_select_fusion
  56.6 1.2 collective-permute-done.1.far_ref
  57.8 1.4 %copy-done.4 = bf16[12,256,256]{2,1,0:T(8,128)(2,1)S(1)} copy-done((bf16[12,256,256]{2,1,0:T(8,128)(2,1)S(1)}, bf16[12,256,256]{2,1,0:T(8,128)(2,1)}, u32[]{:S(2)}) %copy-start.4) | copy-done | bytes 1572888
  59.2 1.2 copy-done.6
  60.4 1.0 copy-done.8
  61.4 1.0 copy-done.12
  62.5 0.8 copy-done.14
  63.2 0.8 copy-done.16
  64.1 0.8 copy-done.18
  64.9 11.2 %step.2 = (f32[2,128,512]{2,1,0:T(8,128)}, f32[512,128]{1,0:T(8,128)S(1)}) custom-call(s32[1]{0:T(128)} %bitcast.1.even_ref, s32[128]{0:T(128)S(1)} %reshape.164.ids_ref, bf16[2,128,512]{2,1,0:T(8,128)(2,1)S(1)} %get-tuple-element.14.picture_ref, bf16[2,32,512]{2,1,0:T(8,128)(2,1)S(1)} %collective-permute-done.near_ref, ...), custom_call_target="tpu_custom_call" | custom-call | tf_op jit(solution)/shard_map/step/pallas_call | solution.py:275
  76.1 10.1 %all_to_all.47 = f32[8,64,128]{2,1,0:T(8,128)} all-to-all(f32[8,64,128]{2,1,0:T(8,128)S(1)} %bitcast.36), channel_id=1, replica_groups=mesh['exp'=8,'sub'=4] {'exp'}, dimensions={0} | all-to-all | bytes 524288 | tf_op jit(solution)/shard_map/all_to_all | solution.py:229
  86.2 1.6 %update.2 = (f32[64,128]{1,0:T(8,128)}, bf16[512,128]{1,0:T(8,128)(2,1)}) custom-call(f32[64,128]{1,0:T(8,128)} %bitcast.39, f32[512,128]{1,0:T(8,128)} %bitcast.38, f32[64,128]{1,0:T(8,128)} %broadcast_bitcast_fusion.counted_ref.counts_ref), custom_call_target="tpu_custom_call" | custom-call | tf_op jit(solution)/shard_map/update/pallas_call | solution.py:296
  87.9 9.5 %all_to_all.48 = bf16[8,64,128]{2,1,0:T(8,128)(2,1)S(1)} all-to-all(bf16[8,64,128]{2,1,0:T(8,128)(2,1)} %bitcast.40), channel_id=1, replica_groups=mesh['exp'=8,'sub'=4] {'exp'}, dimensions={0} | all-to-all | bytes 262144 | tf_op jit(solution)/shard_map/all_to_all | solution.py:229
  97.4 0.7 picture.3
  98.1 5.5 %collective-permute-start.7 = (bf16[2,32,512]{2,1,0:T(8,128)(2,1)S(1)}, bf16[2,32,512]{2,1,0:T(8,128)(2,1)S(1)}, u32[]{:S(2)}, u32[]{:S(2)}) collective-permute-start(bf16[2,32,512]{2,1,0:T(8,128)(2,1)S(1)} %get-tuple-element.22), channel_id=1, source_target_pairs={{1,2},{2,1},{5,6},{6,5},{9,10},{10,9},{13,14},{14,13},{17,18},{18,... | collective-permute-start | bytes 196616 | tf_op jit(solution)/shard_map/ppermute | solution.py:273
  103.6 1.9 %collective-permute-done.7.far_ref = bf16[2,32,512]{2,1,0:T(8,128)(2,1)S(1)} collective-permute-done((bf16[2,32,512]{2,1,0:T(8,128)(2,1)S(1)}, bf16[2,32,512]{2,1,0:T(8,128)(2,1)S(1)}, u32[]{:S(2)}, u32[]{:S(2)}) %collective-permute-start.7) | collective-permute-done | bytes 65568 | tf_op jit(solution)/shard_map/ppermute | solution.py:273
  105.6 1.4 %copy-done.3 = bf16[12,256,256]{2,1,0:T(8,128)(2,1)S(1)} copy-done((bf16[12,256,256]{2,1,0:T(8,128)(2,1)S(1)}, bf16[12,256,256]{2,1,0:T(8,128)(2,1)}, u32[]{:S(2)}) %copy-start.3) | copy-done | bytes 1572888
  107.0 1.4 %copy-done.5 = bf16[12,256,256]{2,1,0:T(8,128)(2,1)S(1)} copy-done((bf16[12,256,256]{2,1,0:T(8,128)(2,1)S(1)}, bf16[12,256,256]{2,1,0:T(8,128)(2,1)}, u32[]{:S(2)}) %copy-start.5) | copy-done | bytes 1572888
  108.4 1.2 copy-done.7
  109.6 1.0 copy-done.9
  110.6 1.0 copy-done.11
  111.6 1.0 copy-done.13
  112.6 0.8 copy-done.15
  113.4 0.8 copy-done.17
  114.2 0.8 copy-done.19
  115.1 11.2 %step.3 = (f32[2,128,512]{2,1,0:T(8,128)}, f32[512,128]{1,0:T(8,128)S(1)}) custom-call(s32[1]{0:T(128)} %bitcast.1.even_ref, s32[128]{0:T(128)S(1)} %reshape.164.ids_ref, bf16[2,128,512]{2,1,0:T(8,128)(2,1)S(1)} %get-tuple-element.20.picture_ref, bf16[2,32,512]{2,1,0:T(8,128)(2,1)S(1)} %collective-permute-done.6.near_ref, ...), custom_call_target="tpu_custom_call" | custom-call | tf_op jit(solution)/shard_map/step/pallas_call | solution.py:275
  126.3 10.1 %all_to_all.49 = f32[8,64,128]{2,1,0:T(8,128)} all-to-all(f32[8,64,128]{2,1,0:T(8,128)S(1)} %bitcast.35), channel_id=1, replica_groups=mesh['exp'=8,'sub'=4] {'exp'}, dimensions={0} | all-to-all | bytes 524288 | tf_op jit(solution)/shard_map/all_to_all | solution.py:229
  136.4 1.6 %update.3 = (f32[64,128]{1,0:T(8,128)}, bf16[512,128]{1,0:T(8,128)(2,1)}) custom-call(f32[64,128]{1,0:T(8,128)} %get-tuple-element.18.sky_ref, f32[512,128]{1,0:T(8,128)} %bitcast.37, f32[64,128]{1,0:T(8,128)} %broadcast_bitcast_fusion.counted_ref.counts_ref), custom_call_target="tpu_custom_call" | custom-call | tf_op jit(solution)/shard_map/update/pallas_call | solution.py:296
  (97 shorter events, 6.9 us)
Async XLA Ops:
  0.6 23.3 %copy-start = (bf16[12,21]{1,0:T(8,128)(2,1)S(1)}, bf16[12,21]{1,0:T(8,128)(2,1)}, u32[]{:S(2)}) copy-start(bf16[12,21]{1,0:T(8,128)(2,1)} %param.11) | copy-start | bytes 1516
  2.7 52.7 %collective-permute-start.2 = (bf16[2,12,16,512]{3,2,1,0:T(8,128)(2,1)}, bf16[2,12,16,512]{3,2,1,0:T(8,128)(2,1)}, u32[]{:S(2)}, u32[]{:S(2)}) collective-permute-start(bf16[2,12,16,512]{3,2,1,0:T(8,128)(2,1)} %get-tuple-element.48), channel_id=1, source_target_pairs={{1,2},{2,1},{5,6},{6,5},{9,10},{10,9},{13,14},{14,13},{17,18},{18,... | collective-permute-start | bytes 1179656 | tf_op jit(solution)/shard_map/ppermute | solution.py:54
  7.3 48.1 %collective-permute-start.3 = (bf16[2,12,16,512]{3,2,1,0:T(8,128)(2,1)}, bf16[2,12,16,512]{3,2,1,0:T(8,128)(2,1)}, u32[]{:S(2)}, u32[]{:S(2)}) collective-permute-start(bf16[2,12,16,512]{3,2,1,0:T(8,128)(2,1)} %get-tuple-element.47), channel_id=1, source_target_pairs={{0,1},{2,3},{1,0},{3,2},{4,5},{6,7},{5,4},{7,6},{8,9},{10,11},{9,8... | collective-permute-start | bytes 1179656 | tf_op jit(solution)/shard_map/ppermute | solution.py:53
  8.8 34.6 %collective-permute-start.4 = (f32[2,16,512]{2,1,0:T(8,128)}, f32[2,16,512]{2,1,0:T(8,128)S(1)}, u32[]{:S(2)}, u32[]{:S(2)}) collective-permute-start(f32[2,16,512]{2,1,0:T(8,128)} %get-tuple-element.52), channel_id=1, source_target_pairs={{1,2},{2,1},{5,6},{6,5},{9,10},{10,9},{13,14},{14,13},{17,18},{18,... | collective-permute-start | bytes 196616 | tf_op jit(solution)/shard_map/ppermute | solution.py:54
  10.8 32.6 %collective-permute-start.5 = (f32[2,16,512]{2,1,0:T(8,128)S(1)}, f32[2,16,512]{2,1,0:T(8,128)S(1)}, u32[]{:S(2)}, u32[]{:S(2)}) collective-permute-start(f32[2,16,512]{2,1,0:T(8,128)S(1)} %get-tuple-element.51), channel_id=1, source_target_pairs={{0,1},{2,3},{1,0},{3,2},{4,5},{6,7},{5,4},{7,6},{8,9},{10,11},{9,8... | collective-permute-start | bytes 196616 | tf_op jit(solution)/shard_map/ppermute | solution.py:53
  13.3 23.4 %all-to-all-start.1 = ((f32[8,8,128]{2,1,0:T(8,128)}), f32[8,8,128]{2,1,0:T(8,128)S(1)}, u32[]{:S(2)}, u32[]{:S(2)}) async-start(f32[8,8,128]{2,1,0:T(8,128)} %broadcast_in_dim.285), calls=%async_computation.1 | async-start | bytes 65536 | tf_op jit(solution)/shard_map/all_to_all | solution.py:229
  23.9 2.9 %copy-start.21 = (bf16[12,21]{1,0:T(8,128)(2,1)S(1)}, bf16[12,21]{1,0:T(8,128)(2,1)}, u32[]{:S(2)}) copy-start(bf16[12,21]{1,0:T(8,128)(2,1)} %param.10) | copy-start | bytes 1516
  28.8 5.2 %copy-start.20 = (f32[1,8,8,128]{3,2,1,0:T(8,128)S(1)}, f32[1,8,8,128]{3,2,1,0:T(8,128)}, u32[]{:S(2)}) copy-start(f32[1,8,8,128]{3,2,1,0:T(8,128)} %param.7) | copy-start | bytes 98308
  33.9 23.8 %copy-start.1 = (bf16[2,12,128,512]{3,2,1,0:T(8,128)(2,1)S(1)}, bf16[2,12,128,512]{3,2,1,0:T(8,128)(2,1)}, u32[]{:S(2)}) copy-start(bf16[2,12,128,512]{3,2,1,0:T(8,128)(2,1)} %coeffs_ref.3) | copy-start | bytes 9437188
  37.3 11.6 %all-to-all-start = ((bf16[8,64,128]{2,1,0:T(8,128)(2,1)}), bf16[8,64,128]{2,1,0:T(8,128)(2,1)S(1)}, u32[]{:S(2)}, u32[]{:S(2)}) async-start(bf16[8,64,128]{2,1,0:T(8,128)(2,1)} %broadcast_in_dim.219), calls=%async_computation | async-start | bytes 262144 | tf_op jit(solution)/shard_map/all_to_all | solution.py:229
  49.0 8.8 %copy-start.2 = (bf16[12,256,256]{2,1,0:T(8,128)(2,1)S(1)}, bf16[12,256,256]{2,1,0:T(8,128)(2,1)}, u32[]{:S(2)}) copy-start(bf16[12,256,256]{2,1,0:T(8,128)(2,1)} %get-tuple-element.57.forward_ref) | copy-start | bytes 4718596
  49.7 6.9 %collective-permute-start = (bf16[2,32,512]{2,1,0:T(8,128)(2,1)S(1)}, bf16[2,32,512]{2,1,0:T(8,128)(2,1)S(1)}, u32[]{:S(2)}, u32[]{:S(2)}) collective-permute-start(bf16[2,32,512]{2,1,0:T(8,128)(2,1)S(1)} %get-tuple-element.15), channel_id=1, source_target_pairs={{0,1},{2,3},{1,0},{3,2},{4,5},{6,7},{5,4},{7,6},{8,9},{10,11},{9,8... | collective-permute-start | bytes 196616 | tf_op jit(solution)/shard_map/ppermute | solution.py:274
  52.2 5.6 %collective-permute-start.1 = (bf16[2,32,512]{2,1,0:T(8,128)(2,1)S(1)}, bf16[2,32,512]{2,1,0:T(8,128)(2,1)S(1)}, u32[]{:S(2)}, u32[]{:S(2)}) collective-permute-start(bf16[2,32,512]{2,1,0:T(8,128)(2,1)S(1)} %get-tuple-element.16), channel_id=1, source_target_pairs={{1,2},{2,1},{5,6},{6,5},{9,10},{10,9},{13,14},{14,13},{17,18},{18,... | collective-permute-start | bytes 196616 | tf_op jit(solution)/shard_map/ppermute | solution.py:273
  56.6 19.5 %copy-start.10 = (bf16[2,12,16,512]{3,2,1,0:T(8,128)(2,1)}, bf16[2,12,16,512]{3,2,1,0:T(8,128)(2,1)S(1)}, u32[]{:S(2)}) copy-start(bf16[2,12,16,512]{3,2,1,0:T(8,128)(2,1)S(1)} %get-tuple-element.50.coeffs_up_ref) | copy-start | bytes 1179652
  57.8 1.4 %copy-start.4 = (bf16[12,256,256]{2,1,0:T(8,128)(2,1)S(1)}, bf16[12,256,256]{2,1,0:T(8,128)(2,1)}, u32[]{:S(2)}) copy-start(bf16[12,256,256]{2,1,0:T(8,128)(2,1)} %get-tuple-element.58.backward_ref) | copy-start | bytes 4718596
  59.2 1.2 copy-start.6
  60.4 1.0 copy-start.8
  61.4 1.0 copy-start.12
  62.5 0.8 copy-start.14
  63.2 0.8 copy-start.16
  64.1 0.8 copy-start.18
  98.0 5.6 %collective-permute-start.6 = (bf16[2,32,512]{2,1,0:T(8,128)(2,1)S(1)}, bf16[2,32,512]{2,1,0:T(8,128)(2,1)S(1)}, u32[]{:S(2)}, u32[]{:S(2)}) collective-permute-start(bf16[2,32,512]{2,1,0:T(8,128)(2,1)S(1)} %get-tuple-element.21), channel_id=1, source_target_pairs={{0,1},{2,3},{1,0},{3,2},{4,5},{6,7},{5,4},{7,6},{8,9},{10,11},{9,8... | collective-permute-start | bytes 196616 | tf_op jit(solution)/shard_map/ppermute | solution.py:274
  98.1 7.4 %collective-permute-start.7 = (bf16[2,32,512]{2,1,0:T(8,128)(2,1)S(1)}, bf16[2,32,512]{2,1,0:T(8,128)(2,1)S(1)}, u32[]{:S(2)}, u32[]{:S(2)}) collective-permute-start(bf16[2,32,512]{2,1,0:T(8,128)(2,1)S(1)} %get-tuple-element.22), channel_id=1, source_target_pairs={{1,2},{2,1},{5,6},{6,5},{9,10},{10,9},{13,14},{14,13},{17,18},{18,... | collective-permute-start | bytes 196616 | tf_op jit(solution)/shard_map/ppermute | solution.py:273
  105.5 1.4 %copy-start.3 = (bf16[12,256,256]{2,1,0:T(8,128)(2,1)S(1)}, bf16[12,256,256]{2,1,0:T(8,128)(2,1)}, u32[]{:S(2)}) copy-start(bf16[12,256,256]{2,1,0:T(8,128)(2,1)} %get-tuple-element.57.forward_ref) | copy-start | bytes 4718596
  107.0 1.4 %copy-start.5 = (bf16[12,256,256]{2,1,0:T(8,128)(2,1)S(1)}, bf16[12,256,256]{2,1,0:T(8,128)(2,1)}, u32[]{:S(2)}) copy-start(bf16[12,256,256]{2,1,0:T(8,128)(2,1)} %get-tuple-element.58.backward_ref) | copy-start | bytes 4718596
  108.4 1.2 copy-start.7
  109.6 1.0 copy-start.9
  110.6 1.0 copy-start.11
  111.6 1.0 copy-start.13
  112.6 0.8 copy-start.15
  113.4 0.8 copy-start.17
  114.2 0.8 copy-start.19

commit v2 on v1

v2 whole, which is shorter than its diff:
```python
import functools

import jax
import jax.numpy as jnp
from jax import lax
from jax.experimental import pallas as pl
from jax.experimental.pallas import tpu as pltpu
from jax.sharding import PartitionSpec as P

STEPS = 2
ETA = 0.5
DELTA = 1.0
ROWS = 16
LANES = 128
PARTS = 3
F32 = jnp.float32
BF16 = jnp.bfloat16


def round_up(value, unit):
    return -(-value // unit) * unit


def divisor(value, most):
    return max(k for k in range(1, most + 1) if value % k == 0)


def pair_routes(axis):
    count = lax.axis_size(axis)
    routes = []
    for first in (0, 1):
        pairs = [(k, k + 1) for k in range(first, count - 1, 2)]
        routes.append(pairs + [(b, a) for a, b in pairs])
    return routes


def rims_kernel(even_ref, coeffs_ref, observed_ref, near_ref, far_ref, seen_ref, sems):
    modes, height = coeffs_ref.shape[1:3]
    ext = near_ref.shape[2]
    even = even_ref[0]
    near_at = pl.multiple_of(even * (height - ext), ROWS)
    far_at = pl.multiple_of((1 - even) * (height - ext), ROWS)
    copies = []
    for side, (start, out_ref) in enumerate(((near_at, near_ref), (far_at, far_ref))):
        copies.append(
            pltpu.make_async_copy(observed_ref.at[:, pl.ds(start, ext), :], seen_ref.at[side], sems.at[2 * side])
        )
        copies.append(
            pltpu.make_async_copy(
                coeffs_ref.at[:, :, pl.ds(start, ext), :], out_ref.at[:, pl.ds(0, modes)], sems.at[2 * side + 1]
            )
        )
    for copy in copies:
        copy.start()
    for side, out_ref in enumerate((near_ref, far_ref)):
        copies[2 * side].wait()
        rest = seen_ref[side]
        for part in range(PARTS):
            piece = rest.astype(BF16)
            out_ref[:, modes + part] = piece
            rest = rest - piece.astype(F32)
    copies[1].wait()
    copies[3].wait()


def prep_kernel(
    owners_ref, offset_ref, vert_ref, horiz_ref, vertical_ref, side_ref, forward_ref, backward_ref, counted_ref,
    taps_ref, turned_ref, *, ext, rim, per_tile,
):
    modes, taps = vert_ref.shape
    margin = (taps - 1) // 2
    width = forward_ref.shape[1]
    height = side_ref.shape[0]
    tall = vertical_ref.shape[0] // modes
    reach = vertical_ref.shape[1]

    taps_ref[...] = jnp.zeros(taps_ref.shape, F32)
    taps_ref[0, :modes, :taps] = vert_ref[...].astype(F32)
    taps_ref[1, :modes, :taps] = horiz_ref[...].astype(F32)
    turn = lax.broadcasted_iota(jnp.int32, (LANES, LANES), 0) + lax.broadcasted_iota(jnp.int32, (LANES, LANES), 1)
    flipped = jnp.dot(
        taps_ref[1].astype(BF16), (turn == taps - 1).astype(F32).astype(BF16), preferred_element_type=F32
    )
    taps_ref[2] = flipped

    def banded(row, shift, rows, cols):
        turned = pltpu.roll(jnp.broadcast_to(row, (8, LANES)), (-shift) % LANES, 1)
        ring = pltpu.roll(jnp.broadcast_to(turned[:1], (LANES, LANES)), 0, 1, stride=1, stride_axis=0)
        lag = (
            lax.broadcasted_iota(jnp.int32, (rows, cols), 1) - lax.broadcasted_iota(jnp.int32, (rows, cols), 0) + shift
        )
        across = jnp.concatenate([ring] * (-(-cols // LANES)), axis=1)[:, :cols]
        whole = jnp.concatenate([across] * (-(-rows // LANES)), axis=0)[:rows]
        return jnp.where((lag >= 0) & (lag < taps), whole, 0.0)

    for mode in range(modes):
        row = taps_ref[0, mode : mode + 1]
        place = slice(mode * tall, (mode + 1) * tall)
        vertical_ref[place, :] = banded(row, margin + ext - rim, tall, reach).astype(BF16)
        turned_ref[place, :] = banded(row, margin + ext, tall, height)
        backward_ref[mode] = banded(taps_ref[1, mode : mode + 1], margin, width, width).astype(BF16)
        forward_ref[mode] = banded(taps_ref[2, mode : mode + 1], margin, width, width).astype(BF16)
    side_ref[...] = turned_ref[...].T.astype(BF16)

    counted_ref[...] = jnp.zeros(counted_ref.shape, F32)
    for piece in range(offset_ref.shape[0]):
        for row in range(offset_ref.shape[1]):
            for col in range(offset_ref.shape[2]):
                index = owners_ref[piece, row, col, 0] * per_tile + offset_ref[piece, row, col]
                counted_ref[pl.ds(index, 1), :] += 1.0


def picture_kernel(even_ref, owners_ref, offset_ref, tiles_ref, picture_ref, near_ref, far_ref, wide_ref, *, patch, per_tile):
    pieces, height, breadth = picture_ref.shape
    rim = near_ref.shape[1]
    patch_rows, patch_cols = patch
    wide_ref[...] = tiles_ref[...].astype(F32)
    cols = breadth // patch_cols
    rows = height // patch_rows
    together = ROWS // patch_rows
    for piece in range(pieces):
        for row in range(0, rows, together):
            for col in range(cols):
                parts = []
                for inner in range(row, row + together):
                    index = owners_ref[piece, inner, col, 0] * per_tile + offset_ref[piece, inner, col]
                    start = pl.multiple_of(index * patch_rows, patch_rows)
                    parts.append(wide_ref[pl.ds(start, patch_rows), :])
                picture_ref[
                    piece, row * patch_rows : (row + together) * patch_rows, col * patch_cols : (col + 1) * patch_cols
                ] = jnp.concatenate(parts, axis=0).astype(BF16)
    even = even_ref[0]
    near_ref[...] = picture_ref[:, pl.ds(pl.multiple_of(even * (height - rim), ROWS), rim), :]
    far_ref[...] = picture_ref[:, pl.ds(pl.multiple_of((1 - even) * (height - rim), ROWS), rim), :]


def windows_of(block, width, stride):
    count = max(1, (block.shape[1] - width) // stride + 1)
    return [block[:, k * stride : k * stride + width] for k in range(count)]


def joined(outs, width, stride):
    if len(outs) == 1:
        return [outs[0][:, k : k + stride] for k in range(0, width, stride)]
    lane = lax.broadcasted_iota(jnp.int32, (outs[0].shape[0], stride), 1)
    blocks = [outs[0][:, :stride]]
    for left, right in zip(outs[:-1], outs[1:]):
        blocks.append(jnp.where(lane < stride // 2, left[:, stride:], right[:, :stride]))
    blocks.append(outs[-1][:, stride:])
    return blocks


def step_kernel(
    even_ref, owners_ref, offset_ref, picture_ref, near_ref, far_ref, counted_ref, coeffs_any, rims_near_any,
    rims_far_any, observed_any, vertical_any, side_any, forward_any, backward_any,
    clipped_ref, sums_ref, image_ref, field_ref, model_ref, gradient_ref, coeffs_ref, seen_ref, seen_rims_ref,
    vertical_ref, side_ref, forward_ref, backward_ref, sems, *, patch, per_tile, slot,
):
    pieces, height, breadth = picture_ref.shape
    modes = coeffs_ref.shape[1]
    rim = near_ref.shape[1]
    tall = coeffs_ref.shape[2]
    ext = (tall - height) // 2
    patch_rows, patch_cols = patch
    width = forward_ref.shape[1]
    stride = patch_cols
    even = even_ref[0]
    near_at = pl.multiple_of(even * (ext + height), ROWS)
    far_at = pl.multiple_of((1 - even) * (ext + height), ROWS)

    moves = [
        (vertical_any, vertical_ref),
        (forward_any, forward_ref),
        (coeffs_any, coeffs_ref.at[:, :, pl.ds(ext, height), :]),
        (rims_near_any.at[:, pl.ds(0, modes)], coeffs_ref.at[:, :, pl.ds(near_at, ext), :]),
        (rims_far_any.at[:, pl.ds(0, modes)], coeffs_ref.at[:, :, pl.ds(far_at, ext), :]),
        (observed_any, seen_ref.at[:, pl.ds(ext, height), :]),
        (rims_near_any.at[:, pl.ds(modes, PARTS)], seen_rims_ref.at[0]),
        (rims_far_any.at[:, pl.ds(modes, PARTS)], seen_rims_ref.at[1]),
        (backward_any, backward_ref),
        (side_any, side_ref),
    ]
    copies = [pltpu.make_async_copy(source, target, sems.at[k]) for k, (source, target) in enumerate(moves)]
    for copy in copies:
        copy.start()

    image_ref[:, rim : rim + height, :] = picture_ref[...]
    image_ref[:, pl.ds(pl.multiple_of(even * (rim + height), ROWS), rim), :] = near_ref[...]
    image_ref[:, pl.ds(pl.multiple_of((1 - even) * (rim + height), ROWS), rim), :] = far_ref[...]

    group = divisor(modes, 4)
    chunk = group * tall
    copies[0].wait()
    for start in range(0, modes * tall, chunk):
        table = vertical_ref[start : start + chunk, :]
        for piece in range(pieces):
            for low in range(0, breadth, width):
                field_ref[piece, start : start + chunk, low : low + width] = jnp.dot(
                    table, image_ref[piece, :, low : low + width], preferred_element_type=F32
                ).astype(BF16)

    def blur(table, blocks):
        cuts = [cut for block in blocks for cut in windows_of(block, width, stride)]
        result = jnp.dot(jnp.concatenate(cuts, axis=0), table, preferred_element_type=F32)
        per = len(cuts) // len(blocks)
        outs = [result[k * tall : (k + 1) * tall] for k in range(len(cuts))]
        return [joined(outs[k * per : (k + 1) * per], width, stride) for k in range(len(blocks))]

    for k in range(1, 5):
        copies[k].wait()
    for mode in range(modes):
        start = mode * tall
        blocks = [field_ref[piece, start : start + tall, :] for piece in range(pieces)]
        for piece, columns in enumerate(blur(forward_ref[mode], blocks)):
            weight = coeffs_ref[piece, mode].astype(F32)
            for k, column in enumerate(columns):
                place = slice(k * stride, (k + 1) * stride)
                if mode == 0:
                    model_ref[piece, :, place] = weight[:, place] * column
                else:
                    model_ref[piece, :, place] += weight[:, place] * column
    for k in range(5, 8):
        copies[k].wait()
    for side, start in enumerate((near_at, far_at)):
        total = seen_rims_ref[side, :, 0].astype(F32)
        for part in range(1, PARTS):
            total = total + seen_rims_ref[side, :, part].astype(F32)
        seen_ref[:, pl.ds(start, ext), :] = total
    model_ref[...] = jnp.clip(model_ref[...] - seen_ref[...], -DELTA, DELTA)
    clipped_ref[...] = model_ref[:, ext : ext + height, :]

    copies[8].wait()
    for mode in range(modes):
        start = mode * tall
        blocks = [(coeffs_ref[piece, mode].astype(F32) * model_ref[piece]).astype(BF16) for piece in range(pieces)]
        for piece, columns in enumerate(blur(backward_ref[mode], blocks)):
            for k, column in enumerate(columns):
                field_ref[piece, start : start + tall, k * stride : (k + 1) * stride] = column.astype(BF16)
    copies[9].wait()
    for piece in range(pieces):
        for low in range(0, breadth, width):
            gradient_ref[piece, :, low : low + width] = jnp.dot(
                side_ref[...], field_ref[piece, :, low : low + width], preferred_element_type=F32
            )
    sums_ref[...] = jnp.zeros(sums_ref.shape, F32)
    if slot > per_tile * patch_rows:
        for owner in range(sums_ref.shape[0] // slot):
            start = owner * slot + per_tile * patch_rows
            sums_ref[start : start + per_tile, :] = counted_ref[owner * per_tile : (owner + 1) * per_tile, :]
    cols = breadth // patch_cols
    rows = height // patch_rows
    for row in range(rows):
        for col in range(cols):
            for piece in range(pieces):
                index = owners_ref[piece, row, col, 0] * slot + offset_ref[piece, row, col] * patch_rows
                place = pl.ds(pl.multiple_of(index, patch_rows), patch_rows)
                sums_ref[place, :] += gradient_ref[
                    piece, row * patch_rows : (row + 1) * patch_rows, col * patch_cols : (col + 1) * patch_cols
                ]


def update_kernel(sky_ref, parts_ref, *refs, slot, first, last):
    refs = list(refs)
    held = sky_ref.shape[0]
    total = parts_ref[:slot, :]
    for start in range(slot, parts_ref.shape[0], slot):
        total = total + parts_ref[start : start + slot, :]
    if first:
        named = total[held:]
        repeat = held // named.shape[0]
        counts = jnp.broadcast_to(named[:, None, :], (named.shape[0], repeat, named.shape[1])).reshape(sky_ref.shape)
        refs.pop()[...] = counts
    else:
        counts = refs.pop(0)[...]
    fresh = sky_ref[...] - ETA * total[:held] / jnp.maximum(counts, 1.0)
    refs[0][...] = fresh
    if not last:
        for start in range(0, refs[1].shape[0], held):
            refs[1][start : start + held, :] = fresh.astype(BF16)


def per_device(sky_map, coeffs, observed, vert_taps, horiz_taps, owner_ids, offset):
    pieces, height, breadth = observed.shape
    modes = coeffs.shape[1]
    per_tile, patch_rows, patch_cols = sky_map.shape[1:]
    patch = (patch_rows, patch_cols)
    margin = (vert_taps.shape[1] - 1) // 2
    exp_count = lax.axis_size("exp")
    held = per_tile * patch_rows
    known = exp_count * held
    ext = round_up(margin, ROWS)
    rim = round_up(ext + margin, ROWS)
    tall = height + 2 * ext
    width = min(breadth, 2 * patch_cols)
    routes = pair_routes("sub")
    vmem = pl.BlockSpec(memory_space=pltpu.VMEM)
    smem = pl.BlockSpec(memory_space=pltpu.SMEM)
    somewhere = pl.BlockSpec(memory_space=pl.ANY)

    def exchange(block):
        return lax.all_to_all(block, "exp", split_axis=0, concat_axis=0, tiled=True)

    sky = sky_map.reshape(held, patch_cols)
    spread = jnp.broadcast_to(sky.astype(BF16)[None], (exp_count, held, patch_cols)).reshape(known, patch_cols)
    tiles = exchange(spread)
    even = (1 - lax.axis_index("sub") % 2).astype(jnp.int32).reshape(1)

    rim_shape = jax.ShapeDtypeStruct((pieces, modes + PARTS, ext, breadth), BF16)
    rims_near, rims_far = pl.pallas_call(
        rims_kernel,
        out_shape=(rim_shape, rim_shape),
        in_specs=[smem, somewhere, somewhere],
        out_specs=(vmem, vmem),
        scratch_shapes=[pltpu.VMEM((2, pieces, ext, breadth), F32), pltpu.SemaphoreType.DMA((4,))],
        compiler_params=pltpu.CompilerParams(vmem_limit_bytes=8 << 20),
        name="rims",
    )(even, coeffs, observed)
    rims_far = lax.ppermute(rims_far, "sub", routes[1])
    rims_near = lax.ppermute(rims_near, "sub", routes[0])
    vertical, side, forward, backward, counted = pl.pallas_call(
        functools.partial(prep_kernel, ext=ext, rim=rim, per_tile=per_tile),
        out_shape=(
            jax.ShapeDtypeStruct((modes * tall, height + 2 * rim), BF16),
            jax.ShapeDtypeStruct((height, modes * tall), BF16),
            jax.ShapeDtypeStruct((modes, width, width), BF16),
            jax.ShapeDtypeStruct((modes, width, width), BF16),
            jax.ShapeDtypeStruct((exp_count * per_tile, patch_cols), F32),
        ),
        in_specs=[smem, smem, vmem, vmem],
        out_specs=(vmem,) * 5,
        scratch_shapes=[
            pltpu.VMEM((3, round_up(modes, 8), LANES), F32),
            pltpu.VMEM((modes * tall, height), F32),
        ],
        compiler_params=pltpu.CompilerParams(vmem_limit_bytes=16 << 20),
        name="prep",
    )(owner_ids, offset, vert_taps, horiz_taps)

    clipped, counts = None, None
    for step in range(STEPS):
        first, last = step == 0, step + 1 == STEPS
        picture, near, far = pl.pallas_call(
            functools.partial(picture_kernel, patch=patch, per_tile=per_tile),
            out_shape=(
                jax.ShapeDtypeStruct((pieces, height, breadth), BF16),
                jax.ShapeDtypeStruct((pieces, rim, breadth), BF16),
                jax.ShapeDtypeStruct((pieces, rim, breadth), BF16),
            ),
            in_specs=[smem, smem, smem, vmem],
            out_specs=(vmem, vmem, vmem),
            scratch_shapes=[pltpu.VMEM((known, patch_cols), F32)],
            compiler_params=pltpu.CompilerParams(vmem_limit_bytes=8 << 20),
            name="picture",
        )(even, owner_ids, offset, tiles)
        far = lax.ppermute(far, "sub", routes[1])
        near = lax.ppermute(near, "sub", routes[0])
        slot = held + (round_up(per_tile, 8) if first else 0)
        clipped, sums = pl.pallas_call(
            functools.partial(step_kernel, patch=patch, per_tile=per_tile, slot=slot),
            out_shape=(
                jax.ShapeDtypeStruct((pieces, height, breadth), F32),
                jax.ShapeDtypeStruct((exp_count * slot, patch_cols), F32),
            ),
            in_specs=[smem] * 3 + [vmem] * 4 + [somewhere] * 8,
            out_specs=(vmem, vmem),
            scratch_shapes=[
                pltpu.VMEM((pieces, height + 2 * rim, breadth), BF16),
                pltpu.VMEM((pieces, modes * tall, breadth), BF16),
                pltpu.VMEM((pieces, tall, breadth), F32),
                pltpu.VMEM((pieces, height, breadth), F32),
                pltpu.VMEM((pieces, modes, tall, breadth), BF16),
                pltpu.VMEM((pieces, tall, breadth), F32),
                pltpu.VMEM((2, pieces, PARTS, ext, breadth), BF16),
                pltpu.VMEM(vertical.shape, BF16),
                pltpu.VMEM(side.shape, BF16),
                pltpu.VMEM(forward.shape, BF16),
                pltpu.VMEM(backward.shape, BF16),
                pltpu.SemaphoreType.DMA((10,)),
            ],
            compiler_params=pltpu.CompilerParams(vmem_limit_bytes=28 << 20),
            name="step",
        )(
            even, owner_ids, offset, picture, near, far, counted, coeffs, rims_near, rims_far, observed,
            vertical, side, forward, backward,
        )
        parts = exchange(sums)
        sky_shape = jax.ShapeDtypeStruct((held, patch_cols), F32)
        results = [sky_shape]
        if not last:
            results.append(jax.ShapeDtypeStruct((known, patch_cols), BF16))
        if first:
            results.append(sky_shape)
        operands = [sky, parts] if first else [sky, parts, counts]
        answer = pl.pallas_call(
            functools.partial(update_kernel, slot=slot, first=first, last=last),
            out_shape=tuple(results),
            in_specs=[vmem] * len(operands),
            out_specs=(vmem,) * len(results),
            name="update",
        )(*operands)
        sky = answer[0]
        if first:
            counts = answer[-1]
        if not last:
            tiles = exchange(answer[1])
    return sky.reshape(sky_map.shape), clipped


def solution(mesh):
    return jax.shard_map(
        per_device,
        mesh=mesh,
        in_specs=(
            P(("exp", "sub"), None, None, None),
            P("exp", None, "sub", None),
            P("exp", "sub", None),
            P(),
            P(),
            P("exp", "sub", None, None),
            P("exp", "sub", None),
        ),
        out_specs=(P(("exp", "sub"), None, None, None), P("exp", "sub", None)),
        check_vma=False,
    )
```

time: 140 us -> 106 us (0.76)
  local copies, waits for them, and re-layouts: 28.7 us -> 11.4 us
  starting transfers between devices: 28.8 us -> 17.6 us
  other arithmetic: 10 us -> 0.01 us
  Pallas kernels: 27 us -> 34 us
  matrix products: 4.83 us -> 0 us
  blocking collectives: 29.7 us -> 32.4 us
    pallas_call x4 -> x6, Pallas kernels: 4.63 us -> 14.5 us  [the longest x1 5.82 us: per_device(): pl.pallas_call(functools.partial(prep_kernel, ext=ext, rim=rim, per_tile=...]
    unnamed x44 -> x38, local copies, waits for them, and re-layouts: 16.7 us -> 10.7 us
    convert_element_type x2 -> x0, local copies, waits for them, and re-layouts: 5.58 us -> none  [band_table(): jnp.einsum('mt,tij->mij', filters, select, preferred_element_type=F32)]
    all_to_all x2 -> x1, starting transfers between devices: 11 us -> 5.53 us  [exchange(): return lax.all_to_all(block, 'exp', split_axis=0, concat_axis=0, tiled=True)]
    select_n x4 -> x0, other arithmetic: 5.41 us -> none  [the longest x2 3.57 us: swap_rims(): near = lax.ppermute(jnp.where(even, lower, upper), axis, routes[0])]
    dot_general x3 -> x0, matrix products: 4.83 us -> none  [band_table(): jnp.einsum('mt,tij->mij', filters, select, preferred_element_type=F32)]
    broadcast_in_dim x44 -> x0, local copies, waits for them, and re-layouts: 4.27 us -> none  [the longest x42 3.48 us: side_table(): spread = jnp.repeat(filters.astype(F32).T, breadth, axis=1)]
    pallas_call x2, Pallas kernels: 22.4 us -> 19.5 us  [per_device(): pl.pallas_call(functools.partial(step_kernel, patch=patch, per_tile=per_t...]
  transfers between devices with their start and end apart: 10 -> 7, of which waited for: 3 -> 2; matrix products, arithmetic and copies ran while one was open for 18% -> 1% of each run, Pallas kernels for 0% -> 8%
where the time goes in v2:
time: 106 us; the launch traced here: 105 us
  Pallas kernels  34 us (32%)
  blocking collectives  32.4 us (31%)
  starting transfers between devices  17.6 us (17%)
  local copies, waits for them, and re-layouts  11.4 us (11%)
  waiting for transfers between devices  8.52 us (8%)
    all_to_all x3, blocking collectives, exchange(): return lax.all_to_all(block, 'exp', split_axis=0, concat_axis=0, tiled=True)  32.4 us
    pallas_call x2, Pallas kernels, per_device(): pl.pallas_call(functools.partial(step_kernel, patch=patch, per_tile=per_t...  19.5 us
    unnamed x38, local copies, waits for them, and re-layouts  10.7 us
    ppermute x2, starting transfers between devices, per_device(): far = lax.ppermute(far, 'sub', routes[1])  6.81 us
    all_to_all x1, waiting for transfers between devices, exchange(): return lax.all_to_all(block, 'exp', split_axis=0, concat_axis=0, tiled=True)  6.17 us
    pallas_call x1, Pallas kernels, per_device(): pl.pallas_call(functools.partial(prep_kernel, ext=ext, rim=rim, per_tile=...  5.82 us
    all_to_all x1, starting transfers between devices, exchange(): return lax.all_to_all(block, 'exp', split_axis=0, concat_axis=0, tiled=True)  5.53 us
    ppermute x1, starting transfers between devices, per_device(): rims_far = lax.ppermute(rims_far, 'sub', routes[1])  4.63 us
  transfers between devices with their start and end apart: 7, of which 2 were waited for; matrix products, arithmetic and copies ran while one was open for 1% of the time, Pallas kernels for 8%

profile of v2, /device:TPU:1, one launch (start us, length us, event | category | flops | bytes accessed | tf_op | source)
XLA Modules:
  0.0 104.8 jit_solution(6291821165544611839)
XLA Ops:
  0.6 0.0 copy-start
  0.7 1.9 %copy-done = bf16[2,12,128,512]{3,2,1,0:T(8,128)(2,1)S(1)} copy-done((bf16[2,12,128,512]{3,2,1,0:T(8,128)(2,1)S(1)}, bf16[2,12,128,512]{3,2,1,0:T(8,128)(2,1)}, u32[]{:S(2)}) %copy-start) | copy-done | bytes 3145752
  2.5 1.0 copy-done.6
  3.6 0.0 copy-start.14
  3.6 0.0 copy-start.1
  3.6 1.2 %rims.1 = (bf16[2,15,16,512]{3,2,1,0:T(8,128)(2,1)}, bf16[2,15,16,512]{3,2,1,0:T(8,128)(2,1)}) custom-call(s32[1]{0:T(128)} %bitcast.1.even_ref, bf16[2,12,128,512]{3,2,1,0:T(8,128)(2,1)S(1)} %copy-done, f32[2,128,512]{2,1,0:T(8,128)S(1)} %copy-done.6), custom_call_target="tpu_custom_call" | custom-call | tf_op jit(solution)/shard_map/rims/pallas_call | solution.py:309
  4.8 0.1 collective-permute-start.2
  4.9 4.6 %collective-permute-start.3 = (bf16[2,15,16,512]{3,2,1,0:T(8,128)(2,1)}, bf16[2,15,16,512]{3,2,1,0:T(8,128)(2,1)}, u32[]{:S(2)}, u32[]{:S(2)}) collective-permute-start(bf16[2,15,16,512]{3,2,1,0:T(8,128)(2,1)} %get-tuple-element.26), channel_id=1, source_target_pairs={{1,2},{2,1},{5,6},{6,5},{9,10},{10,9},{13,14},{14,13},{17,18},{18,... | collective-permute-start | bytes 1474568 | tf_op jit(solution)/shard_map/ppermute | solution.py:318
  9.6 0.0 copy-done.15
  9.6 0.7 broadcast_in_dim.2
  10.2 5.5 %all-to-all-start = ((bf16[8,64,128]{2,1,0:T(8,128)(2,1)}), bf16[8,64,128]{2,1,0:T(8,128)(2,1)S(1)}, u32[]{:S(2)}, u32[]{:S(2)}) async-start(bf16[8,64,128]{2,1,0:T(8,128)(2,1)} %broadcast_in_dim.2), calls=%async_computation | async-start | bytes 262144 | tf_op jit(solution)/shard_map/all_to_all | solution.py:301
  15.8 0.0 copy-done.16
  15.8 0.1 copy.14.offset_ref
  15.9 0.0 copy-done.17
  15.9 0.1 copy.13.owners_ref
  16.0 6.2 %all-to-all-done = bf16[8,64,128]{2,1,0:T(8,128)(2,1)S(1)} async-done(((bf16[8,64,128]{2,1,0:T(8,128)(2,1)}), bf16[8,64,128]{2,1,0:T(8,128)(2,1)S(1)}, u32[]{:S(2)}, u32[]{:S(2)}) %all-to-all-start) | async-done | bytes 131104 | tf_op jit(solution)/shard_map/all_to_all | solution.py:301
  22.2 2.1 %picture.2 = (bf16[2,128,512]{2,1,0:T(8,128)(2,1)S(1)}, bf16[2,32,512]{2,1,0:T(8,128)(2,1)S(1)}, bf16[2,32,512]{2,1,0:T(8,128)(2,1)S(1)}) custom-call(s32[1]{0:T(128)} %bitcast.1.even_ref, s32[2,16,4,1]{3,2,1,0:T(4,128)S(1)} %copy.13.owners_ref, s32[2,16,4]{2,1,0:T(8,128)S(1)} %copy.14.offset_ref, bf16[512,128]{1,0:T(8,128)(2,1)S(1)} %bitcast.11), custom_call_target="tpu_custom_call" | custom-call | tf_op jit(solution)/shard_map/picture/pallas_call | solution.py:342
  24.3 0.1 collective-permute-start
  24.4 3.6 %collective-permute-start.1 = (bf16[2,32,512]{2,1,0:T(8,128)(2,1)S(1)}, bf16[2,32,512]{2,1,0:T(8,128)(2,1)S(1)}, u32[]{:S(2)}, u32[]{:S(2)}) collective-permute-start(bf16[2,32,512]{2,1,0:T(8,128)(2,1)S(1)} %get-tuple-element.23), channel_id=1, source_target_pairs={{1,2},{2,1},{5,6},{6,5},{9,10},{10,9},{13,14},{14,13},{17,18},{18,... | collective-permute-start | bytes 196616 | tf_op jit(solution)/shard_map/ppermute | solution.py:355
  28.0 0.0 copy-done.13
  28.0 0.0 copy-done.14
  28.0 5.8 %prep.1 = (bf16[1920,192]{1,0:T(8,128)(2,1)S(1)}, bf16[128,1920]{1,0:T(8,128)(2,1)S(1)}, bf16[12,256,256]{2,1,0:T(8,128)(2,1)S(1)}, bf16[12,256,256]{2,1,0:T(8,128)(2,1)S(1)}, f32[64,128]{1,0:T(8,128)S(1)}) custom-call(s32[2,16,4,1]{3,2,1,0:T(4,128)S(1)} %copy.13.owners_ref, s32[2,16,4]{2,1,0:T(8,128)S(1)} %copy.14.offset_ref, ...), custom_call_target="tpu_custom_call" | custom-call | tf_op jit(solution)/shard_map/prep/pallas_call | solution.py:320
  33.8 0.0 copy-start.2
  33.8 0.0 copy-start.4
  33.8 0.0 copy-start.9
  33.8 0.0 collective-permute-done.near_ref
  33.9 0.0 collective-permute-done.1.far_ref
  33.9 0.0 collective-permute-done.2.rims_near_any
  33.9 0.0 collective-permute-done.3.rims_far_any
  33.9 0.0 copy-start.7
  33.9 1.4 %copy-done.7 = f32[2,128,512]{2,1,0:T(8,128)S(1)} copy-done((f32[2,128,512]{2,1,0:T(8,128)S(1)}, f32[2,128,512]{2,1,0:T(8,128)}, u32[]{:S(2)}) %copy-start.7) | copy-done | bytes 524312
  35.3 9.6 %step.2 = (f32[2,128,512]{2,1,0:T(8,128)}, f32[576,128]{1,0:T(8,128)S(1)}) custom-call(s32[1]{0:T(128)} %bitcast.1.even_ref, s32[2,16,4,1]{3,2,1,0:T(4,128)S(1)} %copy.13.owners_ref, s32[2,16,4]{2,1,0:T(8,128)S(1)} %copy.14.offset_ref, bf16[2,128,512]{2,1,0:T(8,128)(2,1)S(1)} %get-tuple-element.21.picture_ref, ...), custom_call_target="tpu_custom_call" | custom-call | tf_op jit(solution)/shard_map/step/pallas_call | solution.py:358
  45.0 11.7 %all_to_all.41 = f32[8,72,128]{2,1,0:T(8,128)} all-to-all(f32[8,72,128]{2,1,0:T(8,128)S(1)} %bitcast.13), channel_id=1, replica_groups=mesh['exp'=8,'sub'=4] {'exp'}, dimensions={0} | all-to-all | bytes 589824 | tf_op jit(solution)/shard_map/all_to_all | solution.py:301
  56.7 1.7 %update.2 = (f32[64,128]{1,0:T(8,128)}, bf16[512,128]{1,0:T(8,128)(2,1)}, f32[64,128]{1,0:T(8,128)}) custom-call(f32[64,128]{1,0:T(8,128)} %bitcast.17, f32[576,128]{1,0:T(8,128)} %bitcast.15), custom_call_target="tpu_custom_call" | custom-call | tf_op jit(solution)/shard_map/update/pallas_call | solution.py:394
  58.4 10.5 %all_to_all.42 = bf16[8,64,128]{2,1,0:T(8,128)(2,1)S(1)} all-to-all(bf16[8,64,128]{2,1,0:T(8,128)(2,1)} %bitcast.18), channel_id=1, replica_groups=mesh['exp'=8,'sub'=4] {'exp'}, dimensions={0} | all-to-all | bytes 262144 | tf_op jit(solution)/shard_map/all_to_all | solution.py:301
  68.9 2.1 %picture.3 = (bf16[2,128,512]{2,1,0:T(8,128)(2,1)S(1)}, bf16[2,32,512]{2,1,0:T(8,128)(2,1)S(1)}, bf16[2,32,512]{2,1,0:T(8,128)(2,1)S(1)}) custom-call(s32[1]{0:T(128)} %bitcast.1.even_ref, s32[2,16,4,1]{3,2,1,0:T(4,128)S(1)} %copy.13.owners_ref, s32[2,16,4]{2,1,0:T(8,128)S(1)} %copy.14.offset_ref, bf16[512,128]{1,0:T(8,128)(2,1)S(1)} %bitcast.12), custom_call_target="tpu_custom_call" | custom-call | tf_op jit(solution)/shard_map/picture/pallas_call | solution.py:342
  71.0 0.5 collective-permute-start.4
  71.5 3.2 %collective-permute-start.5 = (bf16[2,32,512]{2,1,0:T(8,128)(2,1)S(1)}, bf16[2,32,512]{2,1,0:T(8,128)(2,1)S(1)}, u32[]{:S(2)}, u32[]{:S(2)}) collective-permute-start(bf16[2,32,512]{2,1,0:T(8,128)(2,1)S(1)} %get-tuple-element.36), channel_id=1, source_target_pairs={{1,2},{2,1},{5,6},{6,5},{9,10},{10,9},{13,14},{14,13},{17,18},{18,... | collective-permute-start | bytes 196616 | tf_op jit(solution)/shard_map/ppermute | solution.py:355
  74.7 0.0 collective-permute-done.4.near_ref
  74.7 2.3 %collective-permute-done.5.far_ref = bf16[2,32,512]{2,1,0:T(8,128)(2,1)S(1)} collective-permute-done((bf16[2,32,512]{2,1,0:T(8,128)(2,1)S(1)}, bf16[2,32,512]{2,1,0:T(8,128)(2,1)S(1)}, u32[]{:S(2)}, u32[]{:S(2)}) %collective-permute-start.5) | collective-permute-done | bytes 65568 | tf_op jit(solution)/shard_map/ppermute | solution.py:355
  77.1 1.4 %copy-done.3 = bf16[12,256,256]{2,1,0:T(8,128)(2,1)S(1)} copy-done((bf16[12,256,256]{2,1,0:T(8,128)(2,1)S(1)}, bf16[12,256,256]{2,1,0:T(8,128)(2,1)}, u32[]{:S(2)}) %copy-start.3) | copy-done | bytes 1572888
  78.5 1.4 %copy-done.5 = bf16[12,256,256]{2,1,0:T(8,128)(2,1)S(1)} copy-done((bf16[12,256,256]{2,1,0:T(8,128)(2,1)S(1)}, bf16[12,256,256]{2,1,0:T(8,128)(2,1)}, u32[]{:S(2)}) %copy-start.5) | copy-done | bytes 1572888
  79.9 1.0 copy-done.8
  80.9 1.2 %copy-done.10 = bf16[1920,192]{1,0:T(8,128)(2,1)S(1)} copy-done((bf16[1920,192]{1,0:T(8,128)(2,1)S(1)}, bf16[1920,192]{1,0:T(8,128)(2,1)}, u32[]{:S(2)}) %copy-start.10) | copy-done | bytes 737304
  82.1 1.0 copy-done.12
  83.2 9.9 %step.3 = (f32[2,128,512]{2,1,0:T(8,128)}, f32[512,128]{1,0:T(8,128)S(1)}) custom-call(s32[1]{0:T(128)} %bitcast.1.even_ref, s32[2,16,4,1]{3,2,1,0:T(4,128)S(1)} %copy.13.owners_ref, s32[2,16,4]{2,1,0:T(8,128)S(1)} %copy.14.offset_ref, bf16[2,128,512]{2,1,0:T(8,128)(2,1)S(1)} %get-tuple-element.34.picture_ref, ...), custom_call_target="tpu_custom_call" | custom-call | tf_op jit(solution)/shard_map/step/pallas_call | solution.py:358
  93.1 10.2 %all_to_all.43 = f32[8,64,128]{2,1,0:T(8,128)} all-to-all(f32[8,64,128]{2,1,0:T(8,128)S(1)} %bitcast.14), channel_id=1, replica_groups=mesh['exp'=8,'sub'=4] {'exp'}, dimensions={0} | all-to-all | bytes 524288 | tf_op jit(solution)/shard_map/all_to_all | solution.py:301
  103.2 1.6 %update.3 = f32[64,128]{1,0:T(8,128)} custom-call(f32[64,128]{1,0:T(8,128)} %get-tuple-element.32.sky_ref, f32[512,128]{1,0:T(8,128)} %bitcast.16, f32[64,128]{1,0:T(8,128)} %get-tuple-element.38.refs_0_), custom_call_target="tpu_custom_call" | custom-call | tf_op jit(solution)/shard_map/update/pallas_call | solution.py:394
  (17 shorter events, 0.0 us)
Async XLA Ops:
  0.6 1.9 %copy-start = (bf16[2,12,128,512]{3,2,1,0:T(8,128)(2,1)S(1)}, bf16[2,12,128,512]{3,2,1,0:T(8,128)(2,1)}, u32[]{:S(2)}) copy-start(bf16[2,12,128,512]{3,2,1,0:T(8,128)(2,1)} %coeffs_any.3) | copy-start | bytes 9437188
  2.5 1.0 copy-start.6
  3.6 6.0 %copy-start.15 = (f32[1,8,8,128]{3,2,1,0:T(8,128)S(1)}, f32[1,8,8,128]{3,2,1,0:T(8,128)}, u32[]{:S(2)}) copy-start(f32[1,8,8,128]{3,2,1,0:T(8,128)} %param.7) | copy-start | bytes 98308
  3.6 12.2 %copy-start.16 = (s32[2,16,4]{1,2,0:T(4,128)S(1)}, s32[2,16,4]{1,2,0:T(4,128)}, u32[]{:S(2)}) copy-start(s32[2,16,4]{1,2,0:T(4,128)} %param.13) | copy-start | bytes 1540
  3.6 12.3 %copy-start.17 = (s32[2,16,4,1]{1,3,2,0:T(1,128)S(1)}, s32[2,16,4,1]{1,3,2,0:T(1,128)}, u32[]{:S(2)}) copy-start(s32[2,16,4,1]{1,3,2,0:T(1,128)} %param.12) | copy-start | bytes 1540
  3.6 24.4 %copy-start.13 = (bf16[12,21]{1,0:T(8,128)(2,1)S(1)}, bf16[12,21]{1,0:T(8,128)(2,1)}, u32[]{:S(2)}) copy-start(bf16[12,21]{1,0:T(8,128)(2,1)} %vert_ref.1) | copy-start | bytes 1516
  3.6 24.4 %copy-start.14 = (bf16[12,21]{1,0:T(8,128)(2,1)S(1)}, bf16[12,21]{1,0:T(8,128)(2,1)}, u32[]{:S(2)}) copy-start(bf16[12,21]{1,0:T(8,128)(2,1)} %horiz_ref.1) | copy-start | bytes 1516
  3.6 30.3 %copy-start.1 = (bf16[2,12,128,512]{3,2,1,0:T(8,128)(2,1)S(1)}, bf16[2,12,128,512]{3,2,1,0:T(8,128)(2,1)}, u32[]{:S(2)}) copy-start(bf16[2,12,128,512]{3,2,1,0:T(8,128)(2,1)} %coeffs_any.3) | copy-start | bytes 9437188
  4.8 29.1 %collective-permute-start.2 = (bf16[2,15,16,512]{3,2,1,0:T(8,128)(2,1)}, bf16[2,15,16,512]{3,2,1,0:T(8,128)(2,1)}, u32[]{:S(2)}, u32[]{:S(2)}) collective-permute-start(bf16[2,15,16,512]{3,2,1,0:T(8,128)(2,1)} %get-tuple-element.25), channel_id=1, source_target_pairs={{0,1},{2,3},{1,0},{3,2},{4,5},{6,7},{5,4},{7,6},{8,9},{10,11},{9,8... | collective-permute-start | bytes 1474568 | tf_op jit(solution)/shard_map/ppermute | solution.py:319
  4.9 29.0 %collective-permute-start.3 = (bf16[2,15,16,512]{3,2,1,0:T(8,128)(2,1)}, bf16[2,15,16,512]{3,2,1,0:T(8,128)(2,1)}, u32[]{:S(2)}, u32[]{:S(2)}) collective-permute-start(bf16[2,15,16,512]{3,2,1,0:T(8,128)(2,1)} %get-tuple-element.26), channel_id=1, source_target_pairs={{1,2},{2,1},{5,6},{6,5},{9,10},{10,9},{13,14},{14,13},{17,18},{18,... | collective-permute-start | bytes 1474568 | tf_op jit(solution)/shard_map/ppermute | solution.py:318
  10.2 11.9 %all-to-all-start = ((bf16[8,64,128]{2,1,0:T(8,128)(2,1)}), bf16[8,64,128]{2,1,0:T(8,128)(2,1)S(1)}, u32[]{:S(2)}, u32[]{:S(2)}) async-start(bf16[8,64,128]{2,1,0:T(8,128)(2,1)} %broadcast_in_dim.2), calls=%async_computation | async-start | bytes 262144 | tf_op jit(solution)/shard_map/all_to_all | solution.py:301
  24.3 9.6 %collective-permute-start = (bf16[2,32,512]{2,1,0:T(8,128)(2,1)S(1)}, bf16[2,32,512]{2,1,0:T(8,128)(2,1)S(1)}, u32[]{:S(2)}, u32[]{:S(2)}) collective-permute-start(bf16[2,32,512]{2,1,0:T(8,128)(2,1)S(1)} %get-tuple-element.22), channel_id=1, source_target_pairs={{0,1},{2,3},{1,0},{3,2},{4,5},{6,7},{5,4},{7,6},{8,9},{10,11},{9,8... | collective-permute-start | bytes 196616 | tf_op jit(solution)/shard_map/ppermute | solution.py:356
  24.4 9.5 %collective-permute-start.1 = (bf16[2,32,512]{2,1,0:T(8,128)(2,1)S(1)}, bf16[2,32,512]{2,1,0:T(8,128)(2,1)S(1)}, u32[]{:S(2)}, u32[]{:S(2)}) collective-permute-start(bf16[2,32,512]{2,1,0:T(8,128)(2,1)S(1)} %get-tuple-element.23), channel_id=1, source_target_pairs={{1,2},{2,1},{5,6},{6,5},{9,10},{10,9},{13,14},{14,13},{17,18},{18,... | collective-permute-start | bytes 196616 | tf_op jit(solution)/shard_map/ppermute | solution.py:355
  33.8 11.2 %copy-start.2 = (bf16[12,256,256]{2,1,0:T(8,128)(2,1)}, bf16[12,256,256]{2,1,0:T(8,128)(2,1)S(1)}, u32[]{:S(2)}) copy-start(bf16[12,256,256]{2,1,0:T(8,128)(2,1)S(1)} %get-tuple-element.29.forward_any) | copy-start | bytes 4718596
  33.8 11.2 %copy-start.4 = (bf16[12,256,256]{2,1,0:T(8,128)(2,1)}, bf16[12,256,256]{2,1,0:T(8,128)(2,1)S(1)}, u32[]{:S(2)}) copy-start(bf16[12,256,256]{2,1,0:T(8,128)(2,1)S(1)} %get-tuple-element.30.backward_any) | copy-start | bytes 4718596
  33.8 11.2 %copy-start.9 = (bf16[1920,192]{1,0:T(8,128)(2,1)}, bf16[1920,192]{1,0:T(8,128)(2,1)S(1)}, u32[]{:S(2)}) copy-start(bf16[1920,192]{1,0:T(8,128)(2,1)S(1)} %get-tuple-element.27.vertical_any) | copy-start | bytes 2211844
  33.8 11.2 %copy-start.11 = (bf16[128,1920]{1,0:T(8,128)(2,1)}, bf16[128,1920]{1,0:T(8,128)(2,1)S(1)}, u32[]{:S(2)}) copy-start(bf16[128,1920]{1,0:T(8,128)(2,1)S(1)} %get-tuple-element.28.side_any) | copy-start | bytes 1474564
  33.9 1.4 %copy-start.7 = (f32[2,128,512]{2,1,0:T(8,128)S(1)}, f32[2,128,512]{2,1,0:T(8,128)}, u32[]{:S(2)}) copy-start(f32[2,128,512]{2,1,0:T(8,128)} %observed_any.3) | copy-start | bytes 1572868
  71.0 3.7 %collective-permute-start.4 = (bf16[2,32,512]{2,1,0:T(8,128)(2,1)S(1)}, bf16[2,32,512]{2,1,0:T(8,128)(2,1)S(1)}, u32[]{:S(2)}, u32[]{:S(2)}) collective-permute-start(bf16[2,32,512]{2,1,0:T(8,128)(2,1)S(1)} %get-tuple-element.35), channel_id=1, source_target_pairs={{0,1},{2,3},{1,0},{3,2},{4,5},{6,7},{5,4},{7,6},{8,9},{10,11},{9,8... | collective-permute-start | bytes 196616 | tf_op jit(solution)/shard_map/ppermute | solution.py:356
  71.5 5.6 %collective-permute-start.5 = (bf16[2,32,512]{2,1,0:T(8,128)(2,1)S(1)}, bf16[2,32,512]{2,1,0:T(8,128)(2,1)S(1)}, u32[]{:S(2)}, u32[]{:S(2)}) collective-permute-start(bf16[2,32,512]{2,1,0:T(8,128)(2,1)S(1)} %get-tuple-element.36), channel_id=1, source_target_pairs={{1,2},{2,1},{5,6},{6,5},{9,10},{10,9},{13,14},{14,13},{17,18},{18,... | collective-permute-start | bytes 196616 | tf_op jit(solution)/shard_map/ppermute | solution.py:355
  77.1 1.4 %copy-start.3 = (bf16[12,256,256]{2,1,0:T(8,128)(2,1)S(1)}, bf16[12,256,256]{2,1,0:T(8,128)(2,1)}, u32[]{:S(2)}) copy-start(bf16[12,256,256]{2,1,0:T(8,128)(2,1)} %copy-done.2) | copy-start | bytes 4718596
  78.5 1.4 %copy-start.5 = (bf16[12,256,256]{2,1,0:T(8,128)(2,1)S(1)}, bf16[12,256,256]{2,1,0:T(8,128)(2,1)}, u32[]{:S(2)}) copy-start(bf16[12,256,256]{2,1,0:T(8,128)(2,1)} %copy-done.4) | copy-start | bytes 4718596
  79.9 1.0 copy-start.8
  80.9 1.2 %copy-start.10 = (bf16[1920,192]{1,0:T(8,128)(2,1)S(1)}, bf16[1920,192]{1,0:T(8,128)(2,1)}, u32[]{:S(2)}) copy-start(bf16[1920,192]{1,0:T(8,128)(2,1)} %copy-done.9) | copy-start | bytes 2211844
  82.1 1.0 copy-start.12

commit v3 on v2

--- a/solution.py
+++ b/solution.py
@@ -63,54 +63,26 @@
     copies[3].wait()
 
 
-def prep_kernel(
-    owners_ref, offset_ref, vert_ref, horiz_ref, vertical_ref, side_ref, forward_ref, backward_ref, counted_ref,
-    taps_ref, turned_ref, *, ext, rim, per_tile,
-):
+def prep_kernel(owners_ref, offset_ref, vert_ref, horiz_ref, ids_ref, counted_ref, taps_ref, *, per_tile):
     modes, taps = vert_ref.shape
-    margin = (taps - 1) // 2
-    width = forward_ref.shape[1]
-    height = side_ref.shape[0]
-    tall = vertical_ref.shape[0] // modes
-    reach = vertical_ref.shape[1]
-
     taps_ref[...] = jnp.zeros(taps_ref.shape, F32)
     taps_ref[0, :modes, :taps] = vert_ref[...].astype(F32)
     taps_ref[1, :modes, :taps] = horiz_ref[...].astype(F32)
     turn = lax.broadcasted_iota(jnp.int32, (LANES, LANES), 0) + lax.broadcasted_iota(jnp.int32, (LANES, LANES), 1)
-    flipped = jnp.dot(
-        taps_ref[1].astype(BF16), (turn == taps - 1).astype(F32).astype(BF16), preferred_element_type=F32
+    taps_ref[2] = jnp.dot(
+        taps_ref[0].astype(BF16), (turn == taps - 1).astype(F32).astype(BF16), preferred_element_type=F32
     )
-    taps_ref[2] = flipped
-
-    def banded(row, shift, rows, cols):
-        turned = pltpu.roll(jnp.broadcast_to(row, (8, LANES)), (-shift) % LANES, 1)
-        ring = pltpu.roll(jnp.broadcast_to(turned[:1], (LANES, LANES)), 0, 1, stride=1, stride_axis=0)
-        lag = (
-            lax.broadcasted_iota(jnp.int32, (rows, cols), 1) - lax.broadcasted_iota(jnp.int32, (rows, cols), 0) + shift
-        )
-        across = jnp.concatenate([ring] * (-(-cols // LANES)), axis=1)[:, :cols]
-        whole = jnp.concatenate([across] * (-(-rows // LANES)), axis=0)[:rows]
-        return jnp.where((lag >= 0) & (lag < taps), whole, 0.0)
-
-    for mode in range(modes):
-        row = taps_ref[0, mode : mode + 1]
-        place = slice(mode * tall, (mode + 1) * tall)
-        vertical_ref[place, :] = banded(row, margin + ext - rim, tall, reach).astype(BF16)
-        turned_ref[place, :] = banded(row, margin + ext, tall, height)
-        backward_ref[mode] = banded(taps_ref[1, mode : mode + 1], margin, width, width).astype(BF16)
-        forward_ref[mode] = banded(taps_ref[2, mode : mode + 1], margin, width, width).astype(BF16)
-    side_ref[...] = turned_ref[...].T.astype(BF16)
-
     counted_ref[...] = jnp.zeros(counted_ref.shape, F32)
-    for piece in range(offset_ref.shape[0]):
-        for row in range(offset_ref.shape[1]):
-            for col in range(offset_ref.shape[2]):
+    pieces, rows, cols = offset_ref.shape
+    for piece in range(pieces):
+        for row in range(rows):
+            for col in range(cols):
                 index = owners_ref[piece, row, col, 0] * per_tile + offset_ref[piece, row, col]
+                ids_ref[(piece * rows + row) * cols + col] = index
                 counted_ref[pl.ds(index, 1), :] += 1.0
 
 
-def picture_kernel(even_ref, owners_ref, offset_ref, tiles_ref, picture_ref, near_ref, far_ref, wide_ref, *, patch, per_tile):
+def picture_kernel(even_ref, ids_ref, tiles_ref, picture_ref, near_ref, far_ref, wide_ref, *, patch):
     pieces, height, breadth = picture_ref.shape
     rim = near_ref.shape[1]
     patch_rows, patch_cols = patch
@@ -123,7 +95,7 @@
             for col in range(cols):
                 parts = []
                 for inner in range(row, row + together):
-                    index = owners_ref[piece, inner, col, 0] * per_tile + offset_ref[piece, inner, col]
+                    index = ids_ref[(piece * rows + inner) * cols + col]
                     start = pl.multiple_of(index * patch_rows, patch_rows)
                     parts.append(wide_ref[pl.ds(start, patch_rows), :])
                 picture_ref[
@@ -150,35 +122,56 @@
     return blocks
 
 
+def lags(rows, cols, shift):
+    return (
+        lax.broadcasted_iota(jnp.int32, (rows, cols), 1) - lax.broadcasted_iota(jnp.int32, (rows, cols), 0) + shift
+    )
+
+
+def within(lag, taps):
+    return ((lag >= 0) & (lag < taps)).astype(F32)
+
+
+def ring_of(row, shift):
+    turned = pltpu.roll(jnp.broadcast_to(row, (8, LANES)), (-shift) % LANES, 1)
+    return pltpu.roll(jnp.broadcast_to(turned[:1], (LANES, LANES)), 0, 1, stride=1, stride_axis=0)
+
+
+def tiled(ring, rows, cols):
+    across = jnp.concatenate([ring] * (-(-cols // LANES)), axis=1)[:, :cols]
+    return jnp.concatenate([across] * (-(-rows // LANES)), axis=0)[:rows]
+
+
 def step_kernel(
-    even_ref, owners_ref, offset_ref, picture_ref, near_ref, far_ref, counted_ref, coeffs_any, rims_near_any,
-    rims_far_any, observed_any, vertical_any, side_any, forward_any, backward_any,
-    clipped_ref, sums_ref, image_ref, field_ref, model_ref, gradient_ref, coeffs_ref, seen_ref, seen_rims_ref,
-    vertical_ref, side_ref, forward_ref, backward_ref, sems, *, patch, per_tile, slot,
+    even_ref, ids_ref, picture_ref, near_ref, far_ref, counted_ref, taps_ref, coeffs_any, rims_near_any,
+    rims_far_any, observed_any, *refs, patch, per_tile, slot, taps, with_clipped,
 ):
+    refs = list(refs)
+    clipped_ref = refs.pop(0) if with_clipped else None
+    (
+        sums_ref, image_ref, field_ref, model_ref, gradient_ref, coeffs_ref, seen_ref, seen_rims_ref,
+        vertical_ref, side_ref, across_ref, band_ref, sems,
+    ) = refs
     pieces, height, breadth = picture_ref.shape
     modes = coeffs_ref.shape[1]
     rim = near_ref.shape[1]
     tall = coeffs_ref.shape[2]
     ext = (tall - height) // 2
+    margin = (taps - 1) // 2
     patch_rows, patch_cols = patch
-    width = forward_ref.shape[1]
+    width = across_ref.shape[1]
     stride = patch_cols
     even = even_ref[0]
     near_at = pl.multiple_of(even * (ext + height), ROWS)
     far_at = pl.multiple_of((1 - even) * (ext + height), ROWS)
 
     moves = [
-        (vertical_any, vertical_ref),
-        (forward_any, forward_ref),
         (coeffs_any, coeffs_ref.at[:, :, pl.ds(ext, height), :]),
         (rims_near_any.at[:, pl.ds(0, modes)], coeffs_ref.at[:, :, pl.ds(near_at, ext), :]),
         (rims_far_any.at[:, pl.ds(0, modes)], coeffs_ref.at[:, :, pl.ds(far_at, ext), :]),
         (observed_any, seen_ref.at[:, pl.ds(ext, height), :]),
         (rims_near_any.at[:, pl.ds(modes, PARTS)], seen_rims_ref.at[0]),
         (rims_far_any.at[:, pl.ds(modes, PARTS)], seen_rims_ref.at[1]),
-        (backward_any, backward_ref),
-        (side_any, side_ref),
     ]
     copies = [pltpu.make_async_copy(source, target, sems.at[k]) for k, (source, target) in enumerate(moves)]
     for copy in copies:
@@ -188,9 +181,16 @@
     image_ref[:, pl.ds(pl.multiple_of(even * (rim + height), ROWS), rim), :] = near_ref[...]
     image_ref[:, pl.ds(pl.multiple_of((1 - even) * (rim + height), ROWS), rim), :] = far_ref[...]
 
+    reach = vertical_ref.shape[1]
+    band_ref[...] = within(lags(width, width, margin), taps)
+    skew = margin + ext - rim
+    inside = within(lags(tall, reach, skew), taps)
+    for mode in range(modes):
+        ring = ring_of(taps_ref[0, mode : mode + 1], skew)
+        vertical_ref[mode * tall : (mode + 1) * tall, :] = (tiled(ring, tall, reach) * inside).astype(BF16)
+
     group = divisor(modes, 4)
     chunk = group * tall
-    copies[0].wait()
     for start in range(0, modes * tall, chunk):
         table = vertical_ref[start : start + chunk, :]
         for piece in range(pieces):
@@ -199,19 +199,22 @@
                     table, image_ref[piece, :, low : low + width], preferred_element_type=F32
                 ).astype(BF16)
 
-    def blur(table, blocks):
+    def blur(blocks, table, side):
         cuts = [cut for block in blocks for cut in windows_of(block, width, stride)]
-        result = jnp.dot(jnp.concatenate(cuts, axis=0), table, preferred_element_type=F32)
+        result = lax.dot_general(
+            jnp.concatenate(cuts, axis=0), table, (((1,), (side,)), ((), ())), preferred_element_type=F32
+        )
         per = len(cuts) // len(blocks)
         outs = [result[k * tall : (k + 1) * tall] for k in range(len(cuts))]
         return [joined(outs[k * per : (k + 1) * per], width, stride) for k in range(len(blocks))]
 
-    for k in range(1, 5):
+    for k in range(3):
         copies[k].wait()
     for mode in range(modes):
         start = mode * tall
+        across_ref[mode] = (tiled(ring_of(taps_ref[1, mode : mode + 1], margin), width, width) * band_ref[...]).astype(BF16)
         blocks = [field_ref[piece, start : start + tall, :] for piece in range(pieces)]
-        for piece, columns in enumerate(blur(forward_ref[mode], blocks)):
+        for piece, columns in enumerate(blur(blocks, across_ref[mode], 1)):
             weight = coeffs_ref[piece, mode].astype(F32)
             for k, column in enumerate(columns):
                 place = slice(k * stride, (k + 1) * stride)
@@ -219,7 +222,7 @@
                     model_ref[piece, :, place] = weight[:, place] * column
                 else:
                     model_ref[piece, :, place] += weight[:, place] * column
-    for k in range(5, 8):
+    for k in range(3, 6):
         copies[k].wait()
     for side, start in enumerate((near_at, far_at)):
         total = seen_rims_ref[side, :, 0].astype(F32)
@@ -227,33 +230,45 @@
             total = total + seen_rims_ref[side, :, part].astype(F32)
         seen_ref[:, pl.ds(start, ext), :] = total
     model_ref[...] = jnp.clip(model_ref[...] - seen_ref[...], -DELTA, DELTA)
-    clipped_ref[...] = model_ref[:, ext : ext + height, :]
-
-    copies[8].wait()
+    if with_clipped:
+        clipped_ref[...] = model_ref[:, ext : ext + height, :]
+
+    total = modes * tall
+    for low in range(0, total, LANES):
+        high = min(low + LANES, total)
+        parts = None
+        for mode in range(low // tall, (high - 1) // tall + 1):
+            back = taps - 1 - (ext + margin) - mode * tall
+            lag = lags(height, LANES, low + back)
+            ring = tiled(ring_of(taps_ref[2, mode : mode + 1], low + back), height, LANES) * within(lag, taps)
+            parts = ring if parts is None else parts + ring
+        side_ref[:, low:high] = parts[:, : high - low].astype(BF16)
+
     for mode in range(modes):
         start = mode * tall
         blocks = [(coeffs_ref[piece, mode].astype(F32) * model_ref[piece]).astype(BF16) for piece in range(pieces)]
-        for piece, columns in enumerate(blur(backward_ref[mode], blocks)):
+        for piece, columns in enumerate(blur(blocks, across_ref[mode], 0)):
             for k, column in enumerate(columns):
                 field_ref[piece, start : start + tall, k * stride : (k + 1) * stride] = column.astype(BF16)
-    copies[9].wait()
     for piece in range(pieces):
         for low in range(0, breadth, width):
             gradient_ref[piece, :, low : low + width] = jnp.dot(
                 side_ref[...], field_ref[piece, :, low : low + width], preferred_element_type=F32
             )
     sums_ref[...] = jnp.zeros(sums_ref.shape, F32)
-    if slot > per_tile * patch_rows:
+    held = per_tile * patch_rows
+    if slot > held:
         for owner in range(sums_ref.shape[0] // slot):
-            start = owner * slot + per_tile * patch_rows
+            start = owner * slot + held
             sums_ref[start : start + per_tile, :] = counted_ref[owner * per_tile : (owner + 1) * per_tile, :]
     cols = breadth // patch_cols
     rows = height // patch_rows
     for row in range(rows):
         for col in range(cols):
             for piece in range(pieces):
-                index = owners_ref[piece, row, col, 0] * slot + offset_ref[piece, row, col] * patch_rows
-                place = pl.ds(pl.multiple_of(index, patch_rows), patch_rows)
+                index = ids_ref[(piece * rows + row) * cols + col]
+                start = index * patch_rows + (index // per_tile) * (slot - held)
+                place = pl.ds(pl.multiple_of(start, patch_rows), patch_rows)
                 sums_ref[place, :] += gradient_ref[
                     piece, row * patch_rows : (row + 1) * patch_rows, col * patch_cols : (col + 1) * patch_cols
                 ]
@@ -317,22 +332,16 @@
     )(even, coeffs, observed)
     rims_far = lax.ppermute(rims_far, "sub", routes[1])
     rims_near = lax.ppermute(rims_near, "sub", routes[0])
-    vertical, side, forward, backward, counted = pl.pallas_call(
-        functools.partial(prep_kernel, ext=ext, rim=rim, per_tile=per_tile),
+    ids, counted, taps = pl.pallas_call(
+        functools.partial(prep_kernel, per_tile=per_tile),
         out_shape=(
-            jax.ShapeDtypeStruct((modes * tall, height + 2 * rim), BF16),
-            jax.ShapeDtypeStruct((height, modes * tall), BF16),
-            jax.ShapeDtypeStruct((modes, width, width), BF16),
-            jax.ShapeDtypeStruct((modes, width, width), BF16),
+            jax.ShapeDtypeStruct((offset.size,), jnp.int32),
             jax.ShapeDtypeStruct((exp_count * per_tile, patch_cols), F32),
+            jax.ShapeDtypeStruct((3, round_up(modes, 8), LANES), F32),
         ),
         in_specs=[smem, smem, vmem, vmem],
-        out_specs=(vmem,) * 5,
-        scratch_shapes=[
-            pltpu.VMEM((3, round_up(modes, 8), LANES), F32),
-            pltpu.VMEM((modes * tall, height), F32),
-        ],
-        compiler_params=pltpu.CompilerParams(vmem_limit_bytes=16 << 20),
+        out_specs=(smem, vmem, vmem),
+        compiler_params=pltpu.CompilerParams(vmem_limit_bytes=4 << 20),
         name="prep",
     )(owner_ids, offset, vert_taps, horiz_taps)
 
@@ -340,29 +349,31 @@
     for step in range(STEPS):
         first, last = step == 0, step + 1 == STEPS
         picture, near, far = pl.pallas_call(
-            functools.partial(picture_kernel, patch=patch, per_tile=per_tile),
+            functools.partial(picture_kernel, patch=patch),
             out_shape=(
                 jax.ShapeDtypeStruct((pieces, height, breadth), BF16),
                 jax.ShapeDtypeStruct((pieces, rim, breadth), BF16),
                 jax.ShapeDtypeStruct((pieces, rim, breadth), BF16),
             ),
-            in_specs=[smem, smem, smem, vmem],
+            in_specs=[smem, smem, vmem],
             out_specs=(vmem, vmem, vmem),
             scratch_shapes=[pltpu.VMEM((known, patch_cols), F32)],
             compiler_params=pltpu.CompilerParams(vmem_limit_bytes=8 << 20),
             name="picture",
-        )(even, owner_ids, offset, tiles)
+        )(even, ids, tiles)
         far = lax.ppermute(far, "sub", routes[1])
         near = lax.ppermute(near, "sub", routes[0])
         slot = held + (round_up(per_tile, 8) if first else 0)
-        clipped, sums = pl.pallas_call(
-            functools.partial(step_kernel, patch=patch, per_tile=per_tile, slot=slot),
-            out_shape=(
-                jax.ShapeDtypeStruct((pieces, height, breadth), F32),
-                jax.ShapeDtypeStruct((exp_count * slot, patch_cols), F32),
+        results = [jax.ShapeDtypeStruct((exp_count * slot, patch_cols), F32)]
+        if last:
+            results.insert(0, jax.ShapeDtypeStruct((pieces, height, breadth), F32))
+        answer = pl.pallas_call(
+            functools.partial(
+                step_kernel, patch=patch, per_tile=per_tile, slot=slot, taps=vert_taps.shape[1], with_clipped=last
             ),
-            in_specs=[smem] * 3 + [vmem] * 4 + [somewhere] * 8,
-            out_specs=(vmem, vmem),
+            out_shape=tuple(results),
+            in_specs=[smem] * 2 + [vmem] * 5 + [somewhere] * 4,
+            out_specs=(vmem,) * len(results),
             scratch_shapes=[
                 pltpu.VMEM((pieces, height + 2 * rim, breadth), BF16),
                 pltpu.VMEM((pieces, modes * tall, breadth), BF16),
@@ -371,18 +382,18 @@
                 pltpu.VMEM((pieces, modes, tall, breadth), BF16),
                 pltpu.VMEM((pieces, tall, breadth), F32),
                 pltpu.VMEM((2, pieces, PARTS, ext, breadth), BF16),
-                pltpu.VMEM(vertical.shape, BF16),
-                pltpu.VMEM(side.shape, BF16),
-                pltpu.VMEM(forward.shape, BF16),
-                pltpu.VMEM(backward.shape, BF16),
-                pltpu.SemaphoreType.DMA((10,)),
+                pltpu.VMEM((modes * tall, height + 2 * rim), BF16),
+                pltpu.VMEM((height, modes * tall), BF16),
+                pltpu.VMEM((modes, width, width), BF16),
+                pltpu.VMEM((width, width), F32),
+                pltpu.SemaphoreType.DMA((6,)),
             ],
-            compiler_params=pltpu.CompilerParams(vmem_limit_bytes=28 << 20),
+            compiler_params=pltpu.CompilerParams(vmem_limit_bytes=56 << 20),
             name="step",
-        )(
-            even, owner_ids, offset, picture, near, far, counted, coeffs, rims_near, rims_far, observed,
-            vertical, side, forward, backward,
-        )
+        )(even, ids, picture, near, far, counted, taps, coeffs, rims_near, rims_far, observed)
+        sums = answer[-1]
+        if last:
+            clipped = answer[0]
         parts = exchange(sums)
         sky_shape = jax.ShapeDtypeStruct((held, patch_cols), F32)
         results = [sky_shape]

time: 106 us -> 93.3 us (0.88)
  Pallas kernels: 34 us -> 24.8 us
  waiting for transfers between devices: 8.52 us -> 5.39 us
  local copies, waits for them, and re-layouts: 11.4 us -> 8.73 us
  starting transfers between devices: 17.6 us -> 20.2 us
    pallas_call x3, Pallas kernels: 10 us -> 4.32 us  [the longest x1 3 us: per_device(): pl.pallas_call(functools.partial(prep_kernel, per_tile=per_tile), out_sha...]
    all_to_all x1, waiting for transfers between devices: 6.17 us -> 1.73 us  [exchange(): return lax.all_to_all(block, 'exp', split_axis=0, concat_axis=0, tiled=True)]
    ppermute x2, starting transfers between devices: 6.81 us -> 10 us  [per_device(): far = lax.ppermute(far, 'sub', routes[1])]
    unnamed x38 -> x40, local copies, waits for them, and re-layouts: 10.7 us -> 8.06 us
    pallas_call x2, Pallas kernels: 19.5 us -> 17 us  [per_device(): pl.pallas_call(functools.partial(step_kernel, patch=patch, per_tile=per_t...]
    ppermute x2, waiting for transfers between devices: 2.34 us -> 3.65 us  [per_device(): far = lax.ppermute(far, 'sub', routes[1])]
  transfers between devices with their start and end apart: 7 -> 7, of which waited for: 2 -> 3; matrix products, arithmetic and copies ran while one was open for 1% -> 1% of each run, Pallas kernels for 8% -> 4%
where the time goes in v3:
time: 93.3 us; the launch traced here: 92.3 us
  blocking collectives  32.3 us (35%)
  Pallas kernels  24.8 us (27%)
  starting transfers between devices  20.2 us (22%)
  local copies, waits for them, and re-layouts  8.73 us (9%)
  waiting for transfers between devices  5.39 us (6%)
    all_to_all x3, blocking collectives, exchange(): return lax.all_to_all(block, 'exp', split_axis=0, concat_axis=0, tiled=True)  32.3 us
    pallas_call x2, Pallas kernels, per_device(): pl.pallas_call(functools.partial(step_kernel, patch=patch, per_tile=per_t...  17 us
    ppermute x2, starting transfers between devices, per_device(): far = lax.ppermute(far, 'sub', routes[1])  10 us
    unnamed x40, local copies, waits for them, and re-layouts  8.06 us
    all_to_all x1, starting transfers between devices, exchange(): return lax.all_to_all(block, 'exp', split_axis=0, concat_axis=0, tiled=True)  5.53 us
    ppermute x1, starting transfers between devices, per_device(): rims_far = lax.ppermute(rims_far, 'sub', routes[1])  4.49 us
    ppermute x2, waiting for transfers between devices, per_device(): far = lax.ppermute(far, 'sub', routes[1])  3.65 us
    pallas_call x2, Pallas kernels, per_device(): pl.pallas_call(functools.partial(update_kernel, slot=slot, first=first, l...  3.27 us
  transfers between devices with their start and end apart: 7, of which 3 were waited for; matrix products, arithmetic and copies ran while one was open for 1% of the time, Pallas kernels for 4%

profile of v3, /device:TPU:1, one launch (start us, length us, event | category | flops | bytes accessed | tf_op | source)
XLA Modules:
  0.0 92.3 jit_solution(10332292838331720430)
XLA Ops:
  0.6 0.0 copy-start.17
  0.6 0.0 copy-start.18
  0.7 0.0 copy-start.9
  0.7 0.0 copy-start.8
  0.7 0.0 copy-start
  0.7 1.9 %copy-done = bf16[2,12,128,512]{3,2,1,0:T(8,128)(2,1)S(1)} copy-done((bf16[2,12,128,512]{3,2,1,0:T(8,128)(2,1)S(1)}, bf16[2,12,128,512]{3,2,1,0:T(8,128)(2,1)}, u32[]{:S(2)}) %copy-start) | copy-done | bytes 3145752
  2.6 1.0 %copy-done.1 = f32[2,128,512]{2,1,0:T(8,128)S(1)} copy-done((f32[2,128,512]{2,1,0:T(8,128)S(1)}, f32[2,128,512]{2,1,0:T(8,128)}, u32[]{:S(2)}) %copy-start.1) | copy-done | bytes 524312
  3.6 0.2 rims.1
  3.9 0.1 collective-permute-start.2
  4.0 4.5 %collective-permute-start.3 = (bf16[2,15,16,512]{3,2,1,0:T(8,128)(2,1)S(1)}, bf16[2,15,16,512]{3,2,1,0:T(8,128)(2,1)S(1)}, u32[]{:S(2)}, u32[]{:S(2)}) collective-permute-start(bf16[2,15,16,512]{3,2,1,0:T(8,128)(2,1)S(1)} %get-tuple-element.25), channel_id=1, source_target_pairs={{1,2},{2,1},{5,6},{6,5},{9,10},{10,9},{13,14},{14,13},{17,18},{18,... | collective-permute-start | bytes 1474568 | tf_op jit(solution)/shard_map/ppermute | solution.py:333
  8.5 0.0 copy-done.12
  8.5 0.7 broadcast_in_dim.2
  9.2 5.5 %all-to-all-start = ((bf16[8,64,128]{2,1,0:T(8,128)(2,1)}), bf16[8,64,128]{2,1,0:T(8,128)(2,1)S(1)}, u32[]{:S(2)}, u32[]{:S(2)}) async-start(bf16[8,64,128]{2,1,0:T(8,128)(2,1)} %broadcast_in_dim.2), calls=%async_computation | async-start | bytes 262144 | tf_op jit(solution)/shard_map/all_to_all | solution.py:316
  14.7 0.0 copy-done.17
  14.7 0.1 copy.10.offset_ref
  14.8 0.1 copy.9.owners_ref
  14.9 0.0 copy-done.8
  14.9 3.0 %prep.1 = (s32[128]{0:T(128)S(1)}, f32[64,128]{1,0:T(8,128)S(1)}, f32[3,16,128]{2,1,0:T(8,128)S(1)}) custom-call(s32[2,16,4,1]{3,2,1,0:T(4,128)S(1)} %copy.9.owners_ref, s32[2,16,4]{2,1,0:T(8,128)S(1)} %copy.10.offset_ref, bf16[12,21]{1,0:T(8,128)(2,1)S(1)} %copy-done.8, bf16[12,21]{1,0:T(8,128)(2,1)S(1)} %copy-done.9), custom_call_target="tpu_custom_call" | custom-call | tf_op jit(solution)/shard_map/prep/pallas_call | solution.py:335
  17.9 0.0 copy-start.4
  18.0 0.6 copy-done.4
  18.6 0.6 copy-done.5
  19.2 1.7 %all-to-all-done = bf16[8,64,128]{2,1,0:T(8,128)(2,1)S(1)} async-done(((bf16[8,64,128]{2,1,0:T(8,128)(2,1)}), bf16[8,64,128]{2,1,0:T(8,128)(2,1)S(1)}, u32[]{:S(2)}, u32[]{:S(2)}) %all-to-all-start) | async-done | bytes 131104 | tf_op jit(solution)/shard_map/all_to_all | solution.py:316
  20.9 0.7 picture.2
  21.6 0.7 copy-done.2
  22.3 0.0 collective-permute-start
  22.3 3.9 %collective-permute-start.1 = (bf16[2,32,512]{2,1,0:T(8,128)(2,1)S(1)}, bf16[2,32,512]{2,1,0:T(8,128)(2,1)S(1)}, u32[]{:S(2)}, u32[]{:S(2)}) collective-permute-start(bf16[2,32,512]{2,1,0:T(8,128)(2,1)S(1)} %get-tuple-element.21), channel_id=1, source_target_pairs={{1,2},{2,1},{5,6},{6,5},{9,10},{10,9},{13,14},{14,13},{17,18},{18,... | collective-permute-start | bytes 196616 | tf_op jit(solution)/shard_map/ppermute | solution.py:364
  26.2 0.0 collective-permute-done.near_ref
  26.2 1.9 %collective-permute-done.1.far_ref = bf16[2,32,512]{2,1,0:T(8,128)(2,1)S(1)} collective-permute-done((bf16[2,32,512]{2,1,0:T(8,128)(2,1)S(1)}, bf16[2,32,512]{2,1,0:T(8,128)(2,1)S(1)}, u32[]{:S(2)}, u32[]{:S(2)}) %collective-permute-start.1) | collective-permute-done | bytes 65568 | tf_op jit(solution)/shard_map/ppermute | solution.py:364
  28.1 0.0 collective-permute-done.2.rims_near_any
  28.1 0.0 collective-permute-done.3.rims_far_any
  28.2 0.6 copy-done.15
  28.8 0.2 copy-done.10
  29.0 0.2 copy-done.11
  29.1 8.6 %step.2 = f32[576,128]{1,0:T(8,128)} custom-call(s32[1]{0:T(128)} %bitcast.1.even_ref, s32[128]{0:T(128)} %copy-done.6, bf16[2,128,512]{2,1,0:T(8,128)(2,1)} %copy-done.2, bf16[2,32,512]{2,1,0:T(8,128)(2,1)} %copy-done.13, bf16[2,32,512]{2,1,0:T(8,128)(2,1)} %copy-done.15, f32[64,128]{1,0:T(8,128)} %copy-done.4, f32[3,16,128]{2,1,0:T(8,128)} %copy-done.5, ...), custom_call_target="tpu_custom_call" | custom-call | tf_op jit(solution)/shard_map/step/pallas_call | solution.py:370
  37.7 11.7 %all_to_all.41 = f32[8,72,128]{2,1,0:T(8,128)} all-to-all(f32[8,72,128]{2,1,0:T(8,128)} %bitcast.13), channel_id=1, replica_groups=mesh['exp'=8,'sub'=4] {'exp'}, dimensions={0} | all-to-all | bytes 589824 | tf_op jit(solution)/shard_map/all_to_all | solution.py:316
  49.5 1.7 %update.2 = (f32[64,128]{1,0:T(8,128)}, bf16[512,128]{1,0:T(8,128)(2,1)}, f32[64,128]{1,0:T(8,128)}) custom-call(f32[64,128]{1,0:T(8,128)} %bitcast.17, f32[576,128]{1,0:T(8,128)} %bitcast.14), custom_call_target="tpu_custom_call" | custom-call | tf_op jit(solution)/shard_map/update/pallas_call | solution.py:405
  51.1 9.5 %all_to_all.42 = bf16[8,64,128]{2,1,0:T(8,128)(2,1)S(1)} all-to-all(bf16[8,64,128]{2,1,0:T(8,128)(2,1)} %bitcast.18), channel_id=1, replica_groups=mesh['exp'=8,'sub'=4] {'exp'}, dimensions={0} | all-to-all | bytes 262144 | tf_op jit(solution)/shard_map/all_to_all | solution.py:316
  60.6 0.7 copy-done.7
  61.3 0.7 picture.3
  62.0 0.7 copy-done.3
  62.7 0.0 collective-permute-start.4
  62.7 6.1 %collective-permute-start.5 = (bf16[2,32,512]{2,1,0:T(8,128)(2,1)S(1)}, bf16[2,32,512]{2,1,0:T(8,128)(2,1)S(1)}, u32[]{:S(2)}, u32[]{:S(2)}) collective-permute-start(bf16[2,32,512]{2,1,0:T(8,128)(2,1)S(1)} %get-tuple-element.30), channel_id=1, source_target_pairs={{1,2},{2,1},{5,6},{6,5},{9,10},{10,9},{13,14},{14,13},{17,18},{18,... | collective-permute-start | bytes 196616 | tf_op jit(solution)/shard_map/ppermute | solution.py:364
  68.8 0.0 collective-permute-done.4.near_ref
  68.8 1.7 %collective-permute-done.5.far_ref = bf16[2,32,512]{2,1,0:T(8,128)(2,1)S(1)} collective-permute-done((bf16[2,32,512]{2,1,0:T(8,128)(2,1)S(1)}, bf16[2,32,512]{2,1,0:T(8,128)(2,1)S(1)}, u32[]{:S(2)}, u32[]{:S(2)}) %collective-permute-start.5) | collective-permute-done | bytes 65568 | tf_op jit(solution)/shard_map/ppermute | solution.py:364
  70.5 0.6 copy-done.16
  71.2 8.4 %step.3 = (f32[2,128,512]{2,1,0:T(8,128)}, f32[512,128]{1,0:T(8,128)}) custom-call(s32[1]{0:T(128)} %bitcast.1.even_ref, s32[128]{0:T(128)} %copy-done.6, bf16[2,128,512]{2,1,0:T(8,128)(2,1)} %copy-done.3, bf16[2,32,512]{2,1,0:T(8,128)(2,1)} %copy-done.14, bf16[2,32,512]{2,1,0:T(8,128)(2,1)} %copy-done.16, f32[64,128]{1,0:T(8,128)} %copy-done.4, ...), custom_call_target="tpu_custom_call" | custom-call | tf_op jit(solution)/shard_map/step/pallas_call | solution.py:370
  79.6 11.1 %all_to_all.43 = f32[8,64,128]{2,1,0:T(8,128)} all-to-all(f32[8,64,128]{2,1,0:T(8,128)} %bitcast.16), channel_id=1, replica_groups=mesh['exp'=8,'sub'=4] {'exp'}, dimensions={0} | all-to-all | bytes 524288 | tf_op jit(solution)/shard_map/all_to_all | solution.py:316
  90.7 1.6 %update.3 = f32[64,128]{1,0:T(8,128)} custom-call(f32[64,128]{1,0:T(8,128)} %get-tuple-element.26.sky_ref, f32[512,128]{1,0:T(8,128)} %bitcast.15, f32[64,128]{1,0:T(8,128)} %get-tuple-element.32.refs_0_), custom_call_target="tpu_custom_call" | custom-call | tf_op jit(solution)/shard_map/update/pallas_call | solution.py:405
  (19 shorter events, 0.0 us)
Async XLA Ops:
  0.6 14.1 %copy-start.17 = (s32[2,16,4]{1,2,0:T(4,128)S(1)}, s32[2,16,4]{1,2,0:T(4,128)}, u32[]{:S(2)}) copy-start(s32[2,16,4]{1,2,0:T(4,128)} %param.13) | copy-start | bytes 1540
  0.6 14.2 %copy-start.18 = (s32[2,16,4,1]{1,3,2,0:T(1,128)S(1)}, s32[2,16,4,1]{1,3,2,0:T(1,128)}, u32[]{:S(2)}) copy-start(s32[2,16,4,1]{1,3,2,0:T(1,128)} %param.12) | copy-start | bytes 1540
  0.7 14.3 %copy-start.9 = (bf16[12,21]{1,0:T(8,128)(2,1)S(1)}, bf16[12,21]{1,0:T(8,128)(2,1)}, u32[]{:S(2)}) copy-start(bf16[12,21]{1,0:T(8,128)(2,1)} %horiz_ref.1) | copy-start | bytes 1516
  0.7 14.3 %copy-start.8 = (bf16[12,21]{1,0:T(8,128)(2,1)S(1)}, bf16[12,21]{1,0:T(8,128)(2,1)}, u32[]{:S(2)}) copy-start(bf16[12,21]{1,0:T(8,128)(2,1)} %vert_ref.1) | copy-start | bytes 1516
  0.7 1.9 %copy-start = (bf16[2,12,128,512]{3,2,1,0:T(8,128)(2,1)S(1)}, bf16[2,12,128,512]{3,2,1,0:T(8,128)(2,1)}, u32[]{:S(2)}) copy-start(bf16[2,12,128,512]{3,2,1,0:T(8,128)(2,1)} %coeffs_any.3) | copy-start | bytes 9437188
  2.6 1.0 %copy-start.1 = (f32[2,128,512]{2,1,0:T(8,128)S(1)}, f32[2,128,512]{2,1,0:T(8,128)}, u32[]{:S(2)}) copy-start(f32[2,128,512]{2,1,0:T(8,128)} %observed_any.3) | copy-start | bytes 1572868
  3.6 4.9 %copy-start.12 = (f32[1,8,8,128]{3,2,1,0:T(8,128)S(1)}, f32[1,8,8,128]{3,2,1,0:T(8,128)}, u32[]{:S(2)}) copy-start(f32[1,8,8,128]{3,2,1,0:T(8,128)} %param.7) | copy-start | bytes 98308
  3.9 24.3 %collective-permute-start.2 = (bf16[2,15,16,512]{3,2,1,0:T(8,128)(2,1)S(1)}, bf16[2,15,16,512]{3,2,1,0:T(8,128)(2,1)S(1)}, u32[]{:S(2)}, u32[]{:S(2)}) collective-permute-start(bf16[2,15,16,512]{3,2,1,0:T(8,128)(2,1)S(1)} %get-tuple-element.24), channel_id=1, source_target_pairs={{0,1},{2,3},{1,0},{3,2},{4,5},{6,7},{5,4},{7,6},{8,9},{10,11},{9,8... | collective-permute-start | bytes 1474568 | tf_op jit(solution)/shard_map/ppermute | solution.py:334
  4.0 24.2 %collective-permute-start.3 = (bf16[2,15,16,512]{3,2,1,0:T(8,128)(2,1)S(1)}, bf16[2,15,16,512]{3,2,1,0:T(8,128)(2,1)S(1)}, u32[]{:S(2)}, u32[]{:S(2)}) collective-permute-start(bf16[2,15,16,512]{3,2,1,0:T(8,128)(2,1)S(1)} %get-tuple-element.25), channel_id=1, source_target_pairs={{1,2},{2,1},{5,6},{6,5},{9,10},{10,9},{13,14},{14,13},{17,18},{18,... | collective-permute-start | bytes 1474568 | tf_op jit(solution)/shard_map/ppermute | solution.py:333
  9.2 11.7 %all-to-all-start = ((bf16[8,64,128]{2,1,0:T(8,128)(2,1)}), bf16[8,64,128]{2,1,0:T(8,128)(2,1)S(1)}, u32[]{:S(2)}, u32[]{:S(2)}) async-start(bf16[8,64,128]{2,1,0:T(8,128)(2,1)} %broadcast_in_dim.2), calls=%async_computation | async-start | bytes 262144 | tf_op jit(solution)/shard_map/all_to_all | solution.py:316
  17.9 0.6 copy-start.4
  18.6 0.6 copy-start.5
  19.2 9.0 %copy-start.6 = (s32[128]{0:T(128)}, s32[128]{0:T(128)S(1)}, u32[]{:S(2)}) copy-start(s32[128]{0:T(128)S(1)} %get-tuple-element.18.ids_ref) | copy-start | bytes 1540
  21.6 0.7 copy-start.2
  22.3 3.9 %collective-permute-start = (bf16[2,32,512]{2,1,0:T(8,128)(2,1)S(1)}, bf16[2,32,512]{2,1,0:T(8,128)(2,1)S(1)}, u32[]{:S(2)}, u32[]{:S(2)}) collective-permute-start(bf16[2,32,512]{2,1,0:T(8,128)(2,1)S(1)} %get-tuple-element.20), channel_id=1, source_target_pairs={{0,1},{2,3},{1,0},{3,2},{4,5},{6,7},{5,4},{7,6},{8,9},{10,11},{9,8... | collective-permute-start | bytes 196616 | tf_op jit(solution)/shard_map/ppermute | solution.py:365
  22.3 5.9 %collective-permute-start.1 = (bf16[2,32,512]{2,1,0:T(8,128)(2,1)S(1)}, bf16[2,32,512]{2,1,0:T(8,128)(2,1)S(1)}, u32[]{:S(2)}, u32[]{:S(2)}) collective-permute-start(bf16[2,32,512]{2,1,0:T(8,128)(2,1)S(1)} %get-tuple-element.21), channel_id=1, source_target_pairs={{1,2},{2,1},{5,6},{6,5},{9,10},{10,9},{13,14},{14,13},{17,18},{18,... | collective-permute-start | bytes 196616 | tf_op jit(solution)/shard_map/ppermute | solution.py:364
  26.2 2.0 %copy-start.13 = (bf16[2,32,512]{2,1,0:T(8,128)(2,1)}, bf16[2,32,512]{2,1,0:T(8,128)(2,1)S(1)}, u32[]{:S(2)}) copy-start(bf16[2,32,512]{2,1,0:T(8,128)(2,1)S(1)} %collective-permute-done.near_ref) | copy-start | bytes 196612
  28.1 0.6 copy-start.15
  28.1 0.8 copy-start.10
  28.1 1.0 %copy-start.11 = (bf16[2,15,16,512]{3,2,1,0:T(8,128)(2,1)}, bf16[2,15,16,512]{3,2,1,0:T(8,128)(2,1)S(1)}, u32[]{:S(2)}) copy-start(bf16[2,15,16,512]{3,2,1,0:T(8,128)(2,1)S(1)} %collective-permute-done.3.rims_far_any) | copy-start | bytes 1474564
  60.6 0.7 copy-start.7
  61.9 0.7 copy-start.3
  62.7 6.1 %collective-permute-start.4 = (bf16[2,32,512]{2,1,0:T(8,128)(2,1)S(1)}, bf16[2,32,512]{2,1,0:T(8,128)(2,1)S(1)}, u32[]{:S(2)}, u32[]{:S(2)}) collective-permute-start(bf16[2,32,512]{2,1,0:T(8,128)(2,1)S(1)} %get-tuple-element.29), channel_id=1, source_target_pairs={{0,1},{2,3},{1,0},{3,2},{4,5},{6,7},{5,4},{7,6},{8,9},{10,11},{9,8... | collective-permute-start | bytes 196616 | tf_op jit(solution)/shard_map/ppermute | solution.py:365
  62.7 7.9 %collective-permute-start.5 = (bf16[2,32,512]{2,1,0:T(8,128)(2,1)S(1)}, bf16[2,32,512]{2,1,0:T(8,128)(2,1)S(1)}, u32[]{:S(2)}, u32[]{:S(2)}) collective-permute-start(bf16[2,32,512]{2,1,0:T(8,128)(2,1)S(1)} %get-tuple-element.30), channel_id=1, source_target_pairs={{1,2},{2,1},{5,6},{6,5},{9,10},{10,9},{13,14},{14,13},{17,18},{18,... | collective-permute-start | bytes 196616 | tf_op jit(solution)/shard_map/ppermute | solution.py:364
  68.8 1.7 %copy-start.14 = (bf16[2,32,512]{2,1,0:T(8,128)(2,1)}, bf16[2,32,512]{2,1,0:T(8,128)(2,1)S(1)}, u32[]{:S(2)}) copy-start(bf16[2,32,512]{2,1,0:T(8,128)(2,1)S(1)} %collective-permute-done.4.near_ref) | copy-start | bytes 196612
  70.5 0.6 copy-start.16

commit v4 on v3

--- a/solution.py
+++ b/solution.py
@@ -34,13 +34,16 @@
     return routes
 
 
-def rims_kernel(even_ref, coeffs_ref, observed_ref, near_ref, far_ref, seen_ref, sems):
+def begin_kernel(even_ref, sky_any, coeffs_ref, observed_ref, spread_any, near_ref, far_ref, seen_ref, sky_ref, spread_ref, sems):
     modes, height = coeffs_ref.shape[1:3]
     ext = near_ref.shape[2]
+    held = sky_ref.shape[0]
     even = even_ref[0]
     near_at = pl.multiple_of(even * (height - ext), ROWS)
     far_at = pl.multiple_of((1 - even) * (height - ext), ROWS)
     copies = []
+    sky_copy = pltpu.make_async_copy(sky_any, sky_ref, sems.at[4])
+    sky_copy.start()
     for side, (start, out_ref) in enumerate(((near_at, near_ref), (far_at, far_ref))):
         copies.append(
             pltpu.make_async_copy(observed_ref.at[:, pl.ds(start, ext), :], seen_ref.at[side], sems.at[2 * side])
@@ -52,6 +55,12 @@
         )
     for copy in copies:
         copy.start()
+    sky_copy.wait()
+    rounded = sky_ref[...].astype(BF16)
+    for start in range(0, spread_ref.shape[0], held):
+        spread_ref[start : start + held, :] = rounded
+    spread_copy = pltpu.make_async_copy(spread_ref, spread_any, sems.at[5])
+    spread_copy.start()
     for side, out_ref in enumerate((near_ref, far_ref)):
         copies[2 * side].wait()
         rest = seen_ref[side]
@@ -61,25 +70,29 @@
             rest = rest - piece.astype(F32)
     copies[1].wait()
     copies[3].wait()
-
-
-def prep_kernel(owners_ref, offset_ref, vert_ref, horiz_ref, ids_ref, counted_ref, taps_ref, *, per_tile):
+    spread_copy.wait()
+
+
+def prep_kernel(ids_ref, vert_any, horiz_any, counted_ref, taps_ref, vert_ref, horiz_ref, sems):
+    copies = [
+        pltpu.make_async_copy(vert_any, vert_ref, sems.at[0]),
+        pltpu.make_async_copy(horiz_any, horiz_ref, sems.at[1]),
+    ]
+    for copy in copies:
+        copy.start()
     modes, taps = vert_ref.shape
+    counted_ref[...] = jnp.zeros(counted_ref.shape, F32)
+    for place in range(ids_ref.shape[0]):
+        counted_ref[pl.ds(ids_ref[place], 1), :] += 1.0
     taps_ref[...] = jnp.zeros(taps_ref.shape, F32)
+    for copy in copies:
+        copy.wait()
     taps_ref[0, :modes, :taps] = vert_ref[...].astype(F32)
     taps_ref[1, :modes, :taps] = horiz_ref[...].astype(F32)
     turn = lax.broadcasted_iota(jnp.int32, (LANES, LANES), 0) + lax.broadcasted_iota(jnp.int32, (LANES, LANES), 1)
     taps_ref[2] = jnp.dot(
         taps_ref[0].astype(BF16), (turn == taps - 1).astype(F32).astype(BF16), preferred_element_type=F32
     )
-    counted_ref[...] = jnp.zeros(counted_ref.shape, F32)
-    pieces, rows, cols = offset_ref.shape
-    for piece in range(pieces):
-        for row in range(rows):
-            for col in range(cols):
-                index = owners_ref[piece, row, col, 0] * per_tile + offset_ref[piece, row, col]
-                ids_ref[(piece * rows + row) * cols + col] = index
-                counted_ref[pl.ds(index, 1), :] += 1.0
 
 
 def picture_kernel(even_ref, ids_ref, tiles_ref, picture_ref, near_ref, far_ref, wide_ref, *, patch):
@@ -150,7 +163,7 @@
     clipped_ref = refs.pop(0) if with_clipped else None
     (
         sums_ref, image_ref, field_ref, model_ref, gradient_ref, coeffs_ref, seen_ref, seen_rims_ref,
-        vertical_ref, side_ref, across_ref, band_ref, sems,
+        vertical_ref, side_ref, across_ref, band_ref, sems, *totals,
     ) = refs
     pieces, height, breadth = picture_ref.shape
     modes = coeffs_ref.shape[1]
@@ -255,31 +268,38 @@
             gradient_ref[piece, :, low : low + width] = jnp.dot(
                 side_ref[...], field_ref[piece, :, low : low + width], preferred_element_type=F32
             )
-    sums_ref[...] = jnp.zeros(sums_ref.shape, F32)
     held = per_tile * patch_rows
-    if slot > held:
-        for owner in range(sums_ref.shape[0] // slot):
-            start = owner * slot + held
-            sums_ref[start : start + per_tile, :] = counted_ref[owner * per_tile : (owner + 1) * per_tile, :]
+    for total_ref in totals:
+        total_ref[...] = jnp.zeros(total_ref.shape, F32)
     cols = breadth // patch_cols
     rows = height // patch_rows
+    turn = 0
     for row in range(rows):
         for col in range(cols):
             for piece in range(pieces):
                 index = ids_ref[(piece * rows + row) * cols + col]
-                start = index * patch_rows + (index // per_tile) * (slot - held)
-                place = pl.ds(pl.multiple_of(start, patch_rows), patch_rows)
-                sums_ref[place, :] += gradient_ref[
+                place = pl.ds(pl.multiple_of(index * patch_rows, patch_rows), patch_rows)
+                totals[turn % len(totals)][place, :] += gradient_ref[
                     piece, row * patch_rows : (row + 1) * patch_rows, col * patch_cols : (col + 1) * patch_cols
                 ]
+                turn += 1
+    for owner in range(sums_ref.shape[0] // slot):
+        place = slice(owner * held, (owner + 1) * held)
+        total = totals[0][place, :]
+        for total_ref in totals[1:]:
+            total = total + total_ref[place, :]
+        sums_ref[owner * slot : owner * slot + held, :] = total.astype(sums_ref.dtype)
+        if slot > held:
+            named = counted_ref[owner * per_tile : (owner + 1) * per_tile, :]
+            sums_ref[owner * slot + held : owner * slot + held + per_tile, :] = named.astype(sums_ref.dtype)
 
 
 def update_kernel(sky_ref, parts_ref, *refs, slot, first, last):
     refs = list(refs)
     held = sky_ref.shape[0]
-    total = parts_ref[:slot, :]
+    total = parts_ref[:slot, :].astype(F32)
     for start in range(slot, parts_ref.shape[0], slot):
-        total = total + parts_ref[start : start + slot, :]
+        total = total + parts_ref[start : start + slot, :].astype(F32)
     if first:
         named = total[held:]
         repeat = held // named.shape[0]
@@ -315,35 +335,50 @@
     def exchange(block):
         return lax.all_to_all(block, "exp", split_axis=0, concat_axis=0, tiled=True)
 
-    sky = sky_map.reshape(held, patch_cols)
-    spread = jnp.broadcast_to(sky.astype(BF16)[None], (exp_count, held, patch_cols)).reshape(known, patch_cols)
+    sky = pltpu.with_memory_space_constraint(sky_map.reshape(held, patch_cols), pltpu.HBM)
+    even = (1 - lax.axis_index("sub") % 2).astype(jnp.int32).reshape(1)
+    coeffs = pltpu.with_memory_space_constraint(coeffs, pltpu.HBM)
+    observed = pltpu.with_memory_space_constraint(observed, pltpu.HBM)
+    rim_shape = jax.ShapeDtypeStruct((pieces, modes + PARTS, ext, breadth), BF16)
+    spread, rims_near, rims_far = pl.pallas_call(
+        begin_kernel,
+        out_shape=(jax.ShapeDtypeStruct((known, patch_cols), BF16), rim_shape, rim_shape),
+        in_specs=[smem, somewhere, somewhere, somewhere],
+        out_specs=(somewhere, vmem, vmem),
+        scratch_shapes=[
+            pltpu.VMEM((2, pieces, ext, breadth), F32),
+            pltpu.VMEM((held, patch_cols), F32),
+            pltpu.VMEM((known, patch_cols), BF16),
+            pltpu.SemaphoreType.DMA((6,)),
+        ],
+        compiler_params=pltpu.CompilerParams(vmem_limit_bytes=8 << 20),
+        name="begin",
+    )(even, sky, coeffs, observed)
     tiles = exchange(spread)
-    even = (1 - lax.axis_index("sub") % 2).astype(jnp.int32).reshape(1)
-
-    rim_shape = jax.ShapeDtypeStruct((pieces, modes + PARTS, ext, breadth), BF16)
-    rims_near, rims_far = pl.pallas_call(
-        rims_kernel,
-        out_shape=(rim_shape, rim_shape),
-        in_specs=[smem, somewhere, somewhere],
-        out_specs=(vmem, vmem),
-        scratch_shapes=[pltpu.VMEM((2, pieces, ext, breadth), F32), pltpu.SemaphoreType.DMA((4,))],
-        compiler_params=pltpu.CompilerParams(vmem_limit_bytes=8 << 20),
-        name="rims",
-    )(even, coeffs, observed)
-    rims_far = lax.ppermute(rims_far, "sub", routes[1])
-    rims_near = lax.ppermute(rims_near, "sub", routes[0])
-    ids, counted, taps = pl.pallas_call(
-        functools.partial(prep_kernel, per_tile=per_tile),
+    ids = (owner_ids.reshape(offset.shape) * per_tile + offset).reshape(-1)
+    counted, taps = pl.pallas_call(
+        prep_kernel,
         out_shape=(
-            jax.ShapeDtypeStruct((offset.size,), jnp.int32),
             jax.ShapeDtypeStruct((exp_count * per_tile, patch_cols), F32),
             jax.ShapeDtypeStruct((3, round_up(modes, 8), LANES), F32),
         ),
-        in_specs=[smem, smem, vmem, vmem],
-        out_specs=(smem, vmem, vmem),
+        in_specs=[smem, somewhere, somewhere],
+        out_specs=(vmem, vmem),
+        scratch_shapes=[
+            pltpu.VMEM(vert_taps.shape, BF16),
+            pltpu.VMEM(horiz_taps.shape, BF16),
+            pltpu.SemaphoreType.DMA((2,)),
+        ],
         compiler_params=pltpu.CompilerParams(vmem_limit_bytes=4 << 20),
         name="prep",
-    )(owner_ids, offset, vert_taps, horiz_taps)
+    )(
+        ids,
+        pltpu.with_memory_space_constraint(vert_taps, pltpu.HBM),
+        pltpu.with_memory_space_constraint(horiz_taps, pltpu.HBM),
+    )
+    rims_far = lax.ppermute(rims_far, "sub", routes[1])
+    rims_near = lax.ppermute(rims_near, "sub", routes[0])
+    ids, counted, taps = lax.optimization_barrier((ids, counted, taps))
 
     clipped, counts = None, None
     for step in range(STEPS):
@@ -387,8 +422,9 @@
                 pltpu.VMEM((modes, width, width), BF16),
                 pltpu.VMEM((width, width), F32),
                 pltpu.SemaphoreType.DMA((6,)),
-            ],
-            compiler_params=pltpu.CompilerParams(vmem_limit_bytes=56 << 20),
+            ]
+            + [pltpu.VMEM((known, patch_cols), F32)] * 4,
+            compiler_params=pltpu.CompilerParams(vmem_limit_bytes=24 << 20),
             name="step",
         )(even, ids, picture, near, far, counted, taps, coeffs, rims_near, rims_far, observed)
         sums = answer[-1]
@@ -407,6 +443,7 @@
             out_shape=tuple(results),
             in_specs=[vmem] * len(operands),
             out_specs=(vmem,) * len(results),
+            compiler_params=pltpu.CompilerParams(vmem_limit_bytes=4 << 20),
             name="update",
         )(*operands)
         sky = answer[0]

time: 93.3 us -> 78.6 us (0.84)
  local copies, waits for them, and re-layouts: 8.73 us -> 0.2 us
  Pallas kernels: 24.8 us -> 20.1 us
  blocking collectives: 32.3 us -> 28.1 us
  waiting for transfers between devices: 5.39 us -> 8.24 us
    unnamed x40 -> x4, local copies, waits for them, and re-layouts: 8.06 us -> 0.01 us
    all_to_all x3, blocking collectives: 32.3 us -> 28.1 us  [exchange(): return lax.all_to_all(block, 'exp', split_axis=0, concat_axis=0, tiled=True)]
    all_to_all x1, waiting for transfers between devices: 1.73 us -> 4.56 us  [exchange(): return lax.all_to_all(block, 'exp', split_axis=0, concat_axis=0, tiled=True)]
    pallas_call x2, Pallas kernels: 17 us -> 14.5 us  [per_device(): pl.pallas_call(functools.partial(step_kernel, patch=patch, per_tile=per_t...]
    pallas_call x2, Pallas kernels: 3.27 us -> 1.43 us  [per_device(): pl.pallas_call(functools.partial(update_kernel, slot=slot, first=first, l...]
  transfers between devices with their start and end apart: 7 -> 7, of which waited for: 3 -> 3; matrix products, arithmetic and copies ran while one was open for 1% -> 0% of each run, Pallas kernels for 4% -> 3%
where the time goes in v4:
time: 78.6 us; the launch traced here: 77.9 us
  blocking collectives  28.1 us (36%)
  starting transfers between devices  20.4 us (26%)
  Pallas kernels  20.1 us (26%)
  waiting for transfers between devices  8.24 us (10%)
  between operations  0.8 us (1%)
    all_to_all x3, blocking collectives, exchange(): return lax.all_to_all(block, 'exp', split_axis=0, concat_axis=0, tiled=True)  28.1 us
    pallas_call x2, Pallas kernels, per_device(): pl.pallas_call(functools.partial(step_kernel, patch=patch, per_tile=per_t...  14.5 us
    ppermute x2, starting transfers between devices, per_device(): far = lax.ppermute(far, 'sub', routes[1])  10.1 us
    all_to_all x1, starting transfers between devices, exchange(): return lax.all_to_all(block, 'exp', split_axis=0, concat_axis=0, tiled=True)  5.54 us
    all_to_all x1, waiting for transfers between devices, exchange(): return lax.all_to_all(block, 'exp', split_axis=0, concat_axis=0, tiled=True)  4.56 us
    ppermute x1, starting transfers between devices, per_device(): rims_far = lax.ppermute(rims_far, 'sub', routes[1])  4.49 us
    ppermute x2, waiting for transfers between devices, per_device(): far = lax.ppermute(far, 'sub', routes[1])  3.67 us
  transfers between devices with their start and end apart: 7, of which 3 were waited for; matrix products, arithmetic and copies ran while one was open for 0% of the time, Pallas kernels for 3%

profile of v4, /device:TPU:1, one launch (start us, length us, event | category | flops | bytes accessed | tf_op | source)
XLA Modules:
  0.0 77.9 jit_solution(5824212936840615439)
XLA Ops:
  0.6 0.0 copy-start.1
  0.6 0.0 copy-start
  0.7 1.5 %begin.1 = (bf16[512,128]{1,0:T(8,128)(2,1)}, bf16[2,15,16,512]{3,2,1,0:T(8,128)(2,1)S(1)}, bf16[2,15,16,512]{3,2,1,0:T(8,128)(2,1)S(1)}) custom-call(s32[1]{0:T(128)} %bitcast.1.even_ref, f32[64,128]{1,0:T(8,128)} %bitcast.19, bf16[2,12,128,512]{3,2,1,0:T(8,128)(2,1)} %coeffs_any.3, f32[2,128,512]{2,1,0:T(8,128)} %observed_any.3), custom_call_target="tpu_custom_call" | custom-call | tf_op jit(solution)/shard_map/begin/pallas_call | solution.py:343
  2.1 0.1 collective-permute-start.2
  2.3 4.5 %collective-permute-start.3 = (bf16[2,15,16,512]{3,2,1,0:T(8,128)(2,1)S(1)}, bf16[2,15,16,512]{3,2,1,0:T(8,128)(2,1)S(1)}, u32[]{:S(2)}, u32[]{:S(2)}) collective-permute-start(bf16[2,15,16,512]{3,2,1,0:T(8,128)(2,1)S(1)} %get-tuple-element.31), channel_id=1, source_target_pairs={{1,2},{2,1},{5,6},{6,5},{9,10},{10,9},{13,14},{14,13},{17,18},{18,... | collective-permute-start | bytes 1474568 | tf_op jit(solution)/shard_map/ppermute | solution.py:379
  6.8 5.5 %all-to-all-start = ((bf16[8,64,128]{2,1,0:T(8,128)(2,1)}), bf16[8,64,128]{2,1,0:T(8,128)(2,1)S(1)}, u32[]{:S(2)}, u32[]{:S(2)}) async-start(bf16[8,64,128]{2,1,0:T(8,128)(2,1)} %bitcast.3), calls=%async_computation | async-start | bytes 262144 | tf_op jit(solution)/shard_map/all_to_all | solution.py:336
  12.3 0.0 copy-done.1
  12.3 0.0 copy-done
  12.3 0.1 copy.10
  12.4 0.1 reshape.29.ids_ref
  12.5 1.4 %prep.1 = (f32[64,128]{1,0:T(8,128)S(1)}, f32[3,16,128]{2,1,0:T(8,128)S(1)}) custom-call(s32[128]{0:T(128)S(1)} %reshape.29.ids_ref, bf16[12,21]{1,0:T(8,128)(2,1)} %vert_any.1, bf16[12,21]{1,0:T(8,128)(2,1)} %horiz_any.1), custom_call_target="tpu_custom_call" | custom-call | tf_op jit(solution)/shard_map/prep/pallas_call | solution.py:359
  13.9 4.6 %all-to-all-done = bf16[8,64,128]{2,1,0:T(8,128)(2,1)S(1)} async-done(((bf16[8,64,128]{2,1,0:T(8,128)(2,1)}), bf16[8,64,128]{2,1,0:T(8,128)(2,1)S(1)}, u32[]{:S(2)}, u32[]{:S(2)}) %all-to-all-start) | async-done | bytes 131104 | tf_op jit(solution)/shard_map/all_to_all | solution.py:336
  18.5 0.7 picture.2
  19.2 0.1 collective-permute-start
  19.3 3.9 %collective-permute-start.1 = (bf16[2,32,512]{2,1,0:T(8,128)(2,1)S(1)}, bf16[2,32,512]{2,1,0:T(8,128)(2,1)S(1)}, u32[]{:S(2)}, u32[]{:S(2)}) collective-permute-start(bf16[2,32,512]{2,1,0:T(8,128)(2,1)S(1)} %get-tuple-element.27), channel_id=1, source_target_pairs={{1,2},{2,1},{5,6},{6,5},{9,10},{10,9},{13,14},{14,13},{17,18},{18,... | collective-permute-start | bytes 196616 | tf_op jit(solution)/shard_map/ppermute | solution.py:399
  23.2 0.0 collective-permute-done.near_ref
  23.2 1.9 %collective-permute-done.1.far_ref = bf16[2,32,512]{2,1,0:T(8,128)(2,1)S(1)} collective-permute-done((bf16[2,32,512]{2,1,0:T(8,128)(2,1)S(1)}, bf16[2,32,512]{2,1,0:T(8,128)(2,1)S(1)}, u32[]{:S(2)}, u32[]{:S(2)}) %collective-permute-start.1) | collective-permute-done | bytes 65568 | tf_op jit(solution)/shard_map/ppermute | solution.py:399
  25.1 0.0 collective-permute-done.2.rims_near_any
  25.1 0.0 collective-permute-done.3.rims_far_any
  25.1 6.9 %step.2 = f32[576,128]{1,0:T(8,128)S(1)} custom-call(s32[1]{0:T(128)} %bitcast.1.even_ref, s32[128]{0:T(128)S(1)} %reshape.29.ids_ref, bf16[2,128,512]{2,1,0:T(8,128)(2,1)S(1)} %get-tuple-element.25.picture_ref, bf16[2,32,512]{2,1,0:T(8,128)(2,1)S(1)} %collective-permute-done.near_ref, bf16[2,32,512]{2,1,0:T(8,128)(2,1)S(1)} %collective-permute-done.1.far_ref, ...), custom_call_target="tpu_custom_call" | custom-call | tf_op jit(solution)/shard_map/step/pallas_call | solution.py:405
  32.0 10.0 %all_to_all.44 = f32[8,72,128]{2,1,0:T(8,128)S(1)} all-to-all(f32[8,72,128]{2,1,0:T(8,128)S(1)} %bitcast.12), channel_id=1, replica_groups=mesh['exp'=8,'sub'=4] {'exp'}, dimensions={0} | all-to-all | bytes 589824 | tf_op jit(solution)/shard_map/all_to_all | solution.py:336
  42.0 0.8 %update.2 = (f32[64,128]{1,0:T(8,128)S(1)}, bf16[512,128]{1,0:T(8,128)(2,1)S(1)}, f32[64,128]{1,0:T(8,128)S(1)}) custom-call(f32[64,128]{1,0:T(8,128)} %bitcast.20, f32[576,128]{1,0:T(8,128)S(1)} %bitcast.13), custom_call_target="tpu_custom_call" | custom-call | tf_op jit(solution)/shard_map/update/pallas_call | solution.py:441
  42.8 8.6 %all_to_all.45 = bf16[8,64,128]{2,1,0:T(8,128)(2,1)S(1)} all-to-all(bf16[8,64,128]{2,1,0:T(8,128)(2,1)S(1)} %bitcast.18), channel_id=1, replica_groups=mesh['exp'=8,'sub'=4] {'exp'}, dimensions={0} | all-to-all | bytes 262144 | tf_op jit(solution)/shard_map/all_to_all | solution.py:336
  51.4 0.7 picture.3
  52.1 0.1 collective-permute-start.4
  52.2 6.2 %collective-permute-start.5 = (bf16[2,32,512]{2,1,0:T(8,128)(2,1)S(1)}, bf16[2,32,512]{2,1,0:T(8,128)(2,1)S(1)}, u32[]{:S(2)}, u32[]{:S(2)}) collective-permute-start(bf16[2,32,512]{2,1,0:T(8,128)(2,1)S(1)} %get-tuple-element.36), channel_id=1, source_target_pairs={{1,2},{2,1},{5,6},{6,5},{9,10},{10,9},{13,14},{14,13},{17,18},{18,... | collective-permute-start | bytes 196616 | tf_op jit(solution)/shard_map/ppermute | solution.py:399
  58.4 0.0 collective-permute-done.4.near_ref
  58.4 1.7 %collective-permute-done.5.far_ref = bf16[2,32,512]{2,1,0:T(8,128)(2,1)S(1)} collective-permute-done((bf16[2,32,512]{2,1,0:T(8,128)(2,1)S(1)}, bf16[2,32,512]{2,1,0:T(8,128)(2,1)S(1)}, u32[]{:S(2)}, u32[]{:S(2)}) %collective-permute-start.5) | collective-permute-done | bytes 65568 | tf_op jit(solution)/shard_map/ppermute | solution.py:399
  60.1 7.6 %step.3 = (f32[2,128,512]{2,1,0:T(8,128)}, f32[512,128]{1,0:T(8,128)S(1)}) custom-call(s32[1]{0:T(128)} %bitcast.1.even_ref, s32[128]{0:T(128)S(1)} %reshape.29.ids_ref, bf16[2,128,512]{2,1,0:T(8,128)(2,1)S(1)} %get-tuple-element.34.picture_ref, bf16[2,32,512]{2,1,0:T(8,128)(2,1)S(1)} %collective-permute-done.4.near_ref, ...), custom_call_target="tpu_custom_call" | custom-call | tf_op jit(solution)/shard_map/step/pallas_call | solution.py:405
  67.7 9.5 %all_to_all.46 = f32[8,64,128]{2,1,0:T(8,128)S(1)} all-to-all(f32[8,64,128]{2,1,0:T(8,128)S(1)} %bitcast.17), channel_id=1, replica_groups=mesh['exp'=8,'sub'=4] {'exp'}, dimensions={0} | all-to-all | bytes 524288 | tf_op jit(solution)/shard_map/all_to_all | solution.py:336
  77.2 0.6 update.3
  (2 shorter events, 0.0 us)
Async XLA Ops:
  0.6 11.7 %copy-start.1 = (s32[2,16,4,1]{1,3,2,0:T(1,128)S(1)}, s32[2,16,4,1]{1,3,2,0:T(1,128)}, u32[]{:S(2)}) copy-start(s32[2,16,4,1]{1,3,2,0:T(1,128)} %param.12) | copy-start | bytes 1540
  0.6 11.7 %copy-start = (s32[2,16,4]{1,2,0:T(4,128)S(1)}, s32[2,16,4]{1,2,0:T(4,128)}, u32[]{:S(2)}) copy-start(s32[2,16,4]{1,2,0:T(4,128)} %param.13) | copy-start | bytes 1540
  2.1 23.0 %collective-permute-start.2 = (bf16[2,15,16,512]{3,2,1,0:T(8,128)(2,1)S(1)}, bf16[2,15,16,512]{3,2,1,0:T(8,128)(2,1)S(1)}, u32[]{:S(2)}, u32[]{:S(2)}) collective-permute-start(bf16[2,15,16,512]{3,2,1,0:T(8,128)(2,1)S(1)} %get-tuple-element.30), channel_id=1, source_target_pairs={{0,1},{2,3},{1,0},{3,2},{4,5},{6,7},{5,4},{7,6},{8,9},{10,11},{9,8... | collective-permute-start | bytes 1474568 | tf_op jit(solution)/shard_map/ppermute | solution.py:380
  2.3 22.9 %collective-permute-start.3 = (bf16[2,15,16,512]{3,2,1,0:T(8,128)(2,1)S(1)}, bf16[2,15,16,512]{3,2,1,0:T(8,128)(2,1)S(1)}, u32[]{:S(2)}, u32[]{:S(2)}) collective-permute-start(bf16[2,15,16,512]{3,2,1,0:T(8,128)(2,1)S(1)} %get-tuple-element.31), channel_id=1, source_target_pairs={{1,2},{2,1},{5,6},{6,5},{9,10},{10,9},{13,14},{14,13},{17,18},{18,... | collective-permute-start | bytes 1474568 | tf_op jit(solution)/shard_map/ppermute | solution.py:379
  6.8 11.7 %all-to-all-start = ((bf16[8,64,128]{2,1,0:T(8,128)(2,1)}), bf16[8,64,128]{2,1,0:T(8,128)(2,1)S(1)}, u32[]{:S(2)}, u32[]{:S(2)}) async-start(bf16[8,64,128]{2,1,0:T(8,128)(2,1)} %bitcast.3), calls=%async_computation | async-start | bytes 262144 | tf_op jit(solution)/shard_map/all_to_all | solution.py:336
  19.2 4.0 %collective-permute-start = (bf16[2,32,512]{2,1,0:T(8,128)(2,1)S(1)}, bf16[2,32,512]{2,1,0:T(8,128)(2,1)S(1)}, u32[]{:S(2)}, u32[]{:S(2)}) collective-permute-start(bf16[2,32,512]{2,1,0:T(8,128)(2,1)S(1)} %get-tuple-element.26), channel_id=1, source_target_pairs={{0,1},{2,3},{1,0},{3,2},{4,5},{6,7},{5,4},{7,6},{8,9},{10,11},{9,8... | collective-permute-start | bytes 196616 | tf_op jit(solution)/shard_map/ppermute | solution.py:400
  19.3 5.9 %collective-permute-start.1 = (bf16[2,32,512]{2,1,0:T(8,128)(2,1)S(1)}, bf16[2,32,512]{2,1,0:T(8,128)(2,1)S(1)}, u32[]{:S(2)}, u32[]{:S(2)}) collective-permute-start(bf16[2,32,512]{2,1,0:T(8,128)(2,1)S(1)} %get-tuple-element.27), channel_id=1, source_target_pairs={{1,2},{2,1},{5,6},{6,5},{9,10},{10,9},{13,14},{14,13},{17,18},{18,... | collective-permute-start | bytes 196616 | tf_op jit(solution)/shard_map/ppermute | solution.py:399
  52.1 6.3 %collective-permute-start.4 = (bf16[2,32,512]{2,1,0:T(8,128)(2,1)S(1)}, bf16[2,32,512]{2,1,0:T(8,128)(2,1)S(1)}, u32[]{:S(2)}, u32[]{:S(2)}) collective-permute-start(bf16[2,32,512]{2,1,0:T(8,128)(2,1)S(1)} %get-tuple-element.35), channel_id=1, source_target_pairs={{0,1},{2,3},{1,0},{3,2},{4,5},{6,7},{5,4},{7,6},{8,9},{10,11},{9,8... | collective-permute-start | bytes 196616 | tf_op jit(solution)/shard_map/ppermute | solution.py:400
  52.2 7.9 %collective-permute-start.5 = (bf16[2,32,512]{2,1,0:T(8,128)(2,1)S(1)}, bf16[2,32,512]{2,1,0:T(8,128)(2,1)S(1)}, u32[]{:S(2)}, u32[]{:S(2)}) collective-permute-start(bf16[2,32,512]{2,1,0:T(8,128)(2,1)S(1)} %get-tuple-element.36), channel_id=1, source_target_pairs={{1,2},{2,1},{5,6},{6,5},{9,10},{10,9},{13,14},{14,13},{17,18},{18,... | collective-permute-start | bytes 196616 | tf_op jit(solution)/shard_map/ppermute | solution.py:399

commit v5 on v4

--- a/solution.py
+++ b/solution.py
@@ -291,18 +291,21 @@
         sums_ref[owner * slot : owner * slot + held, :] = total.astype(sums_ref.dtype)
         if slot > held:
             named = counted_ref[owner * per_tile : (owner + 1) * per_tile, :]
-            sums_ref[owner * slot + held : owner * slot + held + per_tile, :] = named.astype(sums_ref.dtype)
-
-
-def update_kernel(sky_ref, parts_ref, *refs, slot, first, last):
+            spare = jnp.zeros((slot - held - per_tile, named.shape[1]), F32)
+            sums_ref[owner * slot + held : (owner + 1) * slot, :] = jnp.concatenate([named, spare], axis=0).astype(
+                sums_ref.dtype
+            )
+
+
+def update_kernel(sky_ref, parts_ref, *refs, per_tile, slot, first, last):
     refs = list(refs)
     held = sky_ref.shape[0]
     total = parts_ref[:slot, :].astype(F32)
     for start in range(slot, parts_ref.shape[0], slot):
         total = total + parts_ref[start : start + slot, :].astype(F32)
     if first:
-        named = total[held:]
-        repeat = held // named.shape[0]
+        named = total[held : held + per_tile]
+        repeat = held // per_tile
         counts = jnp.broadcast_to(named[:, None, :], (named.shape[0], repeat, named.shape[1])).reshape(sky_ref.shape)
         refs.pop()[...] = counts
     else:
@@ -398,8 +401,8 @@
         )(even, ids, tiles)
         far = lax.ppermute(far, "sub", routes[1])
         near = lax.ppermute(near, "sub", routes[0])
-        slot = held + (round_up(per_tile, 8) if first else 0)
-        results = [jax.ShapeDtypeStruct((exp_count * slot, patch_cols), F32)]
+        slot = held + (round_up(per_tile, ROWS) if first else 0)
+        results = [jax.ShapeDtypeStruct((exp_count * slot, patch_cols), BF16)]
         if last:
             results.insert(0, jax.ShapeDtypeStruct((pieces, height, breadth), F32))
         answer = pl.pallas_call(
@@ -439,7 +442,7 @@
             results.append(sky_shape)
         operands = [sky, parts] if first else [sky, parts, counts]
         answer = pl.pallas_call(
-            functools.partial(update_kernel, slot=slot, first=first, last=last),
+            functools.partial(update_kernel, per_tile=per_tile, slot=slot, first=first, last=last),
             out_shape=tuple(results),
             in_specs=[vmem] * len(operands),
             out_specs=(vmem,) * len(results),

time: 78.6 us -> 76.4 us (0.972)
  blocking collectives: 28.1 us -> 26 us
    all_to_all x3, blocking collectives: 28.1 us -> 26 us  [exchange(): return lax.all_to_all(block, 'exp', split_axis=0, concat_axis=0, tiled=True)]
where the time goes in v5:
time: 76.4 us; the launch traced here: 75.7 us
  blocking collectives  26 us (34%)
  starting transfers between devices  20.3 us (27%)
  Pallas kernels  20.1 us (26%)
  waiting for transfers between devices  8.24 us (11%)
  between operations  0.8 us (1%)
    all_to_all x3, blocking collectives, exchange(): return lax.all_to_all(block, 'exp', split_axis=0, concat_axis=0, tiled=True)  26 us
    pallas_call x2, Pallas kernels, per_device(): pl.pallas_call(functools.partial(step_kernel, patch=patch, per_tile=per_t...  14.5 us
    ppermute x2, starting transfers between devices, per_device(): far = lax.ppermute(far, 'sub', routes[1])  10.1 us
    all_to_all x1, starting transfers between devices, exchange(): return lax.all_to_all(block, 'exp', split_axis=0, concat_axis=0, tiled=True)  5.54 us
    all_to_all x1, waiting for transfers between devices, exchange(): return lax.all_to_all(block, 'exp', split_axis=0, concat_axis=0, tiled=True)  4.56 us
    ppermute x1, starting transfers between devices, per_device(): rims_far = lax.ppermute(rims_far, 'sub', routes[1])  4.49 us
    ppermute x2, waiting for transfers between devices, per_device(): far = lax.ppermute(far, 'sub', routes[1])  3.67 us
  transfers between devices with their start and end apart: 7, of which 3 were waited for; matrix products, arithmetic and copies ran while one was open for 0% of the time, Pallas kernels for 3%

profile of v5, /device:TPU:1, one launch (start us, length us, event | category | flops | bytes accessed | tf_op | source)
XLA Modules:
  0.0 75.7 jit_solution(1524924821524264714)
XLA Ops:
  0.6 0.0 copy-start.1
  0.6 0.0 copy-start
  0.7 1.5 %begin.1 = (bf16[512,128]{1,0:T(8,128)(2,1)}, bf16[2,15,16,512]{3,2,1,0:T(8,128)(2,1)S(1)}, bf16[2,15,16,512]{3,2,1,0:T(8,128)(2,1)S(1)}) custom-call(s32[1]{0:T(128)} %bitcast.1.even_ref, f32[64,128]{1,0:T(8,128)} %bitcast.19, bf16[2,12,128,512]{3,2,1,0:T(8,128)(2,1)} %coeffs_any.3, f32[2,128,512]{2,1,0:T(8,128)} %observed_any.3), custom_call_target="tpu_custom_call" | custom-call | tf_op jit(solution)/shard_map/begin/pallas_call | solution.py:346
  2.1 0.1 collective-permute-start.2
  2.3 4.5 %collective-permute-start.3 = (bf16[2,15,16,512]{3,2,1,0:T(8,128)(2,1)S(1)}, bf16[2,15,16,512]{3,2,1,0:T(8,128)(2,1)S(1)}, u32[]{:S(2)}, u32[]{:S(2)}) collective-permute-start(bf16[2,15,16,512]{3,2,1,0:T(8,128)(2,1)S(1)} %get-tuple-element.31), channel_id=1, source_target_pairs={{1,2},{2,1},{5,6},{6,5},{9,10},{10,9},{13,14},{14,13},{17,18},{18,... | collective-permute-start | bytes 1474568 | tf_op jit(solution)/shard_map/ppermute | solution.py:382
  6.8 5.5 %all-to-all-start = ((bf16[8,64,128]{2,1,0:T(8,128)(2,1)}), bf16[8,64,128]{2,1,0:T(8,128)(2,1)S(1)}, u32[]{:S(2)}, u32[]{:S(2)}) async-start(bf16[8,64,128]{2,1,0:T(8,128)(2,1)} %bitcast.3), calls=%async_computation | async-start | bytes 262144 | tf_op jit(solution)/shard_map/all_to_all | solution.py:339
  12.3 0.0 copy-done.1
  12.3 0.0 copy-done
  12.3 0.1 copy.10
  12.4 0.1 reshape.29.ids_ref
  12.5 1.4 %prep.1 = (f32[64,128]{1,0:T(8,128)S(1)}, f32[3,16,128]{2,1,0:T(8,128)S(1)}) custom-call(s32[128]{0:T(128)S(1)} %reshape.29.ids_ref, bf16[12,21]{1,0:T(8,128)(2,1)} %vert_any.1, bf16[12,21]{1,0:T(8,128)(2,1)} %horiz_any.1), custom_call_target="tpu_custom_call" | custom-call | tf_op jit(solution)/shard_map/prep/pallas_call | solution.py:362
  13.9 4.6 %all-to-all-done = bf16[8,64,128]{2,1,0:T(8,128)(2,1)S(1)} async-done(((bf16[8,64,128]{2,1,0:T(8,128)(2,1)}), bf16[8,64,128]{2,1,0:T(8,128)(2,1)S(1)}, u32[]{:S(2)}, u32[]{:S(2)}) %all-to-all-start) | async-done | bytes 131104 | tf_op jit(solution)/shard_map/all_to_all | solution.py:339
  18.5 0.7 picture.2
  19.2 0.1 collective-permute-start
  19.3 3.9 %collective-permute-start.1 = (bf16[2,32,512]{2,1,0:T(8,128)(2,1)S(1)}, bf16[2,32,512]{2,1,0:T(8,128)(2,1)S(1)}, u32[]{:S(2)}, u32[]{:S(2)}) collective-permute-start(bf16[2,32,512]{2,1,0:T(8,128)(2,1)S(1)} %get-tuple-element.27), channel_id=1, source_target_pairs={{1,2},{2,1},{5,6},{6,5},{9,10},{10,9},{13,14},{14,13},{17,18},{18,... | collective-permute-start | bytes 196616 | tf_op jit(solution)/shard_map/ppermute | solution.py:402
  23.2 0.0 collective-permute-done.near_ref
  23.2 1.9 %collective-permute-done.1.far_ref = bf16[2,32,512]{2,1,0:T(8,128)(2,1)S(1)} collective-permute-done((bf16[2,32,512]{2,1,0:T(8,128)(2,1)S(1)}, bf16[2,32,512]{2,1,0:T(8,128)(2,1)S(1)}, u32[]{:S(2)}, u32[]{:S(2)}) %collective-permute-start.1) | collective-permute-done | bytes 65568 | tf_op jit(solution)/shard_map/ppermute | solution.py:402
  25.1 0.0 collective-permute-done.2.rims_near_any
  25.1 0.0 collective-permute-done.3.rims_far_any
  25.1 6.9 %step.2 = bf16[640,128]{1,0:T(8,128)(2,1)S(1)} custom-call(s32[1]{0:T(128)} %bitcast.1.even_ref, s32[128]{0:T(128)S(1)} %reshape.29.ids_ref, bf16[2,128,512]{2,1,0:T(8,128)(2,1)S(1)} %get-tuple-element.25.picture_ref, bf16[2,32,512]{2,1,0:T(8,128)(2,1)S(1)} %collective-permute-done.near_ref, bf16[2,32,512]{2,1,0:T(8,128)(2,1)S(1)} %collective-permute-done.1.far_ref, ...), custom_call_target="tpu_custom_call" | custom-call | tf_op jit(solution)/shard_map/step/pallas_call | solution.py:408
  32.0 8.8 %all_to_all.44 = bf16[8,80,128]{2,1,0:T(8,128)(2,1)S(1)} all-to-all(bf16[8,80,128]{2,1,0:T(8,128)(2,1)S(1)} %bitcast.12), channel_id=1, replica_groups=mesh['exp'=8,'sub'=4] {'exp'}, dimensions={0} | all-to-all | bytes 327680 | tf_op jit(solution)/shard_map/all_to_all | solution.py:339
  40.8 0.8 %update.2 = (f32[64,128]{1,0:T(8,128)S(1)}, bf16[512,128]{1,0:T(8,128)(2,1)S(1)}, f32[64,128]{1,0:T(8,128)S(1)}) custom-call(f32[64,128]{1,0:T(8,128)} %bitcast.20, bf16[640,128]{1,0:T(8,128)(2,1)S(1)} %bitcast.13), custom_call_target="tpu_custom_call" | custom-call | tf_op jit(solution)/shard_map/update/pallas_call | solution.py:444
  41.6 8.6 %all_to_all.45 = bf16[8,64,128]{2,1,0:T(8,128)(2,1)S(1)} all-to-all(bf16[8,64,128]{2,1,0:T(8,128)(2,1)S(1)} %bitcast.18), channel_id=1, replica_groups=mesh['exp'=8,'sub'=4] {'exp'}, dimensions={0} | all-to-all | bytes 262144 | tf_op jit(solution)/shard_map/all_to_all | solution.py:339
  50.2 0.7 picture.3
  50.9 0.1 collective-permute-start.4
  51.0 6.1 %collective-permute-start.5 = (bf16[2,32,512]{2,1,0:T(8,128)(2,1)S(1)}, bf16[2,32,512]{2,1,0:T(8,128)(2,1)S(1)}, u32[]{:S(2)}, u32[]{:S(2)}) collective-permute-start(bf16[2,32,512]{2,1,0:T(8,128)(2,1)S(1)} %get-tuple-element.36), channel_id=1, source_target_pairs={{1,2},{2,1},{5,6},{6,5},{9,10},{10,9},{13,14},{14,13},{17,18},{18,... | collective-permute-start | bytes 196616 | tf_op jit(solution)/shard_map/ppermute | solution.py:402
  57.1 0.0 collective-permute-done.4.near_ref
  57.1 1.7 %collective-permute-done.5.far_ref = bf16[2,32,512]{2,1,0:T(8,128)(2,1)S(1)} collective-permute-done((bf16[2,32,512]{2,1,0:T(8,128)(2,1)S(1)}, bf16[2,32,512]{2,1,0:T(8,128)(2,1)S(1)}, u32[]{:S(2)}, u32[]{:S(2)}) %collective-permute-start.5) | collective-permute-done | bytes 65568 | tf_op jit(solution)/shard_map/ppermute | solution.py:402
  58.8 7.6 %step.3 = (f32[2,128,512]{2,1,0:T(8,128)}, bf16[512,128]{1,0:T(8,128)(2,1)S(1)}) custom-call(s32[1]{0:T(128)} %bitcast.1.even_ref, s32[128]{0:T(128)S(1)} %reshape.29.ids_ref, bf16[2,128,512]{2,1,0:T(8,128)(2,1)S(1)} %get-tuple-element.34.picture_ref, bf16[2,32,512]{2,1,0:T(8,128)(2,1)S(1)} %collective-permute-done.4.near_ref, ...), custom_call_target="tpu_custom_call" | custom-call | tf_op jit(solution)/shard_map/step/pallas_call | solution.py:408
  66.5 8.6 %all_to_all.46 = bf16[8,64,128]{2,1,0:T(8,128)(2,1)S(1)} all-to-all(bf16[8,64,128]{2,1,0:T(8,128)(2,1)S(1)} %bitcast.17), channel_id=1, replica_groups=mesh['exp'=8,'sub'=4] {'exp'}, dimensions={0} | all-to-all | bytes 262144 | tf_op jit(solution)/shard_map/all_to_all | solution.py:339
  75.1 0.6 update.3
  (2 shorter events, 0.0 us)
Async XLA Ops:
  0.6 11.7 %copy-start.1 = (s32[2,16,4,1]{1,3,2,0:T(1,128)S(1)}, s32[2,16,4,1]{1,3,2,0:T(1,128)}, u32[]{:S(2)}) copy-start(s32[2,16,4,1]{1,3,2,0:T(1,128)} %param.12) | copy-start | bytes 1540
  0.6 11.7 %copy-start = (s32[2,16,4]{1,2,0:T(4,128)S(1)}, s32[2,16,4]{1,2,0:T(4,128)}, u32[]{:S(2)}) copy-start(s32[2,16,4]{1,2,0:T(4,128)} %param.13) | copy-start | bytes 1540
  2.1 23.0 %collective-permute-start.2 = (bf16[2,15,16,512]{3,2,1,0:T(8,128)(2,1)S(1)}, bf16[2,15,16,512]{3,2,1,0:T(8,128)(2,1)S(1)}, u32[]{:S(2)}, u32[]{:S(2)}) collective-permute-start(bf16[2,15,16,512]{3,2,1,0:T(8,128)(2,1)S(1)} %get-tuple-element.30), channel_id=1, source_target_pairs={{0,1},{2,3},{1,0},{3,2},{4,5},{6,7},{5,4},{7,6},{8,9},{10,11},{9,8... | collective-permute-start | bytes 1474568 | tf_op jit(solution)/shard_map/ppermute | solution.py:383
  2.3 22.9 %collective-permute-start.3 = (bf16[2,15,16,512]{3,2,1,0:T(8,128)(2,1)S(1)}, bf16[2,15,16,512]{3,2,1,0:T(8,128)(2,1)S(1)}, u32[]{:S(2)}, u32[]{:S(2)}) collective-permute-start(bf16[2,15,16,512]{3,2,1,0:T(8,128)(2,1)S(1)} %get-tuple-element.31), channel_id=1, source_target_pairs={{1,2},{2,1},{5,6},{6,5},{9,10},{10,9},{13,14},{14,13},{17,18},{18,... | collective-permute-start | bytes 1474568 | tf_op jit(solution)/shard_map/ppermute | solution.py:382
  6.8 11.7 %all-to-all-start = ((bf16[8,64,128]{2,1,0:T(8,128)(2,1)}), bf16[8,64,128]{2,1,0:T(8,128)(2,1)S(1)}, u32[]{:S(2)}, u32[]{:S(2)}) async-start(bf16[8,64,128]{2,1,0:T(8,128)(2,1)} %bitcast.3), calls=%async_computation | async-start | bytes 262144 | tf_op jit(solution)/shard_map/all_to_all | solution.py:339
  19.2 4.0 %collective-permute-start = (bf16[2,32,512]{2,1,0:T(8,128)(2,1)S(1)}, bf16[2,32,512]{2,1,0:T(8,128)(2,1)S(1)}, u32[]{:S(2)}, u32[]{:S(2)}) collective-permute-start(bf16[2,32,512]{2,1,0:T(8,128)(2,1)S(1)} %get-tuple-element.26), channel_id=1, source_target_pairs={{0,1},{2,3},{1,0},{3,2},{4,5},{6,7},{5,4},{7,6},{8,9},{10,11},{9,8... | collective-permute-start | bytes 196616 | tf_op jit(solution)/shard_map/ppermute | solution.py:403
  19.3 5.9 %collective-permute-start.1 = (bf16[2,32,512]{2,1,0:T(8,128)(2,1)S(1)}, bf16[2,32,512]{2,1,0:T(8,128)(2,1)S(1)}, u32[]{:S(2)}, u32[]{:S(2)}) collective-permute-start(bf16[2,32,512]{2,1,0:T(8,128)(2,1)S(1)} %get-tuple-element.27), channel_id=1, source_target_pairs={{1,2},{2,1},{5,6},{6,5},{9,10},{10,9},{13,14},{14,13},{17,18},{18,... | collective-permute-start | bytes 196616 | tf_op jit(solution)/shard_map/ppermute | solution.py:402
  50.9 6.2 %collective-permute-start.4 = (bf16[2,32,512]{2,1,0:T(8,128)(2,1)S(1)}, bf16[2,32,512]{2,1,0:T(8,128)(2,1)S(1)}, u32[]{:S(2)}, u32[]{:S(2)}) collective-permute-start(bf16[2,32,512]{2,1,0:T(8,128)(2,1)S(1)} %get-tuple-element.35), channel_id=1, source_target_pairs={{0,1},{2,3},{1,0},{3,2},{4,5},{6,7},{5,4},{7,6},{8,9},{10,11},{9,8... | collective-permute-start | bytes 196616 | tf_op jit(solution)/shard_map/ppermute | solution.py:403
  51.0 7.9 %collective-permute-start.5 = (bf16[2,32,512]{2,1,0:T(8,128)(2,1)S(1)}, bf16[2,32,512]{2,1,0:T(8,128)(2,1)S(1)}, u32[]{:S(2)}, u32[]{:S(2)}) collective-permute-start(bf16[2,32,512]{2,1,0:T(8,128)(2,1)S(1)} %get-tuple-element.36), channel_id=1, source_target_pairs={{1,2},{2,1},{5,6},{6,5},{9,10},{10,9},{13,14},{14,13},{17,18},{18,... | collective-permute-start | bytes 196616 | tf_op jit(solution)/shard_map/ppermute | solution.py:402

commit v6 on v5

--- a/solution.py
+++ b/solution.py
@@ -155,34 +155,102 @@
     return jnp.concatenate([across] * (-(-rows // LANES)), axis=0)[:rows]
 
 
-def step_kernel(
-    even_ref, ids_ref, picture_ref, near_ref, far_ref, counted_ref, taps_ref, coeffs_any, rims_near_any,
-    rims_far_any, observed_any, *refs, patch, per_tile, slot, taps, with_clipped,
+def build_side(side_ref, taps_ref, modes, tall, shift, taps):
+    height = side_ref.shape[0]
+    total = modes * tall
+    for low in range(0, total, LANES):
+        high = min(low + LANES, total)
+        parts = None
+        for mode in range(low // tall, (high - 1) // tall + 1):
+            back = low + taps - 1 - shift - mode * tall
+            ring = tiled(ring_of(taps_ref[2, mode : mode + 1], back), height, LANES)
+            place = lax.broadcasted_iota(jnp.int32, (height, LANES), 1) + (low - mode * tall)
+            ring = jnp.where((place >= 0) & (place < tall), ring * within(lags(height, LANES, back), taps), 0.0)
+            parts = ring if parts is None else parts + ring
+        side_ref[:, low:high] = parts[:, : high - low].astype(BF16)
+
+
+def smooth(images, vertical_ref, field_ref, taps_ref, modes, skew, taps, width):
+    tall, reach = vertical_ref.shape[0] // modes, vertical_ref.shape[1]
+    inside = within(lags(tall, reach, skew), taps)
+    for mode in range(modes):
+        ring = ring_of(taps_ref[0, mode : mode + 1], skew)
+        vertical_ref[mode * tall : (mode + 1) * tall, :] = (tiled(ring, tall, reach) * inside).astype(BF16)
+    chunk = divisor(modes, 4) * tall
+    for start in range(0, modes * tall, chunk):
+        table = vertical_ref[start : start + chunk, :]
+        for block, image in enumerate(images):
+            for low in range(0, image.shape[1], width):
+                field_ref[block, start : start + chunk, low : low + width] = jnp.dot(
+                    table, image[:, low : low + width], preferred_element_type=F32
+                ).astype(BF16)
+
+
+def blur(blocks, table, side, stride):
+    tall, width = blocks[0].shape[0], table.shape[0]
+    cuts = [cut for block in blocks for cut in windows_of(block, width, stride)]
+    result = lax.dot_general(
+        jnp.concatenate(cuts, axis=0), table, (((1,), (side,)), ((), ())), preferred_element_type=F32
+    )
+    per = len(cuts) // len(blocks)
+    outs = [result[k * tall : (k + 1) * tall] for k in range(len(cuts))]
+    return [joined(outs[k * per : (k + 1) * per], width, stride) for k in range(len(blocks))]
+
+
+def model_all(field_ref, model_ref, weights, across_of, modes, stride):
+    tall = model_ref.shape[1]
+    count = model_ref.shape[0]
+    for mode in range(modes):
+        start = mode * tall
+        blocks = [field_ref[block, start : start + tall, :] for block in range(count)]
+        for block, columns in enumerate(blur(blocks, across_of(mode), 1, stride)):
+            weight = weights(block, mode).astype(F32)
+            for k, column in enumerate(columns):
+                place = slice(k * stride, (k + 1) * stride)
+                if mode == 0:
+                    model_ref[block, :, place] = weight[:, place] * column
+                else:
+                    model_ref[block, :, place] += weight[:, place] * column
+
+
+def adjoint_all(field_ref, model_ref, weights, across_ref, modes, stride):
+    tall = model_ref.shape[1]
+    count = model_ref.shape[0]
+    for mode in range(modes):
+        start = mode * tall
+        blocks = [(weights(block, mode).astype(F32) * model_ref[block]).astype(BF16) for block in range(count)]
+        for block, columns in enumerate(blur(blocks, across_ref[mode], 0, stride)):
+            for k, column in enumerate(columns):
+                field_ref[block, start : start + tall, k * stride : (k + 1) * stride] = column.astype(BF16)
+
+
+def inner_kernel(
+    even_ref, picture_ref, taps_ref, coeffs_any, observed_any, rims_near_any, rims_far_any, gradient_ref, across_ref,
+    edge_coeffs_ref, edge_seen_ref, *refs, patch, taps, with_clipped,
 ):
     refs = list(refs)
     clipped_ref = refs.pop(0) if with_clipped else None
-    (
-        sums_ref, image_ref, field_ref, model_ref, gradient_ref, coeffs_ref, seen_ref, seen_rims_ref,
-        vertical_ref, side_ref, across_ref, band_ref, sems, *totals,
-    ) = refs
+    field_ref, model_ref, coeffs_ref, seen_ref, seen_rims_ref, vertical_ref, side_ref, band_ref, sems = refs
     pieces, height, breadth = picture_ref.shape
     modes = coeffs_ref.shape[1]
-    rim = near_ref.shape[1]
     tall = coeffs_ref.shape[2]
-    ext = (tall - height) // 2
+    ext = (height - tall) // 2
     margin = (taps - 1) // 2
-    patch_rows, patch_cols = patch
+    stride = patch[1]
     width = across_ref.shape[1]
-    stride = patch_cols
     even = even_ref[0]
-    near_at = pl.multiple_of(even * (ext + height), ROWS)
-    far_at = pl.multiple_of((1 - even) * (ext + height), ROWS)
+    near_row = pl.multiple_of(even * ext, ROWS)
+    far_row = pl.multiple_of((1 - even) * ext, ROWS)
 
     moves = [
-        (coeffs_any, coeffs_ref.at[:, :, pl.ds(ext, height), :]),
-        (rims_near_any.at[:, pl.ds(0, modes)], coeffs_ref.at[:, :, pl.ds(near_at, ext), :]),
-        (rims_far_any.at[:, pl.ds(0, modes)], coeffs_ref.at[:, :, pl.ds(far_at, ext), :]),
-        (observed_any, seen_ref.at[:, pl.ds(ext, height), :]),
+        (coeffs_any.at[:, :, pl.ds(ext, tall), :], coeffs_ref),
+        (observed_any.at[:, pl.ds(ext, tall), :], seen_ref),
+        (coeffs_any.at[:, :, pl.ds(0, ext), :], edge_coeffs_ref.at[0, :, :, pl.ds(ext, ext), :]),
+        (coeffs_any.at[:, :, pl.ds(height - ext, ext), :], edge_coeffs_ref.at[1, :, :, pl.ds(0, ext), :]),
+        (rims_near_any.at[:, pl.ds(0, modes)], edge_coeffs_ref.at[even, :, :, pl.ds(near_row, ext), :]),
+        (rims_far_any.at[:, pl.ds(0, modes)], edge_coeffs_ref.at[1 - even, :, :, pl.ds(far_row, ext), :]),
+        (observed_any.at[:, pl.ds(0, ext), :], edge_seen_ref.at[0, :, pl.ds(ext, ext), :]),
+        (observed_any.at[:, pl.ds(height - ext, ext), :], edge_seen_ref.at[1, :, pl.ds(0, ext), :]),
         (rims_near_any.at[:, pl.ds(modes, PARTS)], seen_rims_ref.at[0]),
         (rims_far_any.at[:, pl.ds(modes, PARTS)], seen_rims_ref.at[1]),
     ]
@@ -190,84 +258,91 @@
     for copy in copies:
         copy.start()
 
-    image_ref[:, rim : rim + height, :] = picture_ref[...]
-    image_ref[:, pl.ds(pl.multiple_of(even * (rim + height), ROWS), rim), :] = near_ref[...]
-    image_ref[:, pl.ds(pl.multiple_of((1 - even) * (rim + height), ROWS), rim), :] = far_ref[...]
-
-    reach = vertical_ref.shape[1]
     band_ref[...] = within(lags(width, width, margin), taps)
-    skew = margin + ext - rim
-    inside = within(lags(tall, reach, skew), taps)
-    for mode in range(modes):
-        ring = ring_of(taps_ref[0, mode : mode + 1], skew)
-        vertical_ref[mode * tall : (mode + 1) * tall, :] = (tiled(ring, tall, reach) * inside).astype(BF16)
-
-    group = divisor(modes, 4)
-    chunk = group * tall
-    for start in range(0, modes * tall, chunk):
-        table = vertical_ref[start : start + chunk, :]
-        for piece in range(pieces):
-            for low in range(0, breadth, width):
-                field_ref[piece, start : start + chunk, low : low + width] = jnp.dot(
-                    table, image_ref[piece, :, low : low + width], preferred_element_type=F32
-                ).astype(BF16)
-
-    def blur(blocks, table, side):
-        cuts = [cut for block in blocks for cut in windows_of(block, width, stride)]
-        result = lax.dot_general(
-            jnp.concatenate(cuts, axis=0), table, (((1,), (side,)), ((), ())), preferred_element_type=F32
-        )
-        per = len(cuts) // len(blocks)
-        outs = [result[k * tall : (k + 1) * tall] for k in range(len(cuts))]
-        return [joined(outs[k * per : (k + 1) * per], width, stride) for k in range(len(blocks))]
-
-    for k in range(3):
-        copies[k].wait()
-    for mode in range(modes):
-        start = mode * tall
-        across_ref[mode] = (tiled(ring_of(taps_ref[1, mode : mode + 1], margin), width, width) * band_ref[...]).astype(BF16)
-        blocks = [field_ref[piece, start : start + tall, :] for piece in range(pieces)]
-        for piece, columns in enumerate(blur(blocks, across_ref[mode], 1)):
-            weight = coeffs_ref[piece, mode].astype(F32)
-            for k, column in enumerate(columns):
-                place = slice(k * stride, (k + 1) * stride)
-                if mode == 0:
-                    model_ref[piece, :, place] = weight[:, place] * column
-                else:
-                    model_ref[piece, :, place] += weight[:, place] * column
-    for k in range(3, 6):
-        copies[k].wait()
-    for side, start in enumerate((near_at, far_at)):
-        total = seen_rims_ref[side, :, 0].astype(F32)
-        for part in range(1, PARTS):
-            total = total + seen_rims_ref[side, :, part].astype(F32)
-        seen_ref[:, pl.ds(start, ext), :] = total
+    images = [picture_ref.at[piece] for piece in range(pieces)]
+    smooth(images, vertical_ref, field_ref, taps_ref, modes, margin - ext, taps, width)
+
+    def across_of(mode):
+        ring = tiled(ring_of(taps_ref[1, mode : mode + 1], margin), width, width)
+        across_ref[mode] = (ring * band_ref[...]).astype(BF16)
+        return across_ref[mode]
+
+    def weights(block, mode):
+        return coeffs_ref[block, mode]
+
+    copies[0].wait()
+    copies[1].wait()
+    model_all(field_ref, model_ref, weights, across_of, modes, stride)
     model_ref[...] = jnp.clip(model_ref[...] - seen_ref[...], -DELTA, DELTA)
     if with_clipped:
-        clipped_ref[...] = model_ref[:, ext : ext + height, :]
-
-    total = modes * tall
-    for low in range(0, total, LANES):
-        high = min(low + LANES, total)
-        parts = None
-        for mode in range(low // tall, (high - 1) // tall + 1):
-            back = taps - 1 - (ext + margin) - mode * tall
-            lag = lags(height, LANES, low + back)
-            ring = tiled(ring_of(taps_ref[2, mode : mode + 1], low + back), height, LANES) * within(lag, taps)
-            parts = ring if parts is None else parts + ring
-        side_ref[:, low:high] = parts[:, : high - low].astype(BF16)
-
-    for mode in range(modes):
-        start = mode * tall
-        blocks = [(coeffs_ref[piece, mode].astype(F32) * model_ref[piece]).astype(BF16) for piece in range(pieces)]
-        for piece, columns in enumerate(blur(blocks, across_ref[mode], 0)):
-            for k, column in enumerate(columns):
-                field_ref[piece, start : start + tall, k * stride : (k + 1) * stride] = column.astype(BF16)
+        clipped_ref[...] = model_ref[...]
+    build_side(side_ref, taps_ref, modes, tall, margin - ext, taps)
+    adjoint_all(field_ref, model_ref, weights, across_ref, modes, stride)
     for piece in range(pieces):
         for low in range(0, breadth, width):
             gradient_ref[piece, :, low : low + width] = jnp.dot(
                 side_ref[...], field_ref[piece, :, low : low + width], preferred_element_type=F32
             )
+    for copy in copies[2:]:
+        copy.wait()
+    for rim, end, row in ((0, even, near_row), (1, 1 - even, far_row)):
+        total = seen_rims_ref[rim, :, 0].astype(F32)
+        for part in range(1, PARTS):
+            total = total + seen_rims_ref[rim, :, part].astype(F32)
+        edge_seen_ref[end, :, pl.ds(row, ext), :] = total
+
+
+def outer_kernel(
+    even_ref, ids_ref, picture_ref, near_ref, far_ref, counted_ref, taps_ref, gradient_ref, across_ref,
+    edge_coeffs_ref, edge_seen_ref, *refs, patch, per_tile, slot, taps, with_clipped,
+):
+    refs = list(refs)
+    if with_clipped:
+        inner_ref, clipped_ref = refs[:2]
+        refs = refs[2:]
+    sums_ref, image_ref, field_ref, model_ref, edge_ref, vertical_ref, upper_ref, lower_ref, *totals = refs
+    pieces, height, breadth = picture_ref.shape
+    modes, tall = edge_coeffs_ref.shape[2:4]
+    rim = near_ref.shape[1]
+    ext = tall // 2
+    margin = (taps - 1) // 2
+    patch_rows, patch_cols = patch
+    stride = patch_cols
+    width = across_ref.shape[1]
+    even = even_ref[0]
+    near_row = pl.multiple_of(even * rim, ROWS)
+    far_row = pl.multiple_of((1 - even) * rim, ROWS)
+
+    image_ref[0, :, rim:, :] = picture_ref[:, :rim, :]
+    image_ref[1, :, :rim, :] = picture_ref[:, height - rim :, :]
+    image_ref[even, :, pl.ds(near_row, rim), :] = near_ref[...]
+    image_ref[1 - even, :, pl.ds(far_row, rim), :] = far_ref[...]
+    places = [(end, piece) for end in (0, 1) for piece in range(pieces)]
+    images = [image_ref.at[end, piece] for end, piece in places]
+    smooth(images, vertical_ref, field_ref, taps_ref, modes, margin + ext - rim, taps, width)
+
+    def weights(block, mode):
+        end, piece = places[block]
+        return edge_coeffs_ref[end, piece, mode]
+
+    model_all(field_ref, model_ref, weights, lambda mode: across_ref[mode], modes, stride)
+    for block, (end, piece) in enumerate(places):
+        model_ref[block] = jnp.clip(model_ref[block] - edge_seen_ref[end, piece], -DELTA, DELTA)
+    if with_clipped:
+        for piece in range(pieces):
+            clipped_ref[piece, :ext, :] = model_ref[piece, ext:, :]
+            clipped_ref[piece, ext : height - ext, :] = inner_ref[piece]
+            clipped_ref[piece, height - ext :, :] = model_ref[pieces + piece, :ext, :]
+    build_side(upper_ref, taps_ref, modes, tall, margin + ext, taps)
+    build_side(lower_ref, taps_ref, modes, tall, margin + ext - rim, taps)
+    adjoint_all(field_ref, model_ref, weights, across_ref, modes, stride)
+    for block, (end, piece) in enumerate(places):
+        side = (upper_ref, lower_ref)[end][...]
+        for low in range(0, breadth, width):
+            edge_ref[end, piece, :, low : low + width] = jnp.dot(
+                side, field_ref[block, :, low : low + width], preferred_element_type=F32
+            )
+
     held = per_tile * patch_rows
     for total_ref in totals:
         total_ref[...] = jnp.zeros(total_ref.shape, F32)
@@ -275,13 +350,19 @@
     rows = height // patch_rows
     turn = 0
     for row in range(rows):
+        top = row * patch_rows
         for col in range(cols):
+            across = slice(col * patch_cols, (col + 1) * patch_cols)
             for piece in range(pieces):
                 index = ids_ref[(piece * rows + row) * cols + col]
                 place = pl.ds(pl.multiple_of(index * patch_rows, patch_rows), patch_rows)
-                totals[turn % len(totals)][place, :] += gradient_ref[
-                    piece, row * patch_rows : (row + 1) * patch_rows, col * patch_cols : (col + 1) * patch_cols
-                ]
+                value = gradient_ref[piece, top : top + patch_rows, across]
+                if top < rim:
+                    value = value + edge_ref[0, piece, top : top + patch_rows, across]
+                if top >= height - rim:
+                    start = top - (height - rim)
+                    value = value + edge_ref[1, piece, start : start + patch_rows, across]
+                totals[turn % len(totals)][place, :] += value
                 turn += 1
     for owner in range(sums_ref.shape[0] // slot):
         place = slice(owner * held, (owner + 1) * held)
@@ -328,7 +409,6 @@
     known = exp_count * held
     ext = round_up(margin, ROWS)
     rim = round_up(ext + margin, ROWS)
-    tall = height + 2 * ext
     width = min(breadth, 2 * patch_cols)
     routes = pair_routes("sub")
     vmem = pl.BlockSpec(memory_space=pltpu.VMEM)
@@ -402,34 +482,58 @@
         far = lax.ppermute(far, "sub", routes[1])
         near = lax.ppermute(near, "sub", routes[0])
         slot = held + (round_up(per_tile, ROWS) if first else 0)
+        inner = height - 2 * ext
+        taken = vert_taps.shape[1]
+        results = [
+            pltpu.VMEM((pieces, height, breadth), F32),
+            pltpu.VMEM((modes, width, width), BF16),
+            pltpu.VMEM((2, pieces, modes, 2 * ext, breadth), BF16),
+            pltpu.VMEM((2, pieces, 2 * ext, breadth), F32),
+        ]
+        if last:
+            results.append(pltpu.VMEM((pieces, inner, breadth), F32))
+        middle = pl.pallas_call(
+            functools.partial(inner_kernel, patch=patch, taps=taken, with_clipped=last),
+            out_shape=tuple(results),
+            in_specs=[smem, vmem, vmem] + [somewhere] * 4,
+            out_specs=(vmem,) * len(results),
+            scratch_shapes=[
+                pltpu.VMEM((pieces, modes * inner, breadth), BF16),
+                pltpu.VMEM((pieces, inner, breadth), F32),
+                pltpu.VMEM((pieces, modes, inner, breadth), BF16),
+                pltpu.VMEM((pieces, inner, breadth), F32),
+                pltpu.VMEM((2, pieces, PARTS, ext, breadth), BF16),
+                pltpu.VMEM((modes * inner, height), BF16),
+                pltpu.VMEM((height, modes * inner), BF16),
+                pltpu.VMEM((width, width), F32),
+                pltpu.SemaphoreType.DMA((10,)),
+            ],
+            compiler_params=pltpu.CompilerParams(vmem_limit_bytes=16 << 20),
+            cost_estimate=pl.CostEstimate(flops=3 * 10**9, bytes_accessed=5 * 10**6, transcendentals=0),
+            name="inner",
+        )(even, picture, taps, coeffs, observed, rims_near, rims_far)
         results = [jax.ShapeDtypeStruct((exp_count * slot, patch_cols), BF16)]
         if last:
             results.insert(0, jax.ShapeDtypeStruct((pieces, height, breadth), F32))
+        held_here = [pltpu.with_memory_space_constraint(array, pltpu.VMEM) for array in middle]
         answer = pl.pallas_call(
-            functools.partial(
-                step_kernel, patch=patch, per_tile=per_tile, slot=slot, taps=vert_taps.shape[1], with_clipped=last
-            ),
+            functools.partial(outer_kernel, patch=patch, per_tile=per_tile, slot=slot, taps=taken, with_clipped=last),
             out_shape=tuple(results),
-            in_specs=[smem] * 2 + [vmem] * 5 + [somewhere] * 4,
+            in_specs=[smem] * 2 + [vmem] * (5 + len(middle)),
             out_specs=(vmem,) * len(results),
             scratch_shapes=[
-                pltpu.VMEM((pieces, height + 2 * rim, breadth), BF16),
-                pltpu.VMEM((pieces, modes * tall, breadth), BF16),
-                pltpu.VMEM((pieces, tall, breadth), F32),
-                pltpu.VMEM((pieces, height, breadth), F32),
-                pltpu.VMEM((pieces, modes, tall, breadth), BF16),
-                pltpu.VMEM((pieces, tall, breadth), F32),
-                pltpu.VMEM((2, pieces, PARTS, ext, breadth), BF16),
-                pltpu.VMEM((modes * tall, height + 2 * rim), BF16),
-                pltpu.VMEM((height, modes * tall), BF16),
-                pltpu.VMEM((modes, width, width), BF16),
-                pltpu.VMEM((width, width), F32),
-                pltpu.SemaphoreType.DMA((6,)),
+                pltpu.VMEM((2, pieces, 2 * rim, breadth), BF16),
+                pltpu.VMEM((2 * pieces, modes * 2 * ext, breadth), BF16),
+                pltpu.VMEM((2 * pieces, 2 * ext, breadth), F32),
+                pltpu.VMEM((2, pieces, rim, breadth), F32),
+                pltpu.VMEM((modes * 2 * ext, 2 * rim), BF16),
+                pltpu.VMEM((rim, modes * 2 * ext), BF16),
+                pltpu.VMEM((rim, modes * 2 * ext), BF16),
             ]
             + [pltpu.VMEM((known, patch_cols), F32)] * 4,
-            compiler_params=pltpu.CompilerParams(vmem_limit_bytes=24 << 20),
-            name="step",
-        )(even, ids, picture, near, far, counted, taps, coeffs, rims_near, rims_far, observed)
+            compiler_params=pltpu.CompilerParams(vmem_limit_bytes=12 << 20),
+            name="outer",
+        )(even, ids, picture, near, far, counted, taps, *held_here)
         sums = answer[-1]
         if last:
             clipped = answer[0]

time: 76.4 us -> 72.3 us (0.946)
  waiting for transfers between devices: 8.24 us -> 4.58 us
  starting transfers between devices: 20.3 us -> 18.6 us
  Pallas kernels: 20.1 us -> 21.6 us
    ppermute x2, waiting for transfers between devices: 3.67 us -> 0.01 us  [per_device(): far = lax.ppermute(far, 'sub', routes[1])]
    ppermute x2, starting transfers between devices: 10.1 us -> 8.33 us  [per_device(): far = lax.ppermute(far, 'sub', routes[1])]
    pallas_call x2 -> x4, Pallas kernels: 14.5 us -> 15.9 us  [the longest x2 9.13 us: per_device(): pl.pallas_call(functools.partial(inner_kernel, patch=patch, taps=taken, w...]
  transfers between devices with their start and end apart: 7 -> 7, of which waited for: 3 -> 1; matrix products, arithmetic and copies ran while one was open for 0% -> 0% of each run, Pallas kernels for 3% -> 16%
where the time goes in v6:
time: 72.3 us; the launch traced here: 71.8 us
  blocking collectives  26 us (36%)
  Pallas kernels  21.6 us (30%)
  starting transfers between devices  18.6 us (26%)
  waiting for transfers between devices  4.58 us (6%)
  between operations  0.83 us (1%)
    all_to_all x3, blocking collectives, exchange(): return lax.all_to_all(block, 'exp', split_axis=0, concat_axis=0, tiled=True)  26 us
    pallas_call x2, Pallas kernels, per_device(): pl.pallas_call(functools.partial(inner_kernel, patch=patch, taps=taken, w...  9.13 us
    ppermute x2, starting transfers between devices, per_device(): far = lax.ppermute(far, 'sub', routes[1])  8.33 us
    pallas_call x2, Pallas kernels, per_device(): pl.pallas_call(functools.partial(outer_kernel, patch=patch, per_tile=per_...  6.81 us
    all_to_all x1, starting transfers between devices, exchange(): return lax.all_to_all(block, 'exp', split_axis=0, concat_axis=0, tiled=True)  5.54 us
    all_to_all x1, waiting for transfers between devices, exchange(): return lax.all_to_all(block, 'exp', split_axis=0, concat_axis=0, tiled=True)  4.56 us
    ppermute x1, starting transfers between devices, per_device(): rims_far = lax.ppermute(rims_far, 'sub', routes[1])  4.49 us
    pallas_call x1, Pallas kernels, per_device(): pl.pallas_call(begin_kernel, out_shape=(jax.ShapeDtypeStruct((known, patc...  1.49 us
  transfers between devices with their start and end apart: 7, of which 1 were waited for; matrix products, arithmetic and copies ran while one was open for 0% of the time, Pallas kernels for 16%

profile of v6, /device:TPU:1, one launch (start us, length us, event | category | flops | bytes accessed | tf_op | source)
XLA Modules:
  0.0 71.8 jit_solution(13569313471727750560)
XLA Ops:
  0.6 0.0 copy-start.1
  0.7 0.0 copy-start
  0.7 1.5 %begin.1 = (bf16[512,128]{1,0:T(8,128)(2,1)}, bf16[2,15,16,512]{3,2,1,0:T(8,128)(2,1)S(1)}, bf16[2,15,16,512]{3,2,1,0:T(8,128)(2,1)S(1)}) custom-call(s32[1]{0:T(128)} %bitcast.1.even_ref, f32[64,128]{1,0:T(8,128)} %bitcast.19, bf16[2,12,128,512]{3,2,1,0:T(8,128)(2,1)} %coeffs_any.3, f32[2,128,512]{2,1,0:T(8,128)} %observed_any.3), custom_call_target="tpu_custom_call" | custom-call | tf_op jit(solution)/shard_map/begin/pallas_call | solution.py:426
  2.2 0.1 collective-permute-start.2
  2.3 4.5 %collective-permute-start.3 = (bf16[2,15,16,512]{3,2,1,0:T(8,128)(2,1)S(1)}, bf16[2,15,16,512]{3,2,1,0:T(8,128)(2,1)S(1)}, u32[]{:S(2)}, u32[]{:S(2)}) collective-permute-start(bf16[2,15,16,512]{3,2,1,0:T(8,128)(2,1)S(1)} %get-tuple-element.40), channel_id=1, source_target_pairs={{1,2},{2,1},{5,6},{6,5},{9,10},{10,9},{13,14},{14,13},{17,18},{18,... | collective-permute-start | bytes 1474568 | tf_op jit(solution)/shard_map/ppermute | solution.py:462
  6.8 5.5 %all-to-all-start = ((bf16[8,64,128]{2,1,0:T(8,128)(2,1)}), bf16[8,64,128]{2,1,0:T(8,128)(2,1)S(1)}, u32[]{:S(2)}, u32[]{:S(2)}) async-start(bf16[8,64,128]{2,1,0:T(8,128)(2,1)} %bitcast.3), calls=%async_computation | async-start | bytes 262144 | tf_op jit(solution)/shard_map/all_to_all | solution.py:419
  12.3 0.0 copy-done.1
  12.3 0.0 copy-done
  12.4 0.1 copy.10
  12.4 0.1 reshape.29.ids_ref
  12.6 1.4 %prep.1 = (f32[64,128]{1,0:T(8,128)S(1)}, f32[3,16,128]{2,1,0:T(8,128)S(1)}) custom-call(s32[128]{0:T(128)S(1)} %reshape.29.ids_ref, bf16[12,21]{1,0:T(8,128)(2,1)} %vert_any.1, bf16[12,21]{1,0:T(8,128)(2,1)} %horiz_any.1), custom_call_target="tpu_custom_call" | custom-call | tf_op jit(solution)/shard_map/prep/pallas_call | solution.py:442
  14.0 4.6 %all-to-all-done = bf16[8,64,128]{2,1,0:T(8,128)(2,1)S(1)} async-done(((bf16[8,64,128]{2,1,0:T(8,128)(2,1)}), bf16[8,64,128]{2,1,0:T(8,128)(2,1)S(1)}, u32[]{:S(2)}, u32[]{:S(2)}) %all-to-all-start) | async-done | bytes 131104 | tf_op jit(solution)/shard_map/all_to_all | solution.py:419
  18.5 0.7 picture.2
  19.2 0.1 collective-permute-start
  19.3 3.9 %collective-permute-start.1 = (bf16[2,32,512]{2,1,0:T(8,128)(2,1)S(1)}, bf16[2,32,512]{2,1,0:T(8,128)(2,1)S(1)}, u32[]{:S(2)}, u32[]{:S(2)}) collective-permute-start(bf16[2,32,512]{2,1,0:T(8,128)(2,1)S(1)} %get-tuple-element.36), channel_id=1, source_target_pairs={{1,2},{2,1},{5,6},{6,5},{9,10},{10,9},{13,14},{14,13},{17,18},{18,... | collective-permute-start | bytes 196616 | tf_op jit(solution)/shard_map/ppermute | solution.py:482
  23.2 0.0 collective-permute-done.2.rims_near_any
  23.2 0.0 collective-permute-done.3.rims_far_any
  23.2 4.5 %inner.2 = (f32[2,128,512]{2,1,0:T(8,128)S(1)}, bf16[12,256,256]{2,1,0:T(8,128)(2,1)S(1)}, bf16[2,2,12,32,512]{4,3,2,1,0:T(8,128)(2,1)S(1)}, f32[2,2,32,512]{3,2,1,0:T(8,128)S(1)}) custom-call(s32[1]{0:T(128)} %bitcast.1.even_ref, bf16[2,128,512]{2,1,0:T(8,128)(2,1)S(1)} %get-tuple-element.34.picture_ref, f32[3,16,128]{2,1,0:T(8,128)S(1)} %get-tuple-element.38.taps_ref, ...), custom_call_target="tpu_custom_call" | custom-call | flops 3000000000 | bytes 5000000 | tf_op jit(solution)/shard_map/inner/pallas_call | solution.py:495
  27.8 0.0 collective-permute-done.near_ref
  27.8 0.0 collective-permute-done.1.far_ref
  27.8 3.0 %outer.2 = bf16[640,128]{1,0:T(8,128)(2,1)S(1)} custom-call(s32[1]{0:T(128)} %bitcast.1.even_ref, s32[128]{0:T(128)S(1)} %reshape.29.ids_ref, bf16[2,128,512]{2,1,0:T(8,128)(2,1)S(1)} %get-tuple-element.34.picture_ref, bf16[2,32,512]{2,1,0:T(8,128)(2,1)S(1)} %collective-permute-done.near_ref, bf16[2,32,512]{2,1,0:T(8,128)(2,1)S(1)} %collective-permute-done.1.far_ref, ...), custom_call_target="tpu_custom_call" | custom-call | tf_op jit(solution)/shard_map/outer/pallas_call | solution.py:519
  30.8 8.8 %all_to_all.44 = bf16[8,80,128]{2,1,0:T(8,128)(2,1)S(1)} all-to-all(bf16[8,80,128]{2,1,0:T(8,128)(2,1)S(1)} %bitcast.12), channel_id=1, replica_groups=mesh['exp'=8,'sub'=4] {'exp'}, dimensions={0} | all-to-all | bytes 327680 | tf_op jit(solution)/shard_map/all_to_all | solution.py:419
  39.7 0.8 %update.2 = (f32[64,128]{1,0:T(8,128)S(1)}, bf16[512,128]{1,0:T(8,128)(2,1)S(1)}, f32[64,128]{1,0:T(8,128)S(1)}) custom-call(f32[64,128]{1,0:T(8,128)} %bitcast.20, bf16[640,128]{1,0:T(8,128)(2,1)S(1)} %bitcast.13), custom_call_target="tpu_custom_call" | custom-call | tf_op jit(solution)/shard_map/update/pallas_call | solution.py:548
  40.5 8.6 %all_to_all.45 = bf16[8,64,128]{2,1,0:T(8,128)(2,1)S(1)} all-to-all(bf16[8,64,128]{2,1,0:T(8,128)(2,1)S(1)} %bitcast.18), channel_id=1, replica_groups=mesh['exp'=8,'sub'=4] {'exp'}, dimensions={0} | all-to-all | bytes 262144 | tf_op jit(solution)/shard_map/all_to_all | solution.py:419
  49.0 0.7 picture.3
  49.7 0.1 collective-permute-start.4
  49.8 4.4 %collective-permute-start.5 = (bf16[2,32,512]{2,1,0:T(8,128)(2,1)S(1)}, bf16[2,32,512]{2,1,0:T(8,128)(2,1)S(1)}, u32[]{:S(2)}, u32[]{:S(2)}) collective-permute-start(bf16[2,32,512]{2,1,0:T(8,128)(2,1)S(1)} %get-tuple-element.49), channel_id=1, source_target_pairs={{1,2},{2,1},{5,6},{6,5},{9,10},{10,9},{13,14},{14,13},{17,18},{18,... | collective-permute-start | bytes 196616 | tf_op jit(solution)/shard_map/ppermute | solution.py:482
  54.2 4.6 %inner.3 = (f32[2,128,512]{2,1,0:T(8,128)S(1)}, bf16[12,256,256]{2,1,0:T(8,128)(2,1)S(1)}, bf16[2,2,12,32,512]{4,3,2,1,0:T(8,128)(2,1)S(1)}, f32[2,2,32,512]{3,2,1,0:T(8,128)S(1)}, f32[2,96,512]{2,1,0:T(8,128)S(1)}) custom-call(s32[1]{0:T(128)} %bitcast.1.even_ref, bf16[2,128,512]{2,1,0:T(8,128)(2,1)S(1)} %get-tuple-element.47.picture_ref, ...), custom_call_target="tpu_custom_call" | custom-call | flops 3000000000 | bytes 5000000 | tf_op jit(solution)/shard_map/inner/pallas_call | solution.py:495
  58.8 0.0 collective-permute-done.4.near_ref
  58.8 0.0 collective-permute-done.5.far_ref
  58.8 3.8 %outer.3 = (f32[2,128,512]{2,1,0:T(8,128)}, bf16[512,128]{1,0:T(8,128)(2,1)S(1)}) custom-call(s32[1]{0:T(128)} %bitcast.1.even_ref, s32[128]{0:T(128)S(1)} %reshape.29.ids_ref, bf16[2,128,512]{2,1,0:T(8,128)(2,1)S(1)} %get-tuple-element.47.picture_ref, bf16[2,32,512]{2,1,0:T(8,128)(2,1)S(1)} %collective-permute-done.4.near_ref, ...), custom_call_target="tpu_custom_call" | custom-call | tf_op jit(solution)/shard_map/outer/pallas_call | solution.py:519
  62.6 8.6 %all_to_all.46 = bf16[8,64,128]{2,1,0:T(8,128)(2,1)S(1)} all-to-all(bf16[8,64,128]{2,1,0:T(8,128)(2,1)S(1)} %bitcast.17), channel_id=1, replica_groups=mesh['exp'=8,'sub'=4] {'exp'}, dimensions={0} | all-to-all | bytes 262144 | tf_op jit(solution)/shard_map/all_to_all | solution.py:419
  71.2 0.6 update.3
  (2 shorter events, 0.0 us)
Async XLA Ops:
  0.6 11.7 %copy-start.1 = (s32[2,16,4,1]{1,3,2,0:T(1,128)S(1)}, s32[2,16,4,1]{1,3,2,0:T(1,128)}, u32[]{:S(2)}) copy-start(s32[2,16,4,1]{1,3,2,0:T(1,128)} %param.12) | copy-start | bytes 1540
  0.7 11.7 %copy-start = (s32[2,16,4]{1,2,0:T(4,128)S(1)}, s32[2,16,4]{1,2,0:T(4,128)}, u32[]{:S(2)}) copy-start(s32[2,16,4]{1,2,0:T(4,128)} %param.13) | copy-start | bytes 1540
  2.2 21.1 %collective-permute-start.2 = (bf16[2,15,16,512]{3,2,1,0:T(8,128)(2,1)S(1)}, bf16[2,15,16,512]{3,2,1,0:T(8,128)(2,1)S(1)}, u32[]{:S(2)}, u32[]{:S(2)}) collective-permute-start(bf16[2,15,16,512]{3,2,1,0:T(8,128)(2,1)S(1)} %get-tuple-element.39), channel_id=1, source_target_pairs={{0,1},{2,3},{1,0},{3,2},{4,5},{6,7},{5,4},{7,6},{8,9},{10,11},{9,8... | collective-permute-start | bytes 1474568 | tf_op jit(solution)/shard_map/ppermute | solution.py:463
  2.3 20.9 %collective-permute-start.3 = (bf16[2,15,16,512]{3,2,1,0:T(8,128)(2,1)S(1)}, bf16[2,15,16,512]{3,2,1,0:T(8,128)(2,1)S(1)}, u32[]{:S(2)}, u32[]{:S(2)}) collective-permute-start(bf16[2,15,16,512]{3,2,1,0:T(8,128)(2,1)S(1)} %get-tuple-element.40), channel_id=1, source_target_pairs={{1,2},{2,1},{5,6},{6,5},{9,10},{10,9},{13,14},{14,13},{17,18},{18,... | collective-permute-start | bytes 1474568 | tf_op jit(solution)/shard_map/ppermute | solution.py:462
  6.8 11.7 %all-to-all-start = ((bf16[8,64,128]{2,1,0:T(8,128)(2,1)}), bf16[8,64,128]{2,1,0:T(8,128)(2,1)S(1)}, u32[]{:S(2)}, u32[]{:S(2)}) async-start(bf16[8,64,128]{2,1,0:T(8,128)(2,1)} %bitcast.3), calls=%async_computation | async-start | bytes 262144 | tf_op jit(solution)/shard_map/all_to_all | solution.py:419
  19.2 8.6 %collective-permute-start = (bf16[2,32,512]{2,1,0:T(8,128)(2,1)S(1)}, bf16[2,32,512]{2,1,0:T(8,128)(2,1)S(1)}, u32[]{:S(2)}, u32[]{:S(2)}) collective-permute-start(bf16[2,32,512]{2,1,0:T(8,128)(2,1)S(1)} %get-tuple-element.35), channel_id=1, source_target_pairs={{0,1},{2,3},{1,0},{3,2},{4,5},{6,7},{5,4},{7,6},{8,9},{10,11},{9,8... | collective-permute-start | bytes 196616 | tf_op jit(solution)/shard_map/ppermute | solution.py:483
  19.3 8.5 %collective-permute-start.1 = (bf16[2,32,512]{2,1,0:T(8,128)(2,1)S(1)}, bf16[2,32,512]{2,1,0:T(8,128)(2,1)S(1)}, u32[]{:S(2)}, u32[]{:S(2)}) collective-permute-start(bf16[2,32,512]{2,1,0:T(8,128)(2,1)S(1)} %get-tuple-element.36), channel_id=1, source_target_pairs={{1,2},{2,1},{5,6},{6,5},{9,10},{10,9},{13,14},{14,13},{17,18},{18,... | collective-permute-start | bytes 196616 | tf_op jit(solution)/shard_map/ppermute | solution.py:482
  49.7 9.1 %collective-permute-start.4 = (bf16[2,32,512]{2,1,0:T(8,128)(2,1)S(1)}, bf16[2,32,512]{2,1,0:T(8,128)(2,1)S(1)}, u32[]{:S(2)}, u32[]{:S(2)}) collective-permute-start(bf16[2,32,512]{2,1,0:T(8,128)(2,1)S(1)} %get-tuple-element.48), channel_id=1, source_target_pairs={{0,1},{2,3},{1,0},{3,2},{4,5},{6,7},{5,4},{7,6},{8,9},{10,11},{9,8... | collective-permute-start | bytes 196616 | tf_op jit(solution)/shard_map/ppermute | solution.py:483
  49.8 9.0 %collective-permute-start.5 = (bf16[2,32,512]{2,1,0:T(8,128)(2,1)S(1)}, bf16[2,32,512]{2,1,0:T(8,128)(2,1)S(1)}, u32[]{:S(2)}, u32[]{:S(2)}) collective-permute-start(bf16[2,32,512]{2,1,0:T(8,128)(2,1)S(1)} %get-tuple-element.49), channel_id=1, source_target_pairs={{1,2},{2,1},{5,6},{6,5},{9,10},{10,9},{13,14},{14,13},{17,18},{18,... | collective-permute-start | bytes 196616 | tf_op jit(solution)/shard_map/ppermute | solution.py:482

commit v7 on v6

--- a/solution.py
+++ b/solution.py
@@ -155,35 +155,36 @@
     return jnp.concatenate([across] * (-(-rows // LANES)), axis=0)[:rows]
 
 
-def build_side(side_ref, taps_ref, modes, tall, shift, taps):
-    height = side_ref.shape[0]
-    total = modes * tall
-    for low in range(0, total, LANES):
-        high = min(low + LANES, total)
-        parts = None
-        for mode in range(low // tall, (high - 1) // tall + 1):
-            back = low + taps - 1 - shift - mode * tall
-            ring = tiled(ring_of(taps_ref[2, mode : mode + 1], back), height, LANES)
-            place = lax.broadcasted_iota(jnp.int32, (height, LANES), 1) + (low - mode * tall)
-            ring = jnp.where((place >= 0) & (place < tall), ring * within(lags(height, LANES, back), taps), 0.0)
-            parts = ring if parts is None else parts + ring
-        side_ref[:, low:high] = parts[:, : high - low].astype(BF16)
-
-
-def smooth(images, vertical_ref, field_ref, taps_ref, modes, skew, taps, width):
+def build_vertical(vertical_ref, taps_ref, modes, skew, taps, turned=None):
     tall, reach = vertical_ref.shape[0] // modes, vertical_ref.shape[1]
     inside = within(lags(tall, reach, skew), taps)
     for mode in range(modes):
         ring = ring_of(taps_ref[0, mode : mode + 1], skew)
-        vertical_ref[mode * tall : (mode + 1) * tall, :] = (tiled(ring, tall, reach) * inside).astype(BF16)
+        table = (tiled(ring, tall, reach) * inside).astype(BF16)
+        start = mode * tall
+        vertical_ref[start : start + tall, :] = table
+        if turned is not None:
+            turned[start : start + tall // 2, :] = table[tall // 2 :]
+            turned[start + tall // 2 : start + tall, :] = table[: tall // 2]
+
+
+def smooth(groups, field_ref, modes, tall, width, unroll):
     chunk = divisor(modes, 4) * tall
-    for start in range(0, modes * tall, chunk):
-        table = vertical_ref[start : start + chunk, :]
-        for block, image in enumerate(images):
-            for low in range(0, image.shape[1], width):
-                field_ref[block, start : start + chunk, low : low + width] = jnp.dot(
-                    table, image[:, low : low + width], preferred_element_type=F32
-                ).astype(BF16)
+
+    def some_modes(turn, carry):
+        start = pl.multiple_of(turn * chunk, ROWS)
+        block = 0
+        for table_ref, images in groups:
+            table = table_ref[pl.ds(start, chunk), :]
+            for image in images:
+                for low in range(0, image.shape[1], width):
+                    field_ref[block, pl.ds(start, chunk), low : low + width] = jnp.dot(
+                        table, image[:, low : low + width], preferred_element_type=F32
+                    ).astype(BF16)
+                block += 1
+        return carry
+
+    lax.fori_loop(0, modes * tall // chunk, some_modes, 0, unroll=unroll)
 
 
 def blur(blocks, table, side, stride):
@@ -224,13 +225,16 @@
                 field_ref[block, start : start + tall, k * stride : (k + 1) * stride] = column.astype(BF16)
 
 
+def gathered(table, field):
+    return lax.dot_general(table, field, (((0,), (0,)), ((), ())), preferred_element_type=F32)
+
+
 def inner_kernel(
-    even_ref, picture_ref, taps_ref, coeffs_any, observed_any, rims_near_any, rims_far_any, gradient_ref, across_ref,
-    edge_coeffs_ref, edge_seen_ref, *refs, patch, taps, with_clipped,
+    picture_ref, taps_ref, coeffs_any, observed_any, gradient_ref, across_ref, *refs, patch, taps, with_clipped,
 ):
     refs = list(refs)
     clipped_ref = refs.pop(0) if with_clipped else None
-    field_ref, model_ref, coeffs_ref, seen_ref, seen_rims_ref, vertical_ref, side_ref, band_ref, sems = refs
+    field_ref, model_ref, coeffs_ref, seen_ref, vertical_ref, band_ref, sems = refs
     pieces, height, breadth = picture_ref.shape
     modes = coeffs_ref.shape[1]
     tall = coeffs_ref.shape[2]
@@ -238,29 +242,18 @@
     margin = (taps - 1) // 2
     stride = patch[1]
     width = across_ref.shape[1]
-    even = even_ref[0]
-    near_row = pl.multiple_of(even * ext, ROWS)
-    far_row = pl.multiple_of((1 - even) * ext, ROWS)
 
     moves = [
         (coeffs_any.at[:, :, pl.ds(ext, tall), :], coeffs_ref),
         (observed_any.at[:, pl.ds(ext, tall), :], seen_ref),
-        (coeffs_any.at[:, :, pl.ds(0, ext), :], edge_coeffs_ref.at[0, :, :, pl.ds(ext, ext), :]),
-        (coeffs_any.at[:, :, pl.ds(height - ext, ext), :], edge_coeffs_ref.at[1, :, :, pl.ds(0, ext), :]),
-        (rims_near_any.at[:, pl.ds(0, modes)], edge_coeffs_ref.at[even, :, :, pl.ds(near_row, ext), :]),
-        (rims_far_any.at[:, pl.ds(0, modes)], edge_coeffs_ref.at[1 - even, :, :, pl.ds(far_row, ext), :]),
-        (observed_any.at[:, pl.ds(0, ext), :], edge_seen_ref.at[0, :, pl.ds(ext, ext), :]),
-        (observed_any.at[:, pl.ds(height - ext, ext), :], edge_seen_ref.at[1, :, pl.ds(0, ext), :]),
-        (rims_near_any.at[:, pl.ds(modes, PARTS)], seen_rims_ref.at[0]),
-        (rims_far_any.at[:, pl.ds(modes, PARTS)], seen_rims_ref.at[1]),
     ]
     copies = [pltpu.make_async_copy(source, target, sems.at[k]) for k, (source, target) in enumerate(moves)]
     for copy in copies:
         copy.start()
 
     band_ref[...] = within(lags(width, width, margin), taps)
-    images = [picture_ref.at[piece] for piece in range(pieces)]
-    smooth(images, vertical_ref, field_ref, taps_ref, modes, margin - ext, taps, width)
+    build_vertical(vertical_ref, taps_ref, modes, margin - ext, taps)
+    smooth([(vertical_ref, [picture_ref.at[piece] for piece in range(pieces)])], field_ref, modes, tall, width, False)
 
     def across_of(mode):
         ring = tiled(ring_of(taps_ref[1, mode : mode + 1], margin), width, width)
@@ -270,41 +263,31 @@
     def weights(block, mode):
         return coeffs_ref[block, mode]
 
-    copies[0].wait()
-    copies[1].wait()
+    for copy in copies:
+        copy.wait()
     model_all(field_ref, model_ref, weights, across_of, modes, stride)
     model_ref[...] = jnp.clip(model_ref[...] - seen_ref[...], -DELTA, DELTA)
     if with_clipped:
         clipped_ref[...] = model_ref[...]
-    build_side(side_ref, taps_ref, modes, tall, margin - ext, taps)
     adjoint_all(field_ref, model_ref, weights, across_ref, modes, stride)
     for piece in range(pieces):
         for low in range(0, breadth, width):
-            gradient_ref[piece, :, low : low + width] = jnp.dot(
-                side_ref[...], field_ref[piece, :, low : low + width], preferred_element_type=F32
-            )
-    for copy in copies[2:]:
-        copy.wait()
-    for rim, end, row in ((0, even, near_row), (1, 1 - even, far_row)):
-        total = seen_rims_ref[rim, :, 0].astype(F32)
-        for part in range(1, PARTS):
-            total = total + seen_rims_ref[rim, :, part].astype(F32)
-        edge_seen_ref[end, :, pl.ds(row, ext), :] = total
+            gradient_ref[piece, :, low : low + width] = gathered(vertical_ref[...], field_ref[piece, :, low : low + width])
 
 
 def outer_kernel(
-    even_ref, ids_ref, picture_ref, near_ref, far_ref, counted_ref, taps_ref, gradient_ref, across_ref,
-    edge_coeffs_ref, edge_seen_ref, *refs, patch, per_tile, slot, taps, with_clipped,
+    even_ref, ids_ref, picture_ref, near_ref, far_ref, counted_ref, taps_ref, own_near_ref, own_far_ref,
+    rims_near_ref, rims_far_ref, gradient_ref, across_ref, *refs, patch, per_tile, slot, taps, with_clipped,
 ):
     refs = list(refs)
     if with_clipped:
         inner_ref, clipped_ref = refs[:2]
         refs = refs[2:]
-    sums_ref, image_ref, field_ref, model_ref, edge_ref, vertical_ref, upper_ref, lower_ref, *totals = refs
+    sums_ref, image_ref, field_ref, model_ref, edge_ref, vertical_ref, *totals = refs
     pieces, height, breadth = picture_ref.shape
-    modes, tall = edge_coeffs_ref.shape[2:4]
+    modes, ext = own_near_ref.shape[1] - PARTS, own_near_ref.shape[2]
     rim = near_ref.shape[1]
-    ext = tall // 2
+    tall = 2 * ext
     margin = (taps - 1) // 2
     patch_rows, patch_cols = patch
     stride = patch_cols
@@ -317,30 +300,43 @@
     image_ref[1, :, :rim, :] = picture_ref[:, height - rim :, :]
     image_ref[even, :, pl.ds(near_row, rim), :] = near_ref[...]
     image_ref[1 - even, :, pl.ds(far_row, rim), :] = far_ref[...]
-    places = [(end, piece) for end in (0, 1) for piece in range(pieces)]
-    images = [image_ref.at[end, piece] for end, piece in places]
-    smooth(images, vertical_ref, field_ref, taps_ref, modes, margin + ext - rim, taps, width)
+    build_vertical(vertical_ref.at[0], taps_ref, modes, margin + ext - rim, taps, vertical_ref.at[1])
+    ends = ((even, 1 - even, own_near_ref, rims_near_ref), (1 - even, even, own_far_ref, rims_far_ref))
+    places = [(side, piece) for side in (0, 1) for piece in range(pieces)]
+    groups = [
+        (vertical_ref.at[order], [image_ref.at[end, piece] for piece in range(pieces)]) for end, order, *_ in ends
+    ]
+    smooth(groups, field_ref, modes, tall, width, True)
 
     def weights(block, mode):
-        end, piece = places[block]
-        return edge_coeffs_ref[end, piece, mode]
+        side, piece = places[block]
+        return jnp.concatenate([ends[side][2][piece, mode], ends[side][3][piece, mode]], axis=0)
+
+    def seen(block):
+        side, piece = places[block]
+        halves = []
+        for rims_ref in ends[side][2:]:
+            total = rims_ref[piece, modes].astype(F32)
+            for part in range(1, PARTS):
+                total = total + rims_ref[piece, modes + part].astype(F32)
+            halves.append(total)
+        return jnp.concatenate(halves, axis=0)
 
     model_all(field_ref, model_ref, weights, lambda mode: across_ref[mode], modes, stride)
-    for block, (end, piece) in enumerate(places):
-        model_ref[block] = jnp.clip(model_ref[block] - edge_seen_ref[end, piece], -DELTA, DELTA)
+    for block in range(len(places)):
+        model_ref[block] = jnp.clip(model_ref[block] - seen(block), -DELTA, DELTA)
     if with_clipped:
+        for block, (side, piece) in enumerate(places):
+            start = pl.multiple_of(ends[side][0] * (height - ext), ROWS)
+            clipped_ref[piece, pl.ds(start, ext), :] = model_ref[block, :ext, :]
         for piece in range(pieces):
-            clipped_ref[piece, :ext, :] = model_ref[piece, ext:, :]
             clipped_ref[piece, ext : height - ext, :] = inner_ref[piece]
-            clipped_ref[piece, height - ext :, :] = model_ref[pieces + piece, :ext, :]
-    build_side(upper_ref, taps_ref, modes, tall, margin + ext, taps)
-    build_side(lower_ref, taps_ref, modes, tall, margin + ext - rim, taps)
     adjoint_all(field_ref, model_ref, weights, across_ref, modes, stride)
-    for block, (end, piece) in enumerate(places):
-        side = (upper_ref, lower_ref)[end][...]
+    for block, (side, piece) in enumerate(places):
+        end, order = ends[side][:2]
         for low in range(0, breadth, width):
-            edge_ref[end, piece, :, low : low + width] = jnp.dot(
-                side, field_ref[block, :, low : low + width], preferred_element_type=F32
+            edge_ref[end, piece, :, low : low + width] = gathered(
+                vertical_ref[order], field_ref[block, :, low : low + width]
             )
 
     held = per_tile * patch_rows
@@ -358,7 +354,7 @@
                 place = pl.ds(pl.multiple_of(index * patch_rows, patch_rows), patch_rows)
                 value = gradient_ref[piece, top : top + patch_rows, across]
                 if top < rim:
-                    value = value + edge_ref[0, piece, top : top + patch_rows, across]
+                    value = value + edge_ref[0, piece, rim + top : rim + top + patch_rows, across]
                 if top >= height - rim:
                     start = top - (height - rim)
                     value = value + edge_ref[1, piece, start : start + patch_rows, across]
@@ -423,7 +419,7 @@
     coeffs = pltpu.with_memory_space_constraint(coeffs, pltpu.HBM)
     observed = pltpu.with_memory_space_constraint(observed, pltpu.HBM)
     rim_shape = jax.ShapeDtypeStruct((pieces, modes + PARTS, ext, breadth), BF16)
-    spread, rims_near, rims_far = pl.pallas_call(
+    spread, own_near, own_far = pl.pallas_call(
         begin_kernel,
         out_shape=(jax.ShapeDtypeStruct((known, patch_cols), BF16), rim_shape, rim_shape),
         in_specs=[smem, somewhere, somewhere, somewhere],
@@ -459,8 +455,8 @@
         pltpu.with_memory_space_constraint(vert_taps, pltpu.HBM),
         pltpu.with_memory_space_constraint(horiz_taps, pltpu.HBM),
     )
-    rims_far = lax.ppermute(rims_far, "sub", routes[1])
-    rims_near = lax.ppermute(rims_near, "sub", routes[0])
+    rims_far = lax.ppermute(own_far, "sub", routes[1])
+    rims_near = lax.ppermute(own_near, "sub", routes[0])
     ids, counted, taps = lax.optimization_barrier((ids, counted, taps))
 
     clipped, counts = None, None
@@ -487,31 +483,27 @@
         results = [
             pltpu.VMEM((pieces, height, breadth), F32),
             pltpu.VMEM((modes, width, width), BF16),
-            pltpu.VMEM((2, pieces, modes, 2 * ext, breadth), BF16),
-            pltpu.VMEM((2, pieces, 2 * ext, breadth), F32),
         ]
         if last:
             results.append(pltpu.VMEM((pieces, inner, breadth), F32))
         middle = pl.pallas_call(
             functools.partial(inner_kernel, patch=patch, taps=taken, with_clipped=last),
             out_shape=tuple(results),
-            in_specs=[smem, vmem, vmem] + [somewhere] * 4,
+            in_specs=[vmem, vmem] + [somewhere] * 2,
             out_specs=(vmem,) * len(results),
             scratch_shapes=[
                 pltpu.VMEM((pieces, modes * inner, breadth), BF16),
                 pltpu.VMEM((pieces, inner, breadth), F32),
                 pltpu.VMEM((pieces, modes, inner, breadth), BF16),
                 pltpu.VMEM((pieces, inner, breadth), F32),
-                pltpu.VMEM((2, pieces, PARTS, ext, breadth), BF16),
                 pltpu.VMEM((modes * inner, height), BF16),
-                pltpu.VMEM((height, modes * inner), BF16),
                 pltpu.VMEM((width, width), F32),
-                pltpu.SemaphoreType.DMA((10,)),
+                pltpu.SemaphoreType.DMA((2,)),
             ],
             compiler_params=pltpu.CompilerParams(vmem_limit_bytes=16 << 20),
             cost_estimate=pl.CostEstimate(flops=3 * 10**9, bytes_accessed=5 * 10**6, transcendentals=0),
             name="inner",
-        )(even, picture, taps, coeffs, observed, rims_near, rims_far)
+        )(picture, taps, coeffs, observed)
         results = [jax.ShapeDtypeStruct((exp_count * slot, patch_cols), BF16)]
         if last:
             results.insert(0, jax.ShapeDtypeStruct((pieces, height, breadth), F32))
@@ -519,21 +511,19 @@
         answer = pl.pallas_call(
             functools.partial(outer_kernel, patch=patch, per_tile=per_tile, slot=slot, taps=taken, with_clipped=last),
             out_shape=tuple(results),
-            in_specs=[smem] * 2 + [vmem] * (5 + len(middle)),
+            in_specs=[smem] * 2 + [vmem] * (9 + len(middle)),
             out_specs=(vmem,) * len(results),
             scratch_shapes=[
                 pltpu.VMEM((2, pieces, 2 * rim, breadth), BF16),
                 pltpu.VMEM((2 * pieces, modes * 2 * ext, breadth), BF16),
                 pltpu.VMEM((2 * pieces, 2 * ext, breadth), F32),
-                pltpu.VMEM((2, pieces, rim, breadth), F32),
-                pltpu.VMEM((modes * 2 * ext, 2 * rim), BF16),
-                pltpu.VMEM((rim, modes * 2 * ext), BF16),
-                pltpu.VMEM((rim, modes * 2 * ext), BF16),
+                pltpu.VMEM((2, pieces, 2 * rim, breadth), F32),
+                pltpu.VMEM((2, modes * 2 * ext, 2 * rim), BF16),
             ]
             + [pltpu.VMEM((known, patch_cols), F32)] * 4,
             compiler_params=pltpu.CompilerParams(vmem_limit_bytes=12 << 20),
             name="outer",
-        )(even, ids, picture, near, far, counted, taps, *held_here)
+        )(even, ids, picture, near, far, counted, taps, own_near, own_far, rims_near, rims_far, *held_here)
         sums = answer[-1]
         if last:
             clipped = answer[0]

time: 72.3 us -> 71.6 us (level)
  waiting for transfers between devices: 4.58 us -> 0.58 us
  starting transfers between devices: 18.6 us -> 20.6 us
  blocking collectives: 26 us -> 26.8 us
    all_to_all x1, waiting for transfers between devices: 4.56 us -> 0.57 us  [exchange(): return lax.all_to_all(block, 'exp', split_axis=0, concat_axis=0, tiled=True)]
    ppermute x2, starting transfers between devices: 0.14 us -> 4.02 us  [per_device(): near = lax.ppermute(near, 'sub', routes[0])]
    ppermute x2, starting transfers between devices: 8.33 us -> 6.22 us  [per_device(): far = lax.ppermute(far, 'sub', routes[1])]
    all_to_all x1, starting transfers between devices: 5.54 us -> 6.37 us  [exchange(): return lax.all_to_all(block, 'exp', split_axis=0, concat_axis=0, tiled=True)]
    all_to_all x3, blocking collectives: 26 us -> 26.8 us  [exchange(): return lax.all_to_all(block, 'exp', split_axis=0, concat_axis=0, tiled=True)]
where the time goes in v7:
time: 71.6 us; the launch traced here: 71.1 us
  blocking collectives  26.8 us (37%)
  Pallas kernels  22.1 us (31%)
  starting transfers between devices  20.6 us (29%)
  between operations  0.82 us (1%)
    all_to_all x3, blocking collectives, exchange(): return lax.all_to_all(block, 'exp', split_axis=0, concat_axis=0, tiled=True)  26.8 us
    pallas_call x2, Pallas kernels, per_device(): pl.pallas_call(functools.partial(inner_kernel, patch=patch, taps=taken, w...  9.34 us
    pallas_call x2, Pallas kernels, per_device(): pl.pallas_call(functools.partial(outer_kernel, patch=patch, per_tile=per_...  7.12 us
    all_to_all x1, starting transfers between devices, exchange(): return lax.all_to_all(block, 'exp', split_axis=0, concat_axis=0, tiled=True)  6.37 us
    ppermute x2, starting transfers between devices, per_device(): far = lax.ppermute(far, 'sub', routes[1])  6.22 us
    ppermute x2, starting transfers between devices, per_device(): near = lax.ppermute(near, 'sub', routes[0])  4.02 us
    ppermute x1, starting transfers between devices, per_device(): rims_far = lax.ppermute(own_far, 'sub', routes[1])  3.04 us
    pallas_call x1, Pallas kernels, per_device(): pl.pallas_call(begin_kernel, out_shape=(jax.ShapeDtypeStruct((known, patc...  1.49 us
  transfers between devices with their start and end apart: 7, of which 1 were waited for; matrix products, arithmetic and copies ran while one was open for 0% of the time, Pallas kernels for 16%

profile of v7, /device:TPU:1, one launch (start us, length us, event | category | flops | bytes accessed | tf_op | source)
XLA Modules:
  0.0 71.1 jit_solution(9616983371104754830)
XLA Ops:
  0.6 0.0 copy-start.1
  0.7 0.0 copy-start
  0.7 1.5 %begin.1 = (bf16[512,128]{1,0:T(8,128)(2,1)}, bf16[2,15,16,512]{3,2,1,0:T(8,128)(2,1)S(1)}, bf16[2,15,16,512]{3,2,1,0:T(8,128)(2,1)S(1)}) custom-call(s32[1]{0:T(128)} %bitcast.1.even_ref, f32[64,128]{1,0:T(8,128)} %bitcast.19, bf16[2,12,128,512]{3,2,1,0:T(8,128)(2,1)} %coeffs_any.3, f32[2,128,512]{2,1,0:T(8,128)} %observed_any.3), custom_call_target="tpu_custom_call" | custom-call | tf_op jit(solution)/shard_map/begin/pallas_call | solution.py:422
  2.2 6.4 %all-to-all-start = ((bf16[8,64,128]{2,1,0:T(8,128)(2,1)}), bf16[8,64,128]{2,1,0:T(8,128)(2,1)S(1)}, u32[]{:S(2)}, u32[]{:S(2)}) async-start(bf16[8,64,128]{2,1,0:T(8,128)(2,1)} %bitcast.3), calls=%async_computation | async-start | bytes 262144 | tf_op jit(solution)/shard_map/all_to_all | solution.py:415
  8.5 1.0 %collective-permute-start.2 = (bf16[2,15,16,512]{3,2,1,0:T(8,128)(2,1)S(1)}, bf16[2,15,16,512]{3,2,1,0:T(8,128)(2,1)S(1)}, u32[]{:S(2)}, u32[]{:S(2)}) collective-permute-start(bf16[2,15,16,512]{3,2,1,0:T(8,128)(2,1)S(1)} %get-tuple-element.35.own_near_ref), channel_id=1, source_target_pairs={{0,1},{2,3},{1,0},{3,2},{4,5},{6,7},{5,4},{7,6},{8,9},{10,11},{9,8... | collective-permute-start | bytes 1474568 | tf_op jit(solution)/shard_map/ppermute | solution.py:459
  9.5 3.0 %collective-permute-start.3 = (bf16[2,15,16,512]{3,2,1,0:T(8,128)(2,1)S(1)}, bf16[2,15,16,512]{3,2,1,0:T(8,128)(2,1)S(1)}, u32[]{:S(2)}, u32[]{:S(2)}) collective-permute-start(bf16[2,15,16,512]{3,2,1,0:T(8,128)(2,1)S(1)} %get-tuple-element.36.own_far_ref), channel_id=1, source_target_pairs={{1,2},{2,1},{5,6},{6,5},{9,10},{10,9},{13,14},{14,13},{17,18},{18,... | collective-permute-start | bytes 1474568 | tf_op jit(solution)/shard_map/ppermute | solution.py:458
  12.5 0.0 copy-done.1
  12.6 0.0 copy-done
  12.6 0.1 copy.10
  12.7 0.1 reshape.29.ids_ref
  12.8 1.4 %prep.1 = (f32[64,128]{1,0:T(8,128)S(1)}, f32[3,16,128]{2,1,0:T(8,128)S(1)}) custom-call(s32[128]{0:T(128)S(1)} %reshape.29.ids_ref, bf16[12,21]{1,0:T(8,128)(2,1)} %vert_any.1, bf16[12,21]{1,0:T(8,128)(2,1)} %horiz_any.1), custom_call_target="tpu_custom_call" | custom-call | tf_op jit(solution)/shard_map/prep/pallas_call | solution.py:438
  14.2 0.6 all-to-all-done
  14.7 0.7 picture.2
  15.4 2.2 %collective-permute-start = (bf16[2,32,512]{2,1,0:T(8,128)(2,1)S(1)}, bf16[2,32,512]{2,1,0:T(8,128)(2,1)S(1)}, u32[]{:S(2)}, u32[]{:S(2)}) collective-permute-start(bf16[2,32,512]{2,1,0:T(8,128)(2,1)S(1)} %get-tuple-element.31), channel_id=1, source_target_pairs={{0,1},{2,3},{1,0},{3,2},{4,5},{6,7},{5,4},{7,6},{8,9},{10,11},{9,8... | collective-permute-start | bytes 196616 | tf_op jit(solution)/shard_map/ppermute | solution.py:479
  17.6 3.0 %collective-permute-start.1 = (bf16[2,32,512]{2,1,0:T(8,128)(2,1)S(1)}, bf16[2,32,512]{2,1,0:T(8,128)(2,1)S(1)}, u32[]{:S(2)}, u32[]{:S(2)}) collective-permute-start(bf16[2,32,512]{2,1,0:T(8,128)(2,1)S(1)} %get-tuple-element.32), channel_id=1, source_target_pairs={{1,2},{2,1},{5,6},{6,5},{9,10},{10,9},{13,14},{14,13},{17,18},{18,... | collective-permute-start | bytes 196616 | tf_op jit(solution)/shard_map/ppermute | solution.py:478
  20.6 4.7 %inner.2 = (f32[2,128,512]{2,1,0:T(8,128)S(1)}, bf16[12,256,256]{2,1,0:T(8,128)(2,1)S(1)}) custom-call(bf16[2,128,512]{2,1,0:T(8,128)(2,1)S(1)} %get-tuple-element.30.picture_ref, f32[3,16,128]{2,1,0:T(8,128)S(1)} %get-tuple-element.34.taps_ref, bf16[2,12,128,512]{3,2,1,0:T(8,128)(2,1)} %coeffs_any.3, f32[2,128,512]{2,1,0:T(8,128)} %observed_any.3), custom_call_target="tpu_custom_call" | custom-call | flops 3000000000 | bytes 5000000 | tf_op jit(solution)/shard_map/inner/pallas_call | solution.py:489
  25.3 0.0 collective-permute-done.near_ref
  25.3 0.0 collective-permute-done.1.far_ref
  25.3 0.0 collective-permute-done.2.rims_near_ref
  25.3 0.0 collective-permute-done.3.rims_far_ref
  25.3 3.2 %outer.2 = bf16[640,128]{1,0:T(8,128)(2,1)S(1)} custom-call(s32[1]{0:T(128)} %bitcast.1.even_ref, s32[128]{0:T(128)S(1)} %reshape.29.ids_ref, bf16[2,128,512]{2,1,0:T(8,128)(2,1)S(1)} %get-tuple-element.30.picture_ref, bf16[2,32,512]{2,1,0:T(8,128)(2,1)S(1)} %collective-permute-done.near_ref, bf16[2,32,512]{2,1,0:T(8,128)(2,1)S(1)} %collective-permute-done.1.far_ref, ...), custom_call_target="tpu_custom_call" | custom-call | tf_op jit(solution)/shard_map/outer/pallas_call | solution.py:511
  28.5 9.4 %all_to_all.44 = bf16[8,80,128]{2,1,0:T(8,128)(2,1)S(1)} all-to-all(bf16[8,80,128]{2,1,0:T(8,128)(2,1)S(1)} %bitcast.12), channel_id=1, replica_groups=mesh['exp'=8,'sub'=4] {'exp'}, dimensions={0} | all-to-all | bytes 327680 | tf_op jit(solution)/shard_map/all_to_all | solution.py:415
  38.0 0.8 %update.2 = (f32[64,128]{1,0:T(8,128)S(1)}, bf16[512,128]{1,0:T(8,128)(2,1)S(1)}, f32[64,128]{1,0:T(8,128)S(1)}) custom-call(f32[64,128]{1,0:T(8,128)} %bitcast.20, bf16[640,128]{1,0:T(8,128)(2,1)S(1)} %bitcast.13), custom_call_target="tpu_custom_call" | custom-call | tf_op jit(solution)/shard_map/update/pallas_call | solution.py:538
  38.8 8.7 %all_to_all.45 = bf16[8,64,128]{2,1,0:T(8,128)(2,1)S(1)} all-to-all(bf16[8,64,128]{2,1,0:T(8,128)(2,1)S(1)} %bitcast.18), channel_id=1, replica_groups=mesh['exp'=8,'sub'=4] {'exp'}, dimensions={0} | all-to-all | bytes 262144 | tf_op jit(solution)/shard_map/all_to_all | solution.py:415
  47.5 0.7 picture.3
  48.2 1.9 %collective-permute-start.4 = (bf16[2,32,512]{2,1,0:T(8,128)(2,1)S(1)}, bf16[2,32,512]{2,1,0:T(8,128)(2,1)S(1)}, u32[]{:S(2)}, u32[]{:S(2)}) collective-permute-start(bf16[2,32,512]{2,1,0:T(8,128)(2,1)S(1)} %get-tuple-element.42), channel_id=1, source_target_pairs={{0,1},{2,3},{1,0},{3,2},{4,5},{6,7},{5,4},{7,6},{8,9},{10,11},{9,8... | collective-permute-start | bytes 196616 | tf_op jit(solution)/shard_map/ppermute | solution.py:479
  50.0 3.2 %collective-permute-start.5 = (bf16[2,32,512]{2,1,0:T(8,128)(2,1)S(1)}, bf16[2,32,512]{2,1,0:T(8,128)(2,1)S(1)}, u32[]{:S(2)}, u32[]{:S(2)}) collective-permute-start(bf16[2,32,512]{2,1,0:T(8,128)(2,1)S(1)} %get-tuple-element.43), channel_id=1, source_target_pairs={{1,2},{2,1},{5,6},{6,5},{9,10},{10,9},{13,14},{14,13},{17,18},{18,... | collective-permute-start | bytes 196616 | tf_op jit(solution)/shard_map/ppermute | solution.py:478
  53.2 4.7 %inner.3 = (f32[2,128,512]{2,1,0:T(8,128)S(1)}, bf16[12,256,256]{2,1,0:T(8,128)(2,1)S(1)}, f32[2,96,512]{2,1,0:T(8,128)S(1)}) custom-call(bf16[2,128,512]{2,1,0:T(8,128)(2,1)S(1)} %get-tuple-element.41.picture_ref, f32[3,16,128]{2,1,0:T(8,128)S(1)} %get-tuple-element.34.taps_ref, bf16[2,12,128,512]{3,2,1,0:T(8,128)(2,1)} %coeffs_any.3, ...), custom_call_target="tpu_custom_call" | custom-call | flops 3000000000 | bytes 5000000 | tf_op jit(solution)/shard_map/inner/pallas_call | solution.py:489
  57.9 0.0 collective-permute-done.4.near_ref
  57.9 0.0 collective-permute-done.5.far_ref
  57.9 3.9 %outer.3 = (f32[2,128,512]{2,1,0:T(8,128)}, bf16[512,128]{1,0:T(8,128)(2,1)S(1)}) custom-call(s32[1]{0:T(128)} %bitcast.1.even_ref, s32[128]{0:T(128)S(1)} %reshape.29.ids_ref, bf16[2,128,512]{2,1,0:T(8,128)(2,1)S(1)} %get-tuple-element.41.picture_ref, bf16[2,32,512]{2,1,0:T(8,128)(2,1)S(1)} %collective-permute-done.4.near_ref, ...), custom_call_target="tpu_custom_call" | custom-call | tf_op jit(solution)/shard_map/outer/pallas_call | solution.py:511
  61.9 8.6 %all_to_all.46 = bf16[8,64,128]{2,1,0:T(8,128)(2,1)S(1)} all-to-all(bf16[8,64,128]{2,1,0:T(8,128)(2,1)S(1)} %bitcast.17), channel_id=1, replica_groups=mesh['exp'=8,'sub'=4] {'exp'}, dimensions={0} | all-to-all | bytes 262144 | tf_op jit(solution)/shard_map/all_to_all | solution.py:415
  70.4 0.6 update.3
  (2 shorter events, 0.0 us)
Async XLA Ops:
  0.6 11.9 %copy-start.1 = (s32[2,16,4,1]{1,3,2,0:T(1,128)S(1)}, s32[2,16,4,1]{1,3,2,0:T(1,128)}, u32[]{:S(2)}) copy-start(s32[2,16,4,1]{1,3,2,0:T(1,128)} %param.12) | copy-start | bytes 1540
  0.7 11.9 %copy-start = (s32[2,16,4]{1,2,0:T(4,128)S(1)}, s32[2,16,4]{1,2,0:T(4,128)}, u32[]{:S(2)}) copy-start(s32[2,16,4]{1,2,0:T(4,128)} %param.13) | copy-start | bytes 1540
  2.2 12.6 %all-to-all-start = ((bf16[8,64,128]{2,1,0:T(8,128)(2,1)}), bf16[8,64,128]{2,1,0:T(8,128)(2,1)S(1)}, u32[]{:S(2)}, u32[]{:S(2)}) async-start(bf16[8,64,128]{2,1,0:T(8,128)(2,1)} %bitcast.3), calls=%async_computation | async-start | bytes 262144 | tf_op jit(solution)/shard_map/all_to_all | solution.py:415
  8.5 16.8 %collective-permute-start.2 = (bf16[2,15,16,512]{3,2,1,0:T(8,128)(2,1)S(1)}, bf16[2,15,16,512]{3,2,1,0:T(8,128)(2,1)S(1)}, u32[]{:S(2)}, u32[]{:S(2)}) collective-permute-start(bf16[2,15,16,512]{3,2,1,0:T(8,128)(2,1)S(1)} %get-tuple-element.35.own_near_ref), channel_id=1, source_target_pairs={{0,1},{2,3},{1,0},{3,2},{4,5},{6,7},{5,4},{7,6},{8,9},{10,11},{9,8... | collective-permute-start | bytes 1474568 | tf_op jit(solution)/shard_map/ppermute | solution.py:459
  9.5 15.8 %collective-permute-start.3 = (bf16[2,15,16,512]{3,2,1,0:T(8,128)(2,1)S(1)}, bf16[2,15,16,512]{3,2,1,0:T(8,128)(2,1)S(1)}, u32[]{:S(2)}, u32[]{:S(2)}) collective-permute-start(bf16[2,15,16,512]{3,2,1,0:T(8,128)(2,1)S(1)} %get-tuple-element.36.own_far_ref), channel_id=1, source_target_pairs={{1,2},{2,1},{5,6},{6,5},{9,10},{10,9},{13,14},{14,13},{17,18},{18,... | collective-permute-start | bytes 1474568 | tf_op jit(solution)/shard_map/ppermute | solution.py:458
  15.4 9.9 %collective-permute-start = (bf16[2,32,512]{2,1,0:T(8,128)(2,1)S(1)}, bf16[2,32,512]{2,1,0:T(8,128)(2,1)S(1)}, u32[]{:S(2)}, u32[]{:S(2)}) collective-permute-start(bf16[2,32,512]{2,1,0:T(8,128)(2,1)S(1)} %get-tuple-element.31), channel_id=1, source_target_pairs={{0,1},{2,3},{1,0},{3,2},{4,5},{6,7},{5,4},{7,6},{8,9},{10,11},{9,8... | collective-permute-start | bytes 196616 | tf_op jit(solution)/shard_map/ppermute | solution.py:479
  17.6 7.7 %collective-permute-start.1 = (bf16[2,32,512]{2,1,0:T(8,128)(2,1)S(1)}, bf16[2,32,512]{2,1,0:T(8,128)(2,1)S(1)}, u32[]{:S(2)}, u32[]{:S(2)}) collective-permute-start(bf16[2,32,512]{2,1,0:T(8,128)(2,1)S(1)} %get-tuple-element.32), channel_id=1, source_target_pairs={{1,2},{2,1},{5,6},{6,5},{9,10},{10,9},{13,14},{14,13},{17,18},{18,... | collective-permute-start | bytes 196616 | tf_op jit(solution)/shard_map/ppermute | solution.py:478
  48.2 9.7 %collective-permute-start.4 = (bf16[2,32,512]{2,1,0:T(8,128)(2,1)S(1)}, bf16[2,32,512]{2,1,0:T(8,128)(2,1)S(1)}, u32[]{:S(2)}, u32[]{:S(2)}) collective-permute-start(bf16[2,32,512]{2,1,0:T(8,128)(2,1)S(1)} %get-tuple-element.42), channel_id=1, source_target_pairs={{0,1},{2,3},{1,0},{3,2},{4,5},{6,7},{5,4},{7,6},{8,9},{10,11},{9,8... | collective-permute-start | bytes 196616 | tf_op jit(solution)/shard_map/ppermute | solution.py:479
  50.0 7.9 %collective-permute-start.5 = (bf16[2,32,512]{2,1,0:T(8,128)(2,1)S(1)}, bf16[2,32,512]{2,1,0:T(8,128)(2,1)S(1)}, u32[]{:S(2)}, u32[]{:S(2)}) collective-permute-start(bf16[2,32,512]{2,1,0:T(8,128)(2,1)S(1)} %get-tuple-element.43), channel_id=1, source_target_pairs={{1,2},{2,1},{5,6},{6,5},{9,10},{10,9},{13,14},{14,13},{17,18},{18,... | collective-permute-start | bytes 196616 | tf_op jit(solution)/shard_map/ppermute | solution.py:478

commit v8 on v7

--- a/solution.py
+++ b/solution.py
@@ -34,11 +34,18 @@
     return routes
 
 
-def begin_kernel(even_ref, sky_any, coeffs_ref, observed_ref, spread_any, near_ref, far_ref, seen_ref, sky_ref, spread_ref, sems):
+def is_even():
+    return 1 - lax.rem(lax.axis_index("sub"), 2)
+
+
+def begin_kernel(
+    sky_any, coeffs_ref, observed_ref, vert_any, horiz_any, spread_any, near_ref, far_ref, taps_ref,
+    seen_ref, sky_ref, spread_ref, vert_ref, horiz_ref, sems,
+):
     modes, height = coeffs_ref.shape[1:3]
     ext = near_ref.shape[2]
     held = sky_ref.shape[0]
-    even = even_ref[0]
+    even = is_even()
     near_at = pl.multiple_of(even * (height - ext), ROWS)
     far_at = pl.multiple_of((1 - even) * (height - ext), ROWS)
     copies = []
@@ -55,6 +62,12 @@
         )
     for copy in copies:
         copy.start()
+    filters = [
+        pltpu.make_async_copy(vert_any, vert_ref, sems.at[6]),
+        pltpu.make_async_copy(horiz_any, horiz_ref, sems.at[7]),
+    ]
+    for copy in filters:
+        copy.start()
     sky_copy.wait()
     rounded = sky_ref[...].astype(BF16)
     for start in range(0, spread_ref.shape[0], held):
@@ -68,34 +81,16 @@
             piece = rest.astype(BF16)
             out_ref[:, modes + part] = piece
             rest = rest - piece.astype(F32)
+    taps_ref[...] = jnp.zeros(taps_ref.shape, F32)
+    for place, (copy, filter_ref) in enumerate(zip(filters, (vert_ref, horiz_ref))):
+        copy.wait()
+        taps_ref[place, :modes, : filter_ref.shape[1]] = filter_ref[...].astype(F32)
     copies[1].wait()
     copies[3].wait()
     spread_copy.wait()
 
 
-def prep_kernel(ids_ref, vert_any, horiz_any, counted_ref, taps_ref, vert_ref, horiz_ref, sems):
-    copies = [
-        pltpu.make_async_copy(vert_any, vert_ref, sems.at[0]),
-        pltpu.make_async_copy(horiz_any, horiz_ref, sems.at[1]),
-    ]
-    for copy in copies:
-        copy.start()
-    modes, taps = vert_ref.shape
-    counted_ref[...] = jnp.zeros(counted_ref.shape, F32)
-    for place in range(ids_ref.shape[0]):
-        counted_ref[pl.ds(ids_ref[place], 1), :] += 1.0
-    taps_ref[...] = jnp.zeros(taps_ref.shape, F32)
-    for copy in copies:
-        copy.wait()
-    taps_ref[0, :modes, :taps] = vert_ref[...].astype(F32)
-    taps_ref[1, :modes, :taps] = horiz_ref[...].astype(F32)
-    turn = lax.broadcasted_iota(jnp.int32, (LANES, LANES), 0) + lax.broadcasted_iota(jnp.int32, (LANES, LANES), 1)
-    taps_ref[2] = jnp.dot(
-        taps_ref[0].astype(BF16), (turn == taps - 1).astype(F32).astype(BF16), preferred_element_type=F32
-    )
-
-
-def picture_kernel(even_ref, ids_ref, tiles_ref, picture_ref, near_ref, far_ref, wide_ref, *, patch):
+def picture_kernel(ids_ref, tiles_ref, picture_ref, near_ref, far_ref, wide_ref, *, patch):
     pieces, height, breadth = picture_ref.shape
     rim = near_ref.shape[1]
     patch_rows, patch_cols = patch
@@ -114,7 +109,7 @@
                 picture_ref[
                     piece, row * patch_rows : (row + together) * patch_rows, col * patch_cols : (col + 1) * patch_cols
                 ] = jnp.concatenate(parts, axis=0).astype(BF16)
-    even = even_ref[0]
+    even = is_even()
     near_ref[...] = picture_ref[:, pl.ds(pl.multiple_of(even * (height - rim), ROWS), rim), :]
     far_ref[...] = picture_ref[:, pl.ds(pl.multiple_of((1 - even) * (height - rim), ROWS), rim), :]
 
@@ -276,14 +271,15 @@
 
 
 def outer_kernel(
-    even_ref, ids_ref, picture_ref, near_ref, far_ref, counted_ref, taps_ref, own_near_ref, own_far_ref,
+    ids_any, picture_ref, near_ref, far_ref, taps_ref, own_near_ref, own_far_ref,
     rims_near_ref, rims_far_ref, gradient_ref, across_ref, *refs, patch, per_tile, slot, taps, with_clipped,
 ):
     refs = list(refs)
-    if with_clipped:
-        inner_ref, clipped_ref = refs[:2]
-        refs = refs[2:]
-    sums_ref, image_ref, field_ref, model_ref, edge_ref, vertical_ref, *totals = refs
+    inner_ref = refs.pop(0) if with_clipped else None
+    clipped_ref = refs.pop(0) if with_clipped else None
+    sums_ref, image_ref, field_ref, model_ref, edge_ref, vertical_ref, counted_ref, ids_ref, sem, *totals = refs
+    listed = pltpu.make_async_copy(ids_any, ids_ref, sem)
+    listed.start()
     pieces, height, breadth = picture_ref.shape
     modes, ext = own_near_ref.shape[1] - PARTS, own_near_ref.shape[2]
     rim = near_ref.shape[1]
@@ -292,7 +288,7 @@
     patch_rows, patch_cols = patch
     stride = patch_cols
     width = across_ref.shape[1]
-    even = even_ref[0]
+    even = is_even()
     near_row = pl.multiple_of(even * rim, ROWS)
     far_row = pl.multiple_of((1 - even) * rim, ROWS)
 
@@ -322,6 +318,11 @@
             halves.append(total)
         return jnp.concatenate(halves, axis=0)
 
+    listed.wait()
+    if slot > per_tile * patch_rows:
+        counted_ref[...] = jnp.zeros(counted_ref.shape, F32)
+        for place in range(ids_ref.shape[0]):
+            counted_ref[pl.ds(ids_ref[place], 1), :] += 1.0
     model_all(field_ref, model_ref, weights, lambda mode: across_ref[mode], modes, stride)
     for block in range(len(places)):
         model_ref[block] = jnp.clip(model_ref[block] - seen(block), -DELTA, DELTA)
@@ -415,49 +416,38 @@
         return lax.all_to_all(block, "exp", split_axis=0, concat_axis=0, tiled=True)
 
     sky = pltpu.with_memory_space_constraint(sky_map.reshape(held, patch_cols), pltpu.HBM)
-    even = (1 - lax.axis_index("sub") % 2).astype(jnp.int32).reshape(1)
     coeffs = pltpu.with_memory_space_constraint(coeffs, pltpu.HBM)
     observed = pltpu.with_memory_space_constraint(observed, pltpu.HBM)
     rim_shape = jax.ShapeDtypeStruct((pieces, modes + PARTS, ext, breadth), BF16)
-    spread, own_near, own_far = pl.pallas_call(
+    spread, own_near, own_far, taps = pl.pallas_call(
         begin_kernel,
-        out_shape=(jax.ShapeDtypeStruct((known, patch_cols), BF16), rim_shape, rim_shape),
-        in_specs=[smem, somewhere, somewhere, somewhere],
-        out_specs=(somewhere, vmem, vmem),
+        out_shape=(
+            jax.ShapeDtypeStruct((known, patch_cols), BF16),
+            rim_shape,
+            rim_shape,
+            jax.ShapeDtypeStruct((2, round_up(modes, 8), LANES), F32),
+        ),
+        in_specs=[somewhere] * 5,
+        out_specs=(somewhere, vmem, vmem, vmem),
         scratch_shapes=[
             pltpu.VMEM((2, pieces, ext, breadth), F32),
             pltpu.VMEM((held, patch_cols), F32),
             pltpu.VMEM((known, patch_cols), BF16),
-            pltpu.SemaphoreType.DMA((6,)),
+            pltpu.VMEM(vert_taps.shape, BF16),
+            pltpu.VMEM(horiz_taps.shape, BF16),
+            pltpu.SemaphoreType.DMA((8,)),
         ],
         compiler_params=pltpu.CompilerParams(vmem_limit_bytes=8 << 20),
         name="begin",
-    )(even, sky, coeffs, observed)
-    tiles = exchange(spread)
-    ids = (owner_ids.reshape(offset.shape) * per_tile + offset).reshape(-1)
-    counted, taps = pl.pallas_call(
-        prep_kernel,
-        out_shape=(
-            jax.ShapeDtypeStruct((exp_count * per_tile, patch_cols), F32),
-            jax.ShapeDtypeStruct((3, round_up(modes, 8), LANES), F32),
-        ),
-        in_specs=[smem, somewhere, somewhere],
-        out_specs=(vmem, vmem),
-        scratch_shapes=[
-            pltpu.VMEM(vert_taps.shape, BF16),
-            pltpu.VMEM(horiz_taps.shape, BF16),
-            pltpu.SemaphoreType.DMA((2,)),
-        ],
-        compiler_params=pltpu.CompilerParams(vmem_limit_bytes=4 << 20),
-        name="prep",
     )(
-        ids,
+        sky, coeffs, observed,
         pltpu.with_memory_space_constraint(vert_taps, pltpu.HBM),
         pltpu.with_memory_space_constraint(horiz_taps, pltpu.HBM),
     )
+    tiles = exchange(spread)
+    ids = (owner_ids.reshape(offset.shape) * per_tile + offset).reshape(-1)
     rims_far = lax.ppermute(own_far, "sub", routes[1])
     rims_near = lax.ppermute(own_near, "sub", routes[0])
-    ids, counted, taps = lax.optimization_barrier((ids, counted, taps))
 
     clipped, counts = None, None
     for step in range(STEPS):
@@ -469,12 +459,12 @@
                 jax.ShapeDtypeStruct((pieces, rim, breadth), BF16),
                 jax.ShapeDtypeStruct((pieces, rim, breadth), BF16),
             ),
-            in_specs=[smem, smem, vmem],
+            in_specs=[smem, vmem],
             out_specs=(vmem, vmem, vmem),
             scratch_shapes=[pltpu.VMEM((known, patch_cols), F32)],
             compiler_params=pltpu.CompilerParams(vmem_limit_bytes=8 << 20),
             name="picture",
-        )(even, ids, tiles)
+        )(ids, tiles)
         far = lax.ppermute(far, "sub", routes[1])
         near = lax.ppermute(near, "sub", routes[0])
         slot = held + (round_up(per_tile, ROWS) if first else 0)
@@ -511,7 +501,7 @@
         answer = pl.pallas_call(
             functools.partial(outer_kernel, patch=patch, per_tile=per_tile, slot=slot, taps=taken, with_clipped=last),
             out_shape=tuple(results),
-            in_specs=[smem] * 2 + [vmem] * (9 + len(middle)),
+            in_specs=[somewhere] + [vmem] * (8 + len(middle)),
             out_specs=(vmem,) * len(results),
             scratch_shapes=[
                 pltpu.VMEM((2, pieces, 2 * rim, breadth), BF16),
@@ -519,11 +509,14 @@
                 pltpu.VMEM((2 * pieces, 2 * ext, breadth), F32),
                 pltpu.VMEM((2, pieces, 2 * rim, breadth), F32),
                 pltpu.VMEM((2, modes * 2 * ext, 2 * rim), BF16),
+                pltpu.VMEM((exp_count * per_tile, patch_cols), F32),
+                pltpu.SMEM(ids.shape, jnp.int32),
+                pltpu.SemaphoreType.DMA,
             ]
             + [pltpu.VMEM((known, patch_cols), F32)] * 4,
             compiler_params=pltpu.CompilerParams(vmem_limit_bytes=12 << 20),
             name="outer",
-        )(even, ids, picture, near, far, counted, taps, own_near, own_far, rims_near, rims_far, *held_here)
+        )(ids, picture, near, far, taps, own_near, own_far, rims_near, rims_far, *held_here)
         sums = answer[-1]
         if last:
             clipped = answer[0]

time: 71.6 us -> 70.4 us (0.983)
  Pallas kernels: 22.1 us -> 20.3 us
  waiting for transfers between devices: 0.58 us -> 1.98 us
    ppermute x2, starting transfers between devices: 4.02 us -> 2.22 us  [per_device(): near = lax.ppermute(near, 'sub', routes[0])]
    ppermute x2, starting transfers between devices: 6.22 us -> 7.73 us  [per_device(): far = lax.ppermute(far, 'sub', routes[1])]
    all_to_all x1, waiting for transfers between devices: 0.57 us -> 1.96 us  [exchange(): return lax.all_to_all(block, 'exp', split_axis=0, concat_axis=0, tiled=True)]
    pallas_call x1 -> x0, Pallas kernels: 1.39 us -> none  [per_device(): pl.pallas_call(prep_kernel, out_shape=(jax.ShapeDtypeStruct((exp_count *...]
  transfers between devices with their start and end apart: 7 -> 7, of which waited for: 1 -> 1; matrix products, arithmetic and copies ran while one was open for 0% -> 0% of each run, Pallas kernels for 16% -> 14%
where the time goes in v8:
time: 70.4 us; the launch traced here: 69.9 us
  blocking collectives  26.3 us (37%)
  Pallas kernels  20.3 us (29%)
  starting transfers between devices  20.3 us (29%)
  waiting for transfers between devices  1.98 us (3%)
  between operations  0.82 us (1%)
    all_to_all x3, blocking collectives, exchange(): return lax.all_to_all(block, 'exp', split_axis=0, concat_axis=0, tiled=True)  26.3 us
    pallas_call x2, Pallas kernels, per_device(): pl.pallas_call(functools.partial(inner_kernel, patch=patch, taps=taken, w...  9.17 us
    ppermute x2, starting transfers between devices, per_device(): far = lax.ppermute(far, 'sub', routes[1])  7.73 us
    pallas_call x2, Pallas kernels, per_device(): pl.pallas_call(functools.partial(outer_kernel, patch=patch, per_tile=per_...  6.81 us
    all_to_all x1, starting transfers between devices, exchange(): return lax.all_to_all(block, 'exp', split_axis=0, concat_axis=0, tiled=True)  6.37 us
    ppermute x1, starting transfers between devices, per_device(): rims_far = lax.ppermute(own_far, 'sub', routes[1])  3.04 us
    ppermute x2, starting transfers between devices, per_device(): near = lax.ppermute(near, 'sub', routes[0])  2.22 us
    all_to_all x1, waiting for transfers between devices, exchange(): return lax.all_to_all(block, 'exp', split_axis=0, concat_axis=0, tiled=True)  1.96 us
  transfers between devices with their start and end apart: 7, of which 1 were waited for; matrix products, arithmetic and copies ran while one was open for 0% of the time, Pallas kernels for 14%

profile of v8, /device:TPU:1, one launch (start us, length us, event | category | flops | bytes accessed | tf_op | source)
XLA Modules:
  0.0 69.9 jit_solution(16616295409498097595)
XLA Ops:
  0.6 0.0 copy-start.1
  0.6 0.0 copy-start
  0.7 1.5 %begin.1 = (bf16[512,128]{1,0:T(8,128)(2,1)}, bf16[2,15,16,512]{3,2,1,0:T(8,128)(2,1)S(1)}, bf16[2,15,16,512]{3,2,1,0:T(8,128)(2,1)S(1)}, f32[2,16,128]{2,1,0:T(8,128)S(1)}) custom-call(f32[64,128]{1,0:T(8,128)} %bitcast.18, bf16[2,12,128,512]{3,2,1,0:T(8,128)(2,1)} %coeffs_any.3, f32[2,128,512]{2,1,0:T(8,128)} %observed_any.3, bf16[12,21]{1,0:T(8,128)(2,1)} %vert_any.1, ...), custom_call_target="tpu_custom_call" | custom-call | tf_op jit(solution)/shard_map/begin/pallas_call | solution.py:422
  2.2 6.4 %all-to-all-start = ((bf16[8,64,128]{2,1,0:T(8,128)(2,1)}), bf16[8,64,128]{2,1,0:T(8,128)(2,1)S(1)}, u32[]{:S(2)}, u32[]{:S(2)}) async-start(bf16[8,64,128]{2,1,0:T(8,128)(2,1)} %bitcast.2), calls=%async_computation | async-start | bytes 262144 | tf_op jit(solution)/shard_map/all_to_all | solution.py:416
  8.5 1.0 %collective-permute-start.2 = (bf16[2,15,16,512]{3,2,1,0:T(8,128)(2,1)S(1)}, bf16[2,15,16,512]{3,2,1,0:T(8,128)(2,1)S(1)}, u32[]{:S(2)}, u32[]{:S(2)}) collective-permute-start(bf16[2,15,16,512]{3,2,1,0:T(8,128)(2,1)S(1)} %get-tuple-element.27.own_near_ref), channel_id=1, source_target_pairs={{0,1},{2,3},{1,0},{3,2},{4,5},{6,7},{5,4},{7,6},{8,9},{10,11},{9,8... | collective-permute-start | bytes 1474568 | tf_op jit(solution)/shard_map/ppermute | solution.py:450
  9.5 3.0 %collective-permute-start.3 = (bf16[2,15,16,512]{3,2,1,0:T(8,128)(2,1)S(1)}, bf16[2,15,16,512]{3,2,1,0:T(8,128)(2,1)S(1)}, u32[]{:S(2)}, u32[]{:S(2)}) collective-permute-start(bf16[2,15,16,512]{3,2,1,0:T(8,128)(2,1)S(1)} %get-tuple-element.28.own_far_ref), channel_id=1, source_target_pairs={{1,2},{2,1},{5,6},{6,5},{9,10},{10,9},{13,14},{14,13},{17,18},{18,... | collective-permute-start | bytes 1474568 | tf_op jit(solution)/shard_map/ppermute | solution.py:449
  12.5 0.0 copy-done.1
  12.6 0.0 copy-done
  12.6 0.1 copy.10
  12.7 0.1 reshape.25.ids_ref.ids_any
  12.8 2.0 %all-to-all-done = bf16[8,64,128]{2,1,0:T(8,128)(2,1)S(1)} async-done(((bf16[8,64,128]{2,1,0:T(8,128)(2,1)}), bf16[8,64,128]{2,1,0:T(8,128)(2,1)S(1)}, u32[]{:S(2)}, u32[]{:S(2)}) %all-to-all-start) | async-done | bytes 131104 | tf_op jit(solution)/shard_map/all_to_all | solution.py:416
  14.7 0.7 picture.2
  15.4 2.2 %collective-permute-start = (bf16[2,32,512]{2,1,0:T(8,128)(2,1)S(1)}, bf16[2,32,512]{2,1,0:T(8,128)(2,1)S(1)}, u32[]{:S(2)}, u32[]{:S(2)}) collective-permute-start(bf16[2,32,512]{2,1,0:T(8,128)(2,1)S(1)} %get-tuple-element.24), channel_id=1, source_target_pairs={{0,1},{2,3},{1,0},{3,2},{4,5},{6,7},{5,4},{7,6},{8,9},{10,11},{9,8... | collective-permute-start | bytes 196616 | tf_op jit(solution)/shard_map/ppermute | solution.py:469
  17.6 3.0 %collective-permute-start.1 = (bf16[2,32,512]{2,1,0:T(8,128)(2,1)S(1)}, bf16[2,32,512]{2,1,0:T(8,128)(2,1)S(1)}, u32[]{:S(2)}, u32[]{:S(2)}) collective-permute-start(bf16[2,32,512]{2,1,0:T(8,128)(2,1)S(1)} %get-tuple-element.25), channel_id=1, source_target_pairs={{1,2},{2,1},{5,6},{6,5},{9,10},{10,9},{13,14},{14,13},{17,18},{18,... | collective-permute-start | bytes 196616 | tf_op jit(solution)/shard_map/ppermute | solution.py:468
  20.6 4.6 %inner.2 = (f32[2,128,512]{2,1,0:T(8,128)S(1)}, bf16[12,256,256]{2,1,0:T(8,128)(2,1)S(1)}) custom-call(bf16[2,128,512]{2,1,0:T(8,128)(2,1)S(1)} %get-tuple-element.23.picture_ref, f32[2,16,128]{2,1,0:T(8,128)S(1)} %get-tuple-element.26.taps_ref, bf16[2,12,128,512]{3,2,1,0:T(8,128)(2,1)} %coeffs_any.3, f32[2,128,512]{2,1,0:T(8,128)} %observed_any.3), custom_call_target="tpu_custom_call" | custom-call | flops 3000000000 | bytes 5000000 | tf_op jit(solution)/shard_map/inner/pallas_call | solution.py:479
  25.2 0.0 collective-permute-done.near_ref
  25.2 0.0 collective-permute-done.1.far_ref
  25.2 0.0 collective-permute-done.2.rims_near_ref
  25.2 0.0 collective-permute-done.3.rims_far_ref
  25.2 3.1 %outer.2 = bf16[640,128]{1,0:T(8,128)(2,1)S(1)} custom-call(s32[128]{0:T(128)S(1)} %reshape.25.ids_ref.ids_any, bf16[2,128,512]{2,1,0:T(8,128)(2,1)S(1)} %get-tuple-element.23.picture_ref, bf16[2,32,512]{2,1,0:T(8,128)(2,1)S(1)} %collective-permute-done.near_ref, bf16[2,32,512]{2,1,0:T(8,128)(2,1)S(1)} %collective-permute-done.1.far_ref, ...), custom_call_target="tpu_custom_call" | custom-call | tf_op jit(solution)/shard_map/outer/pallas_call | solution.py:501
  28.3 8.8 %all_to_all.44 = bf16[8,80,128]{2,1,0:T(8,128)(2,1)S(1)} all-to-all(bf16[8,80,128]{2,1,0:T(8,128)(2,1)S(1)} %bitcast.11), channel_id=1, replica_groups=mesh['exp'=8,'sub'=4] {'exp'}, dimensions={0} | all-to-all | bytes 327680 | tf_op jit(solution)/shard_map/all_to_all | solution.py:416
  37.1 0.8 %update.2 = (f32[64,128]{1,0:T(8,128)S(1)}, bf16[512,128]{1,0:T(8,128)(2,1)S(1)}, f32[64,128]{1,0:T(8,128)S(1)}) custom-call(f32[64,128]{1,0:T(8,128)} %bitcast.19, bf16[640,128]{1,0:T(8,128)(2,1)S(1)} %bitcast.12), custom_call_target="tpu_custom_call" | custom-call | tf_op jit(solution)/shard_map/update/pallas_call | solution.py:531
  37.9 8.9 %all_to_all.45 = bf16[8,64,128]{2,1,0:T(8,128)(2,1)S(1)} all-to-all(bf16[8,64,128]{2,1,0:T(8,128)(2,1)S(1)} %bitcast.17), channel_id=1, replica_groups=mesh['exp'=8,'sub'=4] {'exp'}, dimensions={0} | all-to-all | bytes 262144 | tf_op jit(solution)/shard_map/all_to_all | solution.py:416
  46.8 0.7 picture.3
  47.5 0.1 collective-permute-start.4
  47.5 4.7 %collective-permute-start.5 = (bf16[2,32,512]{2,1,0:T(8,128)(2,1)S(1)}, bf16[2,32,512]{2,1,0:T(8,128)(2,1)S(1)}, u32[]{:S(2)}, u32[]{:S(2)}) collective-permute-start(bf16[2,32,512]{2,1,0:T(8,128)(2,1)S(1)} %get-tuple-element.35), channel_id=1, source_target_pairs={{1,2},{2,1},{5,6},{6,5},{9,10},{10,9},{13,14},{14,13},{17,18},{18,... | collective-permute-start | bytes 196616 | tf_op jit(solution)/shard_map/ppermute | solution.py:468
  52.2 4.6 %inner.3 = (f32[2,128,512]{2,1,0:T(8,128)S(1)}, bf16[12,256,256]{2,1,0:T(8,128)(2,1)S(1)}, f32[2,96,512]{2,1,0:T(8,128)S(1)}) custom-call(bf16[2,128,512]{2,1,0:T(8,128)(2,1)S(1)} %get-tuple-element.33.picture_ref, f32[2,16,128]{2,1,0:T(8,128)S(1)} %get-tuple-element.26.taps_ref, bf16[2,12,128,512]{3,2,1,0:T(8,128)(2,1)} %coeffs_any.3, ...), custom_call_target="tpu_custom_call" | custom-call | flops 3000000000 | bytes 5000000 | tf_op jit(solution)/shard_map/inner/pallas_call | solution.py:479
  56.9 0.0 collective-permute-done.4.near_ref
  56.9 0.0 collective-permute-done.5.far_ref
  56.9 3.7 %outer.3 = (f32[2,128,512]{2,1,0:T(8,128)}, bf16[512,128]{1,0:T(8,128)(2,1)S(1)}) custom-call(s32[128]{0:T(128)S(1)} %reshape.25.ids_ref.ids_any, bf16[2,128,512]{2,1,0:T(8,128)(2,1)S(1)} %get-tuple-element.33.picture_ref, bf16[2,32,512]{2,1,0:T(8,128)(2,1)S(1)} %collective-permute-done.4.near_ref, bf16[2,32,512]{2,1,0:T(8,128)(2,1)S(1)} %collective-permute-done.5.far_ref, ...), custom_call_target="tpu_custom_call" | custom-call | tf_op jit(solution)/shard_map/outer/pallas_call | solution.py:501
  60.6 8.6 %all_to_all.46 = bf16[8,64,128]{2,1,0:T(8,128)(2,1)S(1)} all-to-all(bf16[8,64,128]{2,1,0:T(8,128)(2,1)S(1)} %bitcast.16), channel_id=1, replica_groups=mesh['exp'=8,'sub'=4] {'exp'}, dimensions={0} | all-to-all | bytes 262144 | tf_op jit(solution)/shard_map/all_to_all | solution.py:416
  69.2 0.6 update.3
  (2 shorter events, 0.0 us)
Async XLA Ops:
  0.6 11.9 %copy-start.1 = (s32[2,16,4,1]{1,3,2,0:T(1,128)S(1)}, s32[2,16,4,1]{1,3,2,0:T(1,128)}, u32[]{:S(2)}) copy-start(s32[2,16,4,1]{1,3,2,0:T(1,128)} %param.12) | copy-start | bytes 1540
  0.6 11.9 %copy-start = (s32[2,16,4]{1,2,0:T(4,128)S(1)}, s32[2,16,4]{1,2,0:T(4,128)}, u32[]{:S(2)}) copy-start(s32[2,16,4]{1,2,0:T(4,128)} %param.13) | copy-start | bytes 1540
  2.2 12.6 %all-to-all-start = ((bf16[8,64,128]{2,1,0:T(8,128)(2,1)}), bf16[8,64,128]{2,1,0:T(8,128)(2,1)S(1)}, u32[]{:S(2)}, u32[]{:S(2)}) async-start(bf16[8,64,128]{2,1,0:T(8,128)(2,1)} %bitcast.2), calls=%async_computation | async-start | bytes 262144 | tf_op jit(solution)/shard_map/all_to_all | solution.py:416
  8.5 16.7 %collective-permute-start.2 = (bf16[2,15,16,512]{3,2,1,0:T(8,128)(2,1)S(1)}, bf16[2,15,16,512]{3,2,1,0:T(8,128)(2,1)S(1)}, u32[]{:S(2)}, u32[]{:S(2)}) collective-permute-start(bf16[2,15,16,512]{3,2,1,0:T(8,128)(2,1)S(1)} %get-tuple-element.27.own_near_ref), channel_id=1, source_target_pairs={{0,1},{2,3},{1,0},{3,2},{4,5},{6,7},{5,4},{7,6},{8,9},{10,11},{9,8... | collective-permute-start | bytes 1474568 | tf_op jit(solution)/shard_map/ppermute | solution.py:450
  9.5 15.7 %collective-permute-start.3 = (bf16[2,15,16,512]{3,2,1,0:T(8,128)(2,1)S(1)}, bf16[2,15,16,512]{3,2,1,0:T(8,128)(2,1)S(1)}, u32[]{:S(2)}, u32[]{:S(2)}) collective-permute-start(bf16[2,15,16,512]{3,2,1,0:T(8,128)(2,1)S(1)} %get-tuple-element.28.own_far_ref), channel_id=1, source_target_pairs={{1,2},{2,1},{5,6},{6,5},{9,10},{10,9},{13,14},{14,13},{17,18},{18,... | collective-permute-start | bytes 1474568 | tf_op jit(solution)/shard_map/ppermute | solution.py:449
  15.4 9.8 %collective-permute-start = (bf16[2,32,512]{2,1,0:T(8,128)(2,1)S(1)}, bf16[2,32,512]{2,1,0:T(8,128)(2,1)S(1)}, u32[]{:S(2)}, u32[]{:S(2)}) collective-permute-start(bf16[2,32,512]{2,1,0:T(8,128)(2,1)S(1)} %get-tuple-element.24), channel_id=1, source_target_pairs={{0,1},{2,3},{1,0},{3,2},{4,5},{6,7},{5,4},{7,6},{8,9},{10,11},{9,8... | collective-permute-start | bytes 196616 | tf_op jit(solution)/shard_map/ppermute | solution.py:469
  17.6 7.6 %collective-permute-start.1 = (bf16[2,32,512]{2,1,0:T(8,128)(2,1)S(1)}, bf16[2,32,512]{2,1,0:T(8,128)(2,1)S(1)}, u32[]{:S(2)}, u32[]{:S(2)}) collective-permute-start(bf16[2,32,512]{2,1,0:T(8,128)(2,1)S(1)} %get-tuple-element.25), channel_id=1, source_target_pairs={{1,2},{2,1},{5,6},{6,5},{9,10},{10,9},{13,14},{14,13},{17,18},{18,... | collective-permute-start | bytes 196616 | tf_op jit(solution)/shard_map/ppermute | solution.py:468
  47.5 9.4 %collective-permute-start.4 = (bf16[2,32,512]{2,1,0:T(8,128)(2,1)S(1)}, bf16[2,32,512]{2,1,0:T(8,128)(2,1)S(1)}, u32[]{:S(2)}, u32[]{:S(2)}) collective-permute-start(bf16[2,32,512]{2,1,0:T(8,128)(2,1)S(1)} %get-tuple-element.34), channel_id=1, source_target_pairs={{0,1},{2,3},{1,0},{3,2},{4,5},{6,7},{5,4},{7,6},{8,9},{10,11},{9,8... | collective-permute-start | bytes 196616 | tf_op jit(solution)/shard_map/ppermute | solution.py:469
  47.5 9.3 %collective-permute-start.5 = (bf16[2,32,512]{2,1,0:T(8,128)(2,1)S(1)}, bf16[2,32,512]{2,1,0:T(8,128)(2,1)S(1)}, u32[]{:S(2)}, u32[]{:S(2)}) collective-permute-start(bf16[2,32,512]{2,1,0:T(8,128)(2,1)S(1)} %get-tuple-element.35), channel_id=1, source_target_pairs={{1,2},{2,1},{5,6},{6,5},{9,10},{10,9},{13,14},{14,13},{17,18},{18,... | collective-permute-start | bytes 196616 | tf_op jit(solution)/shard_map/ppermute | solution.py:468

commit v9 on v8

--- a/solution.py
+++ b/solution.py
@@ -226,29 +226,29 @@
 
 def inner_kernel(
     picture_ref, taps_ref, coeffs_any, observed_any, gradient_ref, across_ref, *refs, patch, taps, with_clipped,
+    resident,
 ):
     refs = list(refs)
     clipped_ref = refs.pop(0) if with_clipped else None
     field_ref, model_ref, coeffs_ref, seen_ref, vertical_ref, band_ref, sems = refs
     pieces, height, breadth = picture_ref.shape
-    modes = coeffs_ref.shape[1]
-    tall = coeffs_ref.shape[2]
+    modes = coeffs_any.shape[1]
+    tall = model_ref.shape[1]
     ext = (height - tall) // 2
     margin = (taps - 1) // 2
     stride = patch[1]
     width = across_ref.shape[1]
 
-    moves = [
-        (coeffs_any.at[:, :, pl.ds(ext, tall), :], coeffs_ref),
-        (observed_any.at[:, pl.ds(ext, tall), :], seen_ref),
-    ]
+    moves = [(observed_any.at[:, pl.ds(ext, tall), :], seen_ref)]
+    if not resident:
+        moves.append((coeffs_any.at[:, :, pl.ds(ext, tall), :], coeffs_ref))
     copies = [pltpu.make_async_copy(source, target, sems.at[k]) for k, (source, target) in enumerate(moves)]
     for copy in copies:
         copy.start()
 
     band_ref[...] = within(lags(width, width, margin), taps)
     build_vertical(vertical_ref, taps_ref, modes, margin - ext, taps)
-    smooth([(vertical_ref, [picture_ref.at[piece] for piece in range(pieces)])], field_ref, modes, tall, width, False)
+    smooth([(vertical_ref, [picture_ref.at[piece] for piece in range(pieces)])], field_ref, modes, tall, width, resident)
 
     def across_of(mode):
         ring = tiled(ring_of(taps_ref[1, mode : mode + 1], margin), width, width)
@@ -256,11 +256,14 @@
         return across_ref[mode]
 
     def weights(block, mode):
-        return coeffs_ref[block, mode]
-
-    for copy in copies:
-        copy.wait()
+        return coeffs_any[block, mode, ext : ext + tall] if resident else coeffs_ref[block, mode]
+
+    if not resident:
+        for copy in copies:
+            copy.wait()
     model_all(field_ref, model_ref, weights, across_of, modes, stride)
+    if resident:
+        copies[0].wait()
     model_ref[...] = jnp.clip(model_ref[...] - seen_ref[...], -DELTA, DELTA)
     if with_clipped:
         clipped_ref[...] = model_ref[...]
@@ -416,7 +419,6 @@
         return lax.all_to_all(block, "exp", split_axis=0, concat_axis=0, tiled=True)
 
     sky = pltpu.with_memory_space_constraint(sky_map.reshape(held, patch_cols), pltpu.HBM)
-    coeffs = pltpu.with_memory_space_constraint(coeffs, pltpu.HBM)
     observed = pltpu.with_memory_space_constraint(observed, pltpu.HBM)
     rim_shape = jax.ShapeDtypeStruct((pieces, modes + PARTS, ext, breadth), BF16)
     spread, own_near, own_far, taps = pl.pallas_call(
@@ -440,7 +442,7 @@
         compiler_params=pltpu.CompilerParams(vmem_limit_bytes=8 << 20),
         name="begin",
     )(
-        sky, coeffs, observed,
+        sky, pltpu.with_memory_space_constraint(coeffs, pltpu.HBM), observed,
         pltpu.with_memory_space_constraint(vert_taps, pltpu.HBM),
         pltpu.with_memory_space_constraint(horiz_taps, pltpu.HBM),
     )
@@ -477,14 +479,14 @@
         if last:
             results.append(pltpu.VMEM((pieces, inner, breadth), F32))
         middle = pl.pallas_call(
-            functools.partial(inner_kernel, patch=patch, taps=taken, with_clipped=last),
+            functools.partial(inner_kernel, patch=patch, taps=taken, with_clipped=last, resident=last),
             out_shape=tuple(results),
-            in_specs=[vmem, vmem] + [somewhere] * 2,
+            in_specs=[vmem, vmem, vmem if last else somewhere, somewhere],
             out_specs=(vmem,) * len(results),
             scratch_shapes=[
                 pltpu.VMEM((pieces, modes * inner, breadth), BF16),
                 pltpu.VMEM((pieces, inner, breadth), F32),
-                pltpu.VMEM((pieces, modes, inner, breadth), BF16),
+                pltpu.VMEM((1, 1, ROWS, LANES) if last else (pieces, modes, inner, breadth), BF16),
                 pltpu.VMEM((pieces, inner, breadth), F32),
                 pltpu.VMEM((modes * inner, height), BF16),
                 pltpu.VMEM((width, width), F32),
@@ -493,7 +495,7 @@
             compiler_params=pltpu.CompilerParams(vmem_limit_bytes=16 << 20),
             cost_estimate=pl.CostEstimate(flops=3 * 10**9, bytes_accessed=5 * 10**6, transcendentals=0),
             name="inner",
-        )(picture, taps, coeffs, observed)
+        )(picture, taps, pltpu.with_memory_space_constraint(coeffs, pltpu.VMEM if last else pltpu.HBM), observed)
         results = [jax.ShapeDtypeStruct((exp_count * slot, patch_cols), BF16)]
         if last:
             results.insert(0, jax.ShapeDtypeStruct((pieces, height, breadth), F32))

time: 70.4 us -> 69.7 us (0.990)
  Pallas kernels: 20.3 us -> 19.5 us
    pallas_call x2, Pallas kernels: 9.17 us -> 8.44 us  [per_device(): pl.pallas_call(functools.partial(inner_kernel, patch=patch, taps=taken, w...]
  transfers between devices with their start and end apart: 7 -> 7, of which waited for: 1 -> 1; matrix products, arithmetic and copies ran while one was open for 0% -> 0% of each run, Pallas kernels for 14% -> 13%
where the time goes in v9:
time: 69.7 us; the launch traced here: 69.2 us
  blocking collectives  26.3 us (38%)
  starting transfers between devices  20.3 us (29%)
  Pallas kernels  19.5 us (28%)
  waiting for transfers between devices  1.98 us (3%)
  between operations  0.84 us (1%)
    all_to_all x3, blocking collectives, exchange(): return lax.all_to_all(block, 'exp', split_axis=0, concat_axis=0, tiled=True)  26.3 us
    pallas_call x2, Pallas kernels, per_device(): pl.pallas_call(functools.partial(inner_kernel, patch=patch, taps=taken, w...  8.44 us
    ppermute x2, starting transfers between devices, per_device(): far = lax.ppermute(far, 'sub', routes[1])  7.73 us
    pallas_call x2, Pallas kernels, per_device(): pl.pallas_call(functools.partial(outer_kernel, patch=patch, per_tile=per_...  6.81 us
    all_to_all x1, starting transfers between devices, exchange(): return lax.all_to_all(block, 'exp', split_axis=0, concat_axis=0, tiled=True)  6.37 us
    ppermute x1, starting transfers between devices, per_device(): rims_far = lax.ppermute(own_far, 'sub', routes[1])  3.04 us
    ppermute x2, starting transfers between devices, per_device(): near = lax.ppermute(near, 'sub', routes[0])  2.22 us
    all_to_all x1, waiting for transfers between devices, exchange(): return lax.all_to_all(block, 'exp', split_axis=0, concat_axis=0, tiled=True)  1.96 us
  transfers between devices with their start and end apart: 7, of which 1 were waited for; matrix products, arithmetic and copies ran while one was open for 0% of the time, Pallas kernels for 13%

profile of v9, /device:TPU:1, one launch (start us, length us, event | category | flops | bytes accessed | tf_op | source)
XLA Modules:
  0.0 69.2 jit_solution(426398348296050227)
XLA Ops:
  0.6 0.0 copy-start.2
  0.6 0.0 copy-start.1
  0.7 1.5 %begin.1 = (bf16[512,128]{1,0:T(8,128)(2,1)}, bf16[2,15,16,512]{3,2,1,0:T(8,128)(2,1)S(1)}, bf16[2,15,16,512]{3,2,1,0:T(8,128)(2,1)S(1)}, f32[2,16,128]{2,1,0:T(8,128)S(1)}) custom-call(f32[64,128]{1,0:T(8,128)} %bitcast.18, bf16[2,12,128,512]{3,2,1,0:T(8,128)(2,1)} %coeffs_any.3, f32[2,128,512]{2,1,0:T(8,128)} %observed_any.3, bf16[12,21]{1,0:T(8,128)(2,1)} %vert_any.1, ...), custom_call_target="tpu_custom_call" | custom-call | tf_op jit(solution)/shard_map/begin/pallas_call | solution.py:424
  2.2 6.4 %all-to-all-start = ((bf16[8,64,128]{2,1,0:T(8,128)(2,1)}), bf16[8,64,128]{2,1,0:T(8,128)(2,1)S(1)}, u32[]{:S(2)}, u32[]{:S(2)}) async-start(bf16[8,64,128]{2,1,0:T(8,128)(2,1)} %bitcast.2), calls=%async_computation | async-start | bytes 262144 | tf_op jit(solution)/shard_map/all_to_all | solution.py:419
  8.5 1.0 %collective-permute-start.2 = (bf16[2,15,16,512]{3,2,1,0:T(8,128)(2,1)S(1)}, bf16[2,15,16,512]{3,2,1,0:T(8,128)(2,1)S(1)}, u32[]{:S(2)}, u32[]{:S(2)}) collective-permute-start(bf16[2,15,16,512]{3,2,1,0:T(8,128)(2,1)S(1)} %get-tuple-element.27.own_near_ref), channel_id=1, source_target_pairs={{0,1},{2,3},{1,0},{3,2},{4,5},{6,7},{5,4},{7,6},{8,9},{10,11},{9,8... | collective-permute-start | bytes 1474568 | tf_op jit(solution)/shard_map/ppermute | solution.py:452
  9.5 3.0 %collective-permute-start.3 = (bf16[2,15,16,512]{3,2,1,0:T(8,128)(2,1)S(1)}, bf16[2,15,16,512]{3,2,1,0:T(8,128)(2,1)S(1)}, u32[]{:S(2)}, u32[]{:S(2)}) collective-permute-start(bf16[2,15,16,512]{3,2,1,0:T(8,128)(2,1)S(1)} %get-tuple-element.28.own_far_ref), channel_id=1, source_target_pairs={{1,2},{2,1},{5,6},{6,5},{9,10},{10,9},{13,14},{14,13},{17,18},{18,... | collective-permute-start | bytes 1474568 | tf_op jit(solution)/shard_map/ppermute | solution.py:451
  12.5 0.0 copy-done.2
  12.6 0.0 copy-done.1
  12.6 0.1 copy.10
  12.7 0.1 reshape.25.ids_ref.ids_any
  12.8 2.0 %all-to-all-done = bf16[8,64,128]{2,1,0:T(8,128)(2,1)S(1)} async-done(((bf16[8,64,128]{2,1,0:T(8,128)(2,1)}), bf16[8,64,128]{2,1,0:T(8,128)(2,1)S(1)}, u32[]{:S(2)}, u32[]{:S(2)}) %all-to-all-start) | async-done | bytes 131104 | tf_op jit(solution)/shard_map/all_to_all | solution.py:419
  14.7 0.7 picture.2
  15.4 2.2 %collective-permute-start = (bf16[2,32,512]{2,1,0:T(8,128)(2,1)S(1)}, bf16[2,32,512]{2,1,0:T(8,128)(2,1)S(1)}, u32[]{:S(2)}, u32[]{:S(2)}) collective-permute-start(bf16[2,32,512]{2,1,0:T(8,128)(2,1)S(1)} %get-tuple-element.24), channel_id=1, source_target_pairs={{0,1},{2,3},{1,0},{3,2},{4,5},{6,7},{5,4},{7,6},{8,9},{10,11},{9,8... | collective-permute-start | bytes 196616 | tf_op jit(solution)/shard_map/ppermute | solution.py:471
  17.6 3.0 %collective-permute-start.1 = (bf16[2,32,512]{2,1,0:T(8,128)(2,1)S(1)}, bf16[2,32,512]{2,1,0:T(8,128)(2,1)S(1)}, u32[]{:S(2)}, u32[]{:S(2)}) collective-permute-start(bf16[2,32,512]{2,1,0:T(8,128)(2,1)S(1)} %get-tuple-element.25), channel_id=1, source_target_pairs={{1,2},{2,1},{5,6},{6,5},{9,10},{10,9},{13,14},{14,13},{17,18},{18,... | collective-permute-start | bytes 196616 | tf_op jit(solution)/shard_map/ppermute | solution.py:470
  20.6 4.7 %inner.2 = (f32[2,128,512]{2,1,0:T(8,128)S(1)}, bf16[12,256,256]{2,1,0:T(8,128)(2,1)S(1)}) custom-call(bf16[2,128,512]{2,1,0:T(8,128)(2,1)S(1)} %get-tuple-element.23.picture_ref, f32[2,16,128]{2,1,0:T(8,128)S(1)} %get-tuple-element.26.taps_ref, bf16[2,12,128,512]{3,2,1,0:T(8,128)(2,1)} %coeffs_any.3, f32[2,128,512]{2,1,0:T(8,128)} %observed_any.3), custom_call_target="tpu_custom_call" | custom-call | flops 3000000000 | bytes 5000000 | tf_op jit(solution)/shard_map/inner/pallas_call | solution.py:481
  25.3 0.0 collective-permute-done.near_ref
  25.3 0.0 collective-permute-done.1.far_ref
  25.3 0.0 collective-permute-done.2.rims_near_ref
  25.3 0.0 collective-permute-done.3.rims_far_ref
  25.3 0.0 copy-start
  25.3 3.1 %outer.2 = bf16[640,128]{1,0:T(8,128)(2,1)S(1)} custom-call(s32[128]{0:T(128)S(1)} %reshape.25.ids_ref.ids_any, bf16[2,128,512]{2,1,0:T(8,128)(2,1)S(1)} %get-tuple-element.23.picture_ref, bf16[2,32,512]{2,1,0:T(8,128)(2,1)S(1)} %collective-permute-done.near_ref, bf16[2,32,512]{2,1,0:T(8,128)(2,1)S(1)} %collective-permute-done.1.far_ref, ...), custom_call_target="tpu_custom_call" | custom-call | tf_op jit(solution)/shard_map/outer/pallas_call | solution.py:503
  28.4 8.8 %all_to_all.44 = bf16[8,80,128]{2,1,0:T(8,128)(2,1)S(1)} all-to-all(bf16[8,80,128]{2,1,0:T(8,128)(2,1)S(1)} %bitcast.11), channel_id=1, replica_groups=mesh['exp'=8,'sub'=4] {'exp'}, dimensions={0} | all-to-all | bytes 327680 | tf_op jit(solution)/shard_map/all_to_all | solution.py:419
  37.2 0.8 %update.2 = (f32[64,128]{1,0:T(8,128)S(1)}, bf16[512,128]{1,0:T(8,128)(2,1)S(1)}, f32[64,128]{1,0:T(8,128)S(1)}) custom-call(f32[64,128]{1,0:T(8,128)} %bitcast.19, bf16[640,128]{1,0:T(8,128)(2,1)S(1)} %bitcast.12), custom_call_target="tpu_custom_call" | custom-call | tf_op jit(solution)/shard_map/update/pallas_call | solution.py:533
  38.0 8.9 %all_to_all.45 = bf16[8,64,128]{2,1,0:T(8,128)(2,1)S(1)} all-to-all(bf16[8,64,128]{2,1,0:T(8,128)(2,1)S(1)} %bitcast.17), channel_id=1, replica_groups=mesh['exp'=8,'sub'=4] {'exp'}, dimensions={0} | all-to-all | bytes 262144 | tf_op jit(solution)/shard_map/all_to_all | solution.py:419
  46.9 0.7 picture.3
  47.6 0.1 collective-permute-start.4
  47.7 4.7 %collective-permute-start.5 = (bf16[2,32,512]{2,1,0:T(8,128)(2,1)S(1)}, bf16[2,32,512]{2,1,0:T(8,128)(2,1)S(1)}, u32[]{:S(2)}, u32[]{:S(2)}) collective-permute-start(bf16[2,32,512]{2,1,0:T(8,128)(2,1)S(1)} %get-tuple-element.35), channel_id=1, source_target_pairs={{1,2},{2,1},{5,6},{6,5},{9,10},{10,9},{13,14},{14,13},{17,18},{18,... | collective-permute-start | bytes 196616 | tf_op jit(solution)/shard_map/ppermute | solution.py:470
  52.3 0.0 copy-done
  52.4 3.8 %inner.3 = (f32[2,128,512]{2,1,0:T(8,128)S(1)}, bf16[12,256,256]{2,1,0:T(8,128)(2,1)S(1)}, f32[2,96,512]{2,1,0:T(8,128)S(1)}) custom-call(bf16[2,128,512]{2,1,0:T(8,128)(2,1)S(1)} %get-tuple-element.33.picture_ref, f32[2,16,128]{2,1,0:T(8,128)S(1)} %get-tuple-element.26.taps_ref, bf16[2,12,128,512]{3,2,1,0:T(8,128)(2,1)S(1)} %copy-done, ...), custom_call_target="tpu_custom_call" | custom-call | flops 3000000000 | bytes 5000000 | tf_op jit(solution)/shard_map/inner/pallas_call | solution.py:481
  56.1 0.0 collective-permute-done.4.near_ref
  56.2 0.0 collective-permute-done.5.far_ref
  56.2 3.7 %outer.3 = (f32[2,128,512]{2,1,0:T(8,128)}, bf16[512,128]{1,0:T(8,128)(2,1)S(1)}) custom-call(s32[128]{0:T(128)S(1)} %reshape.25.ids_ref.ids_any, bf16[2,128,512]{2,1,0:T(8,128)(2,1)S(1)} %get-tuple-element.33.picture_ref, bf16[2,32,512]{2,1,0:T(8,128)(2,1)S(1)} %collective-permute-done.4.near_ref, bf16[2,32,512]{2,1,0:T(8,128)(2,1)S(1)} %collective-permute-done.5.far_ref, ...), custom_call_target="tpu_custom_call" | custom-call | tf_op jit(solution)/shard_map/outer/pallas_call | solution.py:503
  59.9 8.6 %all_to_all.46 = bf16[8,64,128]{2,1,0:T(8,128)(2,1)S(1)} all-to-all(bf16[8,64,128]{2,1,0:T(8,128)(2,1)S(1)} %bitcast.16), channel_id=1, replica_groups=mesh['exp'=8,'sub'=4] {'exp'}, dimensions={0} | all-to-all | bytes 262144 | tf_op jit(solution)/shard_map/all_to_all | solution.py:419
  68.5 0.6 update.3
  (2 shorter events, 0.0 us)
Async XLA Ops:
  0.6 11.9 %copy-start.2 = (s32[2,16,4,1]{1,3,2,0:T(1,128)S(1)}, s32[2,16,4,1]{1,3,2,0:T(1,128)}, u32[]{:S(2)}) copy-start(s32[2,16,4,1]{1,3,2,0:T(1,128)} %param.12) | copy-start | bytes 1540
  0.6 11.9 %copy-start.1 = (s32[2,16,4]{1,2,0:T(4,128)S(1)}, s32[2,16,4]{1,2,0:T(4,128)}, u32[]{:S(2)}) copy-start(s32[2,16,4]{1,2,0:T(4,128)} %param.13) | copy-start | bytes 1540
  2.2 12.6 %all-to-all-start = ((bf16[8,64,128]{2,1,0:T(8,128)(2,1)}), bf16[8,64,128]{2,1,0:T(8,128)(2,1)S(1)}, u32[]{:S(2)}, u32[]{:S(2)}) async-start(bf16[8,64,128]{2,1,0:T(8,128)(2,1)} %bitcast.2), calls=%async_computation | async-start | bytes 262144 | tf_op jit(solution)/shard_map/all_to_all | solution.py:419
  8.5 16.8 %collective-permute-start.2 = (bf16[2,15,16,512]{3,2,1,0:T(8,128)(2,1)S(1)}, bf16[2,15,16,512]{3,2,1,0:T(8,128)(2,1)S(1)}, u32[]{:S(2)}, u32[]{:S(2)}) collective-permute-start(bf16[2,15,16,512]{3,2,1,0:T(8,128)(2,1)S(1)} %get-tuple-element.27.own_near_ref), channel_id=1, source_target_pairs={{0,1},{2,3},{1,0},{3,2},{4,5},{6,7},{5,4},{7,6},{8,9},{10,11},{9,8... | collective-permute-start | bytes 1474568 | tf_op jit(solution)/shard_map/ppermute | solution.py:452
  9.5 15.8 %collective-permute-start.3 = (bf16[2,15,16,512]{3,2,1,0:T(8,128)(2,1)S(1)}, bf16[2,15,16,512]{3,2,1,0:T(8,128)(2,1)S(1)}, u32[]{:S(2)}, u32[]{:S(2)}) collective-permute-start(bf16[2,15,16,512]{3,2,1,0:T(8,128)(2,1)S(1)} %get-tuple-element.28.own_far_ref), channel_id=1, source_target_pairs={{1,2},{2,1},{5,6},{6,5},{9,10},{10,9},{13,14},{14,13},{17,18},{18,... | collective-permute-start | bytes 1474568 | tf_op jit(solution)/shard_map/ppermute | solution.py:451
  15.4 9.9 %collective-permute-start = (bf16[2,32,512]{2,1,0:T(8,128)(2,1)S(1)}, bf16[2,32,512]{2,1,0:T(8,128)(2,1)S(1)}, u32[]{:S(2)}, u32[]{:S(2)}) collective-permute-start(bf16[2,32,512]{2,1,0:T(8,128)(2,1)S(1)} %get-tuple-element.24), channel_id=1, source_target_pairs={{0,1},{2,3},{1,0},{3,2},{4,5},{6,7},{5,4},{7,6},{8,9},{10,11},{9,8... | collective-permute-start | bytes 196616 | tf_op jit(solution)/shard_map/ppermute | solution.py:471
  17.6 7.7 %collective-permute-start.1 = (bf16[2,32,512]{2,1,0:T(8,128)(2,1)S(1)}, bf16[2,32,512]{2,1,0:T(8,128)(2,1)S(1)}, u32[]{:S(2)}, u32[]{:S(2)}) collective-permute-start(bf16[2,32,512]{2,1,0:T(8,128)(2,1)S(1)} %get-tuple-element.25), channel_id=1, source_target_pairs={{1,2},{2,1},{5,6},{6,5},{9,10},{10,9},{13,14},{14,13},{17,18},{18,... | collective-permute-start | bytes 196616 | tf_op jit(solution)/shard_map/ppermute | solution.py:470
  25.3 27.0 %copy-start = (bf16[2,12,128,512]{3,2,1,0:T(8,128)(2,1)S(1)}, bf16[2,12,128,512]{3,2,1,0:T(8,128)(2,1)}, u32[]{:S(2)}) copy-start(bf16[2,12,128,512]{3,2,1,0:T(8,128)(2,1)} %coeffs_any.3) | copy-start | bytes 9437188
  47.6 8.6 %collective-permute-start.4 = (bf16[2,32,512]{2,1,0:T(8,128)(2,1)S(1)}, bf16[2,32,512]{2,1,0:T(8,128)(2,1)S(1)}, u32[]{:S(2)}, u32[]{:S(2)}) collective-permute-start(bf16[2,32,512]{2,1,0:T(8,128)(2,1)S(1)} %get-tuple-element.34), channel_id=1, source_target_pairs={{0,1},{2,3},{1,0},{3,2},{4,5},{6,7},{5,4},{7,6},{8,9},{10,11},{9,8... | collective-permute-start | bytes 196616 | tf_op jit(solution)/shard_map/ppermute | solution.py:471
  47.7 8.5 %collective-permute-start.5 = (bf16[2,32,512]{2,1,0:T(8,128)(2,1)S(1)}, bf16[2,32,512]{2,1,0:T(8,128)(2,1)S(1)}, u32[]{:S(2)}, u32[]{:S(2)}) collective-permute-start(bf16[2,32,512]{2,1,0:T(8,128)(2,1)S(1)} %get-tuple-element.35), channel_id=1, source_target_pairs={{1,2},{2,1},{5,6},{6,5},{9,10},{10,9},{13,14},{14,13},{17,18},{18,... | collective-permute-start | bytes 196616 | tf_op jit(solution)/shard_map/ppermute | solution.py:470

commit v10 on v9

--- a/solution.py
+++ b/solution.py
@@ -239,8 +239,9 @@
     stride = patch[1]
     width = across_ref.shape[1]
 
-    moves = [(observed_any.at[:, pl.ds(ext, tall), :], seen_ref)]
+    moves = []
     if not resident:
+        moves.append((observed_any.at[:, pl.ds(ext, tall), :], seen_ref))
         moves.append((coeffs_any.at[:, :, pl.ds(ext, tall), :], coeffs_ref))
     copies = [pltpu.make_async_copy(source, target, sems.at[k]) for k, (source, target) in enumerate(moves)]
     for copy in copies:
@@ -262,9 +263,8 @@
         for copy in copies:
             copy.wait()
     model_all(field_ref, model_ref, weights, across_of, modes, stride)
-    if resident:
-        copies[0].wait()
-    model_ref[...] = jnp.clip(model_ref[...] - seen_ref[...], -DELTA, DELTA)
+    seen = observed_any[:, ext : ext + tall, :] if resident else seen_ref[...]
+    model_ref[...] = jnp.clip(model_ref[...] - seen, -DELTA, DELTA)
     if with_clipped:
         clipped_ref[...] = model_ref[...]
     adjoint_all(field_ref, model_ref, weights, across_ref, modes, stride)
@@ -419,7 +419,6 @@
         return lax.all_to_all(block, "exp", split_axis=0, concat_axis=0, tiled=True)
 
     sky = pltpu.with_memory_space_constraint(sky_map.reshape(held, patch_cols), pltpu.HBM)
-    observed = pltpu.with_memory_space_constraint(observed, pltpu.HBM)
     rim_shape = jax.ShapeDtypeStruct((pieces, modes + PARTS, ext, breadth), BF16)
     spread, own_near, own_far, taps = pl.pallas_call(
         begin_kernel,
@@ -442,7 +441,9 @@
         compiler_params=pltpu.CompilerParams(vmem_limit_bytes=8 << 20),
         name="begin",
     )(
-        sky, pltpu.with_memory_space_constraint(coeffs, pltpu.HBM), observed,
+        sky,
+        pltpu.with_memory_space_constraint(coeffs, pltpu.HBM),
+        pltpu.with_memory_space_constraint(observed, pltpu.HBM),
         pltpu.with_memory_space_constraint(vert_taps, pltpu.HBM),
         pltpu.with_memory_space_constraint(horiz_taps, pltpu.HBM),
     )
@@ -481,7 +482,7 @@
         middle = pl.pallas_call(
             functools.partial(inner_kernel, patch=patch, taps=taken, with_clipped=last, resident=last),
             out_shape=tuple(results),
-            in_specs=[vmem, vmem, vmem if last else somewhere, somewhere],
+            in_specs=[vmem, vmem] + [vmem if last else somewhere] * 2,
             out_specs=(vmem,) * len(results),
             scratch_shapes=[
                 pltpu.VMEM((pieces, modes * inner, breadth), BF16),
@@ -495,7 +496,11 @@
             compiler_params=pltpu.CompilerParams(vmem_limit_bytes=16 << 20),
             cost_estimate=pl.CostEstimate(flops=3 * 10**9, bytes_accessed=5 * 10**6, transcendentals=0),
             name="inner",
-        )(picture, taps, pltpu.with_memory_space_constraint(coeffs, pltpu.VMEM if last else pltpu.HBM), observed)
+        )(
+            picture, taps,
+            pltpu.with_memory_space_constraint(coeffs, pltpu.VMEM if last else pltpu.HBM),
+            pltpu.with_memory_space_constraint(observed, pltpu.VMEM if last else pltpu.HBM),
+        )
         results = [jax.ShapeDtypeStruct((exp_count * slot, patch_cols), BF16)]
         if last:
             results.insert(0, jax.ShapeDtypeStruct((pieces, height, breadth), F32))

time: 69.7 us -> 69.1 us (level)
  transfers between devices with their start and end apart: 7 -> 7, of which waited for: 1 -> 1; matrix products, arithmetic and copies ran while one was open for 0% -> 0% of each run, Pallas kernels for 13% -> 12%
where the time goes in v10:
time: 69.1 us; the launch traced here: 68.6 us
  blocking collectives  26.3 us (38%)
  starting transfers between devices  20.3 us (29%)
  Pallas kernels  19 us (27%)
  waiting for transfers between devices  1.98 us (3%)
  between operations  0.85 us (1%)
    all_to_all x3, blocking collectives, exchange(): return lax.all_to_all(block, 'exp', split_axis=0, concat_axis=0, tiled=True)  26.3 us
    pallas_call x2, Pallas kernels, per_device(): pl.pallas_call(functools.partial(inner_kernel, patch=patch, taps=taken, w...  7.89 us
    ppermute x2, starting transfers between devices, per_device(): far = lax.ppermute(far, 'sub', routes[1])  7.72 us
    pallas_call x2, Pallas kernels, per_device(): pl.pallas_call(functools.partial(outer_kernel, patch=patch, per_tile=per_...  6.79 us
    all_to_all x1, starting transfers between devices, exchange(): return lax.all_to_all(block, 'exp', split_axis=0, concat_axis=0, tiled=True)  6.37 us
    ppermute x1, starting transfers between devices, per_device(): rims_far = lax.ppermute(own_far, 'sub', routes[1])  3.04 us
    ppermute x2, starting transfers between devices, per_device(): near = lax.ppermute(near, 'sub', routes[0])  2.22 us
    all_to_all x1, waiting for transfers between devices, exchange(): return lax.all_to_all(block, 'exp', split_axis=0, concat_axis=0, tiled=True)  1.96 us
  transfers between devices with their start and end apart: 7, of which 1 were waited for; matrix products, arithmetic and copies ran while one was open for 0% of the time, Pallas kernels for 12%

profile of v10, /device:TPU:1, one launch (start us, length us, event | category | flops | bytes accessed | tf_op | source)
XLA Modules:
  0.0 68.6 jit_solution(543248656264613486)
XLA Ops:
  0.6 0.0 copy-start.3
  0.6 0.0 copy-start.2
  0.7 1.5 %begin.1 = (bf16[512,128]{1,0:T(8,128)(2,1)}, bf16[2,15,16,512]{3,2,1,0:T(8,128)(2,1)S(1)}, bf16[2,15,16,512]{3,2,1,0:T(8,128)(2,1)S(1)}, f32[2,16,128]{2,1,0:T(8,128)S(1)}) custom-call(f32[64,128]{1,0:T(8,128)} %bitcast.18, bf16[2,12,128,512]{3,2,1,0:T(8,128)(2,1)} %coeffs_any.3, f32[2,128,512]{2,1,0:T(8,128)} %observed_any.3, bf16[12,21]{1,0:T(8,128)(2,1)} %vert_any.1, ...), custom_call_target="tpu_custom_call" | custom-call | tf_op jit(solution)/shard_map/begin/pallas_call | solution.py:423
  2.2 6.4 %all-to-all-start = ((bf16[8,64,128]{2,1,0:T(8,128)(2,1)}), bf16[8,64,128]{2,1,0:T(8,128)(2,1)S(1)}, u32[]{:S(2)}, u32[]{:S(2)}) async-start(bf16[8,64,128]{2,1,0:T(8,128)(2,1)} %bitcast.2), calls=%async_computation | async-start | bytes 262144 | tf_op jit(solution)/shard_map/all_to_all | solution.py:419
  8.5 1.0 %collective-permute-start.2 = (bf16[2,15,16,512]{3,2,1,0:T(8,128)(2,1)S(1)}, bf16[2,15,16,512]{3,2,1,0:T(8,128)(2,1)S(1)}, u32[]{:S(2)}, u32[]{:S(2)}) collective-permute-start(bf16[2,15,16,512]{3,2,1,0:T(8,128)(2,1)S(1)} %get-tuple-element.27.own_near_ref), channel_id=1, source_target_pairs={{0,1},{2,3},{1,0},{3,2},{4,5},{6,7},{5,4},{7,6},{8,9},{10,11},{9,8... | collective-permute-start | bytes 1474568 | tf_op jit(solution)/shard_map/ppermute | solution.py:453
  9.5 3.0 %collective-permute-start.3 = (bf16[2,15,16,512]{3,2,1,0:T(8,128)(2,1)S(1)}, bf16[2,15,16,512]{3,2,1,0:T(8,128)(2,1)S(1)}, u32[]{:S(2)}, u32[]{:S(2)}) collective-permute-start(bf16[2,15,16,512]{3,2,1,0:T(8,128)(2,1)S(1)} %get-tuple-element.28.own_far_ref), channel_id=1, source_target_pairs={{1,2},{2,1},{5,6},{6,5},{9,10},{10,9},{13,14},{14,13},{17,18},{18,... | collective-permute-start | bytes 1474568 | tf_op jit(solution)/shard_map/ppermute | solution.py:452
  12.5 0.0 copy-done.3
  12.6 0.0 copy-done.2
  12.6 0.1 copy.10
  12.7 0.1 reshape.25.ids_ref.ids_any
  12.8 2.0 %all-to-all-done = bf16[8,64,128]{2,1,0:T(8,128)(2,1)S(1)} async-done(((bf16[8,64,128]{2,1,0:T(8,128)(2,1)}), bf16[8,64,128]{2,1,0:T(8,128)(2,1)S(1)}, u32[]{:S(2)}, u32[]{:S(2)}) %all-to-all-start) | async-done | bytes 131104 | tf_op jit(solution)/shard_map/all_to_all | solution.py:419
  14.7 0.7 picture.2
  15.4 2.2 %collective-permute-start = (bf16[2,32,512]{2,1,0:T(8,128)(2,1)S(1)}, bf16[2,32,512]{2,1,0:T(8,128)(2,1)S(1)}, u32[]{:S(2)}, u32[]{:S(2)}) collective-permute-start(bf16[2,32,512]{2,1,0:T(8,128)(2,1)S(1)} %get-tuple-element.24), channel_id=1, source_target_pairs={{0,1},{2,3},{1,0},{3,2},{4,5},{6,7},{5,4},{7,6},{8,9},{10,11},{9,8... | collective-permute-start | bytes 196616 | tf_op jit(solution)/shard_map/ppermute | solution.py:472
  17.6 3.0 %collective-permute-start.1 = (bf16[2,32,512]{2,1,0:T(8,128)(2,1)S(1)}, bf16[2,32,512]{2,1,0:T(8,128)(2,1)S(1)}, u32[]{:S(2)}, u32[]{:S(2)}) collective-permute-start(bf16[2,32,512]{2,1,0:T(8,128)(2,1)S(1)} %get-tuple-element.25), channel_id=1, source_target_pairs={{1,2},{2,1},{5,6},{6,5},{9,10},{10,9},{13,14},{14,13},{17,18},{18,... | collective-permute-start | bytes 196616 | tf_op jit(solution)/shard_map/ppermute | solution.py:471
  20.6 4.7 %inner.2 = (f32[2,128,512]{2,1,0:T(8,128)S(1)}, bf16[12,256,256]{2,1,0:T(8,128)(2,1)S(1)}) custom-call(bf16[2,128,512]{2,1,0:T(8,128)(2,1)S(1)} %get-tuple-element.23.picture_ref, f32[2,16,128]{2,1,0:T(8,128)S(1)} %get-tuple-element.26.taps_ref, bf16[2,12,128,512]{3,2,1,0:T(8,128)(2,1)} %coeffs_any.3, f32[2,128,512]{2,1,0:T(8,128)} %observed_any.3), custom_call_target="tpu_custom_call" | custom-call | flops 3000000000 | bytes 5000000 | tf_op jit(solution)/shard_map/inner/pallas_call | solution.py:482
  25.3 0.0 collective-permute-done.near_ref
  25.3 0.0 collective-permute-done.1.far_ref
  25.3 0.0 collective-permute-done.2.rims_near_ref
  25.3 0.0 collective-permute-done.3.rims_far_ref
  25.3 0.0 copy-start
  25.3 0.0 copy-start.1
  25.4 3.1 %outer.2 = bf16[640,128]{1,0:T(8,128)(2,1)S(1)} custom-call(s32[128]{0:T(128)S(1)} %reshape.25.ids_ref.ids_any, bf16[2,128,512]{2,1,0:T(8,128)(2,1)S(1)} %get-tuple-element.23.picture_ref, bf16[2,32,512]{2,1,0:T(8,128)(2,1)S(1)} %collective-permute-done.near_ref, bf16[2,32,512]{2,1,0:T(8,128)(2,1)S(1)} %collective-permute-done.1.far_ref, ...), custom_call_target="tpu_custom_call" | custom-call | tf_op jit(solution)/shard_map/outer/pallas_call | solution.py:508
  28.4 8.8 %all_to_all.44 = bf16[8,80,128]{2,1,0:T(8,128)(2,1)S(1)} all-to-all(bf16[8,80,128]{2,1,0:T(8,128)(2,1)S(1)} %bitcast.11), channel_id=1, replica_groups=mesh['exp'=8,'sub'=4] {'exp'}, dimensions={0} | all-to-all | bytes 327680 | tf_op jit(solution)/shard_map/all_to_all | solution.py:419
  37.2 0.8 %update.2 = (f32[64,128]{1,0:T(8,128)S(1)}, bf16[512,128]{1,0:T(8,128)(2,1)S(1)}, f32[64,128]{1,0:T(8,128)S(1)}) custom-call(f32[64,128]{1,0:T(8,128)} %bitcast.19, bf16[640,128]{1,0:T(8,128)(2,1)S(1)} %bitcast.12), custom_call_target="tpu_custom_call" | custom-call | tf_op jit(solution)/shard_map/update/pallas_call | solution.py:538
  38.0 8.9 %all_to_all.45 = bf16[8,64,128]{2,1,0:T(8,128)(2,1)S(1)} all-to-all(bf16[8,64,128]{2,1,0:T(8,128)(2,1)S(1)} %bitcast.17), channel_id=1, replica_groups=mesh['exp'=8,'sub'=4] {'exp'}, dimensions={0} | all-to-all | bytes 262144 | tf_op jit(solution)/shard_map/all_to_all | solution.py:419
  46.9 0.7 picture.3
  47.6 0.1 collective-permute-start.4
  47.7 4.7 %collective-permute-start.5 = (bf16[2,32,512]{2,1,0:T(8,128)(2,1)S(1)}, bf16[2,32,512]{2,1,0:T(8,128)(2,1)S(1)}, u32[]{:S(2)}, u32[]{:S(2)}) collective-permute-start(bf16[2,32,512]{2,1,0:T(8,128)(2,1)S(1)} %get-tuple-element.35), channel_id=1, source_target_pairs={{1,2},{2,1},{5,6},{6,5},{9,10},{10,9},{13,14},{14,13},{17,18},{18,... | collective-permute-start | bytes 196616 | tf_op jit(solution)/shard_map/ppermute | solution.py:471
  52.4 0.0 copy-done
  52.4 0.0 copy-done.1
  52.4 3.2 %inner.3 = (f32[2,128,512]{2,1,0:T(8,128)S(1)}, bf16[12,256,256]{2,1,0:T(8,128)(2,1)S(1)}, f32[2,96,512]{2,1,0:T(8,128)S(1)}) custom-call(bf16[2,128,512]{2,1,0:T(8,128)(2,1)S(1)} %get-tuple-element.33.picture_ref, f32[2,16,128]{2,1,0:T(8,128)S(1)} %get-tuple-element.26.taps_ref, bf16[2,12,128,512]{3,2,1,0:T(8,128)(2,1)S(1)} %copy-done, ...), custom_call_target="tpu_custom_call" | custom-call | flops 3000000000 | bytes 5000000 | tf_op jit(solution)/shard_map/inner/pallas_call | solution.py:482
  55.6 0.0 collective-permute-done.4.near_ref
  55.6 0.0 collective-permute-done.5.far_ref
  55.6 3.7 %outer.3 = (f32[2,128,512]{2,1,0:T(8,128)}, bf16[512,128]{1,0:T(8,128)(2,1)S(1)}) custom-call(s32[128]{0:T(128)S(1)} %reshape.25.ids_ref.ids_any, bf16[2,128,512]{2,1,0:T(8,128)(2,1)S(1)} %get-tuple-element.33.picture_ref, bf16[2,32,512]{2,1,0:T(8,128)(2,1)S(1)} %collective-permute-done.4.near_ref, bf16[2,32,512]{2,1,0:T(8,128)(2,1)S(1)} %collective-permute-done.5.far_ref, ...), custom_call_target="tpu_custom_call" | custom-call | tf_op jit(solution)/shard_map/outer/pallas_call | solution.py:508
  59.4 8.6 %all_to_all.46 = bf16[8,64,128]{2,1,0:T(8,128)(2,1)S(1)} all-to-all(bf16[8,64,128]{2,1,0:T(8,128)(2,1)S(1)} %bitcast.16), channel_id=1, replica_groups=mesh['exp'=8,'sub'=4] {'exp'}, dimensions={0} | all-to-all | bytes 262144 | tf_op jit(solution)/shard_map/all_to_all | solution.py:419
  68.0 0.6 update.3
  (2 shorter events, 0.0 us)
Async XLA Ops:
  0.6 11.9 %copy-start.3 = (s32[2,16,4,1]{1,3,2,0:T(1,128)S(1)}, s32[2,16,4,1]{1,3,2,0:T(1,128)}, u32[]{:S(2)}) copy-start(s32[2,16,4,1]{1,3,2,0:T(1,128)} %param.12) | copy-start | bytes 1540
  0.6 11.9 %copy-start.2 = (s32[2,16,4]{1,2,0:T(4,128)S(1)}, s32[2,16,4]{1,2,0:T(4,128)}, u32[]{:S(2)}) copy-start(s32[2,16,4]{1,2,0:T(4,128)} %param.13) | copy-start | bytes 1540
  2.2 12.6 %all-to-all-start = ((bf16[8,64,128]{2,1,0:T(8,128)(2,1)}), bf16[8,64,128]{2,1,0:T(8,128)(2,1)S(1)}, u32[]{:S(2)}, u32[]{:S(2)}) async-start(bf16[8,64,128]{2,1,0:T(8,128)(2,1)} %bitcast.2), calls=%async_computation | async-start | bytes 262144 | tf_op jit(solution)/shard_map/all_to_all | solution.py:419
  8.5 16.8 %collective-permute-start.2 = (bf16[2,15,16,512]{3,2,1,0:T(8,128)(2,1)S(1)}, bf16[2,15,16,512]{3,2,1,0:T(8,128)(2,1)S(1)}, u32[]{:S(2)}, u32[]{:S(2)}) collective-permute-start(bf16[2,15,16,512]{3,2,1,0:T(8,128)(2,1)S(1)} %get-tuple-element.27.own_near_ref), channel_id=1, source_target_pairs={{0,1},{2,3},{1,0},{3,2},{4,5},{6,7},{5,4},{7,6},{8,9},{10,11},{9,8... | collective-permute-start | bytes 1474568 | tf_op jit(solution)/shard_map/ppermute | solution.py:453
  9.5 15.8 %collective-permute-start.3 = (bf16[2,15,16,512]{3,2,1,0:T(8,128)(2,1)S(1)}, bf16[2,15,16,512]{3,2,1,0:T(8,128)(2,1)S(1)}, u32[]{:S(2)}, u32[]{:S(2)}) collective-permute-start(bf16[2,15,16,512]{3,2,1,0:T(8,128)(2,1)S(1)} %get-tuple-element.28.own_far_ref), channel_id=1, source_target_pairs={{1,2},{2,1},{5,6},{6,5},{9,10},{10,9},{13,14},{14,13},{17,18},{18,... | collective-permute-start | bytes 1474568 | tf_op jit(solution)/shard_map/ppermute | solution.py:452
  15.4 9.9 %collective-permute-start = (bf16[2,32,512]{2,1,0:T(8,128)(2,1)S(1)}, bf16[2,32,512]{2,1,0:T(8,128)(2,1)S(1)}, u32[]{:S(2)}, u32[]{:S(2)}) collective-permute-start(bf16[2,32,512]{2,1,0:T(8,128)(2,1)S(1)} %get-tuple-element.24), channel_id=1, source_target_pairs={{0,1},{2,3},{1,0},{3,2},{4,5},{6,7},{5,4},{7,6},{8,9},{10,11},{9,8... | collective-permute-start | bytes 196616 | tf_op jit(solution)/shard_map/ppermute | solution.py:472
  17.6 7.7 %collective-permute-start.1 = (bf16[2,32,512]{2,1,0:T(8,128)(2,1)S(1)}, bf16[2,32,512]{2,1,0:T(8,128)(2,1)S(1)}, u32[]{:S(2)}, u32[]{:S(2)}) collective-permute-start(bf16[2,32,512]{2,1,0:T(8,128)(2,1)S(1)} %get-tuple-element.25), channel_id=1, source_target_pairs={{1,2},{2,1},{5,6},{6,5},{9,10},{10,9},{13,14},{14,13},{17,18},{18,... | collective-permute-start | bytes 196616 | tf_op jit(solution)/shard_map/ppermute | solution.py:471
  25.3 27.0 %copy-start = (bf16[2,12,128,512]{3,2,1,0:T(8,128)(2,1)S(1)}, bf16[2,12,128,512]{3,2,1,0:T(8,128)(2,1)}, u32[]{:S(2)}) copy-start(bf16[2,12,128,512]{3,2,1,0:T(8,128)(2,1)} %coeffs_any.3) | copy-start | bytes 9437188
  25.3 27.0 %copy-start.1 = (f32[2,128,512]{2,1,0:T(8,128)S(1)}, f32[2,128,512]{2,1,0:T(8,128)}, u32[]{:S(2)}) copy-start(f32[2,128,512]{2,1,0:T(8,128)} %observed_any.3) | copy-start | bytes 1572868
  47.6 8.0 %collective-permute-start.4 = (bf16[2,32,512]{2,1,0:T(8,128)(2,1)S(1)}, bf16[2,32,512]{2,1,0:T(8,128)(2,1)S(1)}, u32[]{:S(2)}, u32[]{:S(2)}) collective-permute-start(bf16[2,32,512]{2,1,0:T(8,128)(2,1)S(1)} %get-tuple-element.34), channel_id=1, source_target_pairs={{0,1},{2,3},{1,0},{3,2},{4,5},{6,7},{5,4},{7,6},{8,9},{10,11},{9,8... | collective-permute-start | bytes 196616 | tf_op jit(solution)/shard_map/ppermute | solution.py:472
  47.7 8.0 %collective-permute-start.5 = (bf16[2,32,512]{2,1,0:T(8,128)(2,1)S(1)}, bf16[2,32,512]{2,1,0:T(8,128)(2,1)S(1)}, u32[]{:S(2)}, u32[]{:S(2)}) collective-permute-start(bf16[2,32,512]{2,1,0:T(8,128)(2,1)S(1)} %get-tuple-element.35), channel_id=1, source_target_pairs={{1,2},{2,1},{5,6},{6,5},{9,10},{10,9},{13,14},{14,13},{17,18},{18,... | collective-permute-start | bytes 196616 | tf_op jit(solution)/shard_map/ppermute | solution.py:471
